TPU v7x, 32 devices: a whole 2x2x4 slice. The times are simulated.
32 devices in a mesh: seq: 4 (over y, core), chan: 2 (over x), dp: 4 (over z).
Axes of the slice: x: 2, y: 2, z: 4, core: 2. Of those that a mesh axis runs over, the one named last changes fastest.
Arguments:
- inputs: bfloat16 [8, 4096, 512], P('dp', 'chan', 'seq'), may hold values from -0.0234375 to 0.0234375
- output_grad: bfloat16 [8, 4096, 512], P('dp', 'chan', 'seq'), may hold values from -6 to 6
- filters: bfloat16 [256, 512], P('chan', 'seq'), may hold values from -0.25 to 0.25
Outputs:
- input_grad: bfloat16 [8, 4096, 512], P('dp', 'chan', 'seq')
- filter_grad: float32 [256, 512], P('chan', 'seq')
All inputs are finite; a program needn't handle non-finite values.
Results may differ from a plain program's by a relative error of at most 0.001.
Values may be sent and summed in bfloat16 or wider, within the bound.
No kernel may reach another device: no remote copies, remote signals or barrier semaphores. Data moves between devices by JAX's collectives and lax.ppermute only.
A program may use at most 128 MiB of HBM per device.

v0:
```python
import jax
import jax.numpy as jnp
from jax import lax
from jax.sharding import PartitionSpec as P

GROUP_SIZE = 16


def toeplitz_block(window, positions):
    leading = window.shape[0]
    repeated = jnp.broadcast_to(window[:, None, :], (leading, positions, 2 * positions))
    flattened = repeated.reshape(leading, 2 * positions * positions)[
        :, : positions * (2 * positions - 1)
    ]
    skewed = flattened.reshape(leading, positions, 2 * positions - 1)
    return skewed[:, :, positions - 1 :]


def diagonal_sums(products, positions):
    leading = products.shape[0]
    flattened = products.reshape(leading, 2 * positions * positions)[
        :, : positions * (2 * positions - 1)
    ]
    return jnp.sum(flattened.reshape(leading, positions, 2 * positions - 1), axis=1)


def per_device(inputs, output_grad, filters):
    sequences, channels, positions = inputs.shape
    group_count = channels // GROUP_SIZE
    shard_count = lax.axis_size("seq")
    own_index = lax.axis_index("seq")
    whole_filter = lax.all_gather(filters, "seq", axis=1, tiled=True)
    padded = jnp.pad(whole_filter, ((0, 0), (positions, positions)))
    zero_column = jnp.zeros((group_count, 1), filters.dtype)
    own_grads = output_grad.reshape(sequences, group_count, GROUP_SIZE, positions)
    grads_padded = jnp.pad(own_grads, ((0, 0), (0, 0), (0, 0), (0, positions)))

    def input_term(running, grad_block, lag_block):
        window = lax.dynamic_slice_in_dim(padded, lag_block * positions + 1, 2 * positions - 1, 1)
        matrix = toeplitz_block(jnp.concatenate([window, zero_column], axis=1), positions)
        return running + jnp.einsum(
            "bgct,gst->bgcs", grad_block, matrix, preferred_element_type=jnp.float32
        )

    def filter_term(running, input_block, lag_block):
        products = jnp.einsum(
            "bgcs,bgct->gst",
            input_block[..., ::-1],
            grads_padded,
            preferred_element_type=jnp.float32,
        )
        diagonal = diagonal_sums(products, positions)
        first_row = lag_block * positions + 1
        current = lax.dynamic_slice_in_dim(running, first_row, 2 * positions - 1, 1)
        return lax.dynamic_update_slice_in_dim(running, current + diagonal, first_row, 1)

    def add_input(input_sums, grad_block, source):
        return lax.cond(
            source >= own_index,
            lambda values: input_term(values, grad_block, source - own_index),
            lambda values: values,
            input_sums,
        )

    def add_filter(lag_sums, input_block, source):
        return lax.cond(
            source <= own_index,
            lambda values: filter_term(values, input_block, own_index - source),
            lambda values: values,
            lag_sums,
        )

    input_sums = jnp.zeros((sequences, group_count, GROUP_SIZE, positions), jnp.float32)
    lag_sums = jnp.zeros((group_count, (shard_count + 1) * positions), jnp.float32)
    input_piece = lax.all_gather(inputs, "seq", axis=2, tiled=True)
    grad_piece = lax.all_gather(output_grad, "seq", axis=2, tiled=True)
    block_count = input_piece.shape[2] // positions

    def advance(distance, state):
        input_block = lax.dynamic_slice_in_dim(
            input_piece, distance * positions, positions, 2
        ).reshape(sequences, group_count, GROUP_SIZE, positions)
        grad_block = lax.dynamic_slice_in_dim(
            grad_piece, distance * positions, positions, 2
        ).reshape(sequences, group_count, GROUP_SIZE, positions)
        return (
            add_input(state[0], grad_block, distance),
            add_filter(state[1], input_block, distance),
        )

    input_sums, lag_sums = lax.fori_loop(0, block_count, advance, (input_sums, lag_sums))
    lag_terms = lag_sums[:, positions:]
    shares = lax.psum_scatter(lag_terms, "seq", scatter_dimension=1, tiled=True)
    filter_grad = lax.psum(shares, "dp")
    input_grad = input_sums.reshape(sequences, channels, positions).astype(jnp.bfloat16)
    return (input_grad, filter_grad)


def solution(mesh):
    in_specs = (P("dp", "chan", "seq"), P("dp", "chan", "seq"), P("chan", "seq"))
    out_specs = (P("dp", "chan", "seq"), P("chan", "seq"))
    return jax.shard_map(
        per_device, mesh=mesh, in_specs=in_specs, out_specs=out_specs, check_vma=False
    )
```

profile of v0, /device:TPU:0, one launch (start us, length us, event | category | flops | bytes accessed | tf_op | source)
XLA Modules:
  0.0 488.3 jit_solution(10993493462473023313)
XLA Ops:
  10.5 6.5 %all_gather.9 = bf16[128,512]{1,0:T(8,128)(2,1)S(1)} all-gather(bf16[128,128]{1,0:T(8,128)(2,1)S(1)} %copy-done), channel_id=1, replica_groups=mesh['seq'=4,'chan'=2,'dp'=4] {'seq'}, dimensions={1}, use_global_device_ids=true | all-gather | bytes 163840 | tf_op jit(solution)/shard_map/all_gather | solution.py:32
  17.7 29.6 %all-gather.3.cloned.1.call-done = bf16[2,2048,512]{2,1,0:T(8,128)(2,1)} async-done(((bf16[2,2048,128]{2,1,0:T(8,128)(2,1)}), bf16[2,2048,512]{2,1,0:T(8,128)(2,1)}) %all-gather.3.cloned.1.call-update) | async-done | bytes 4194320 | tf_op jit(solution)/shard_map/all_gather | solution.py:76
  47.3 36.6 %all-gather.5.cloned.1.call-done = bf16[2,2048,512]{2,1,0:T(8,128)(2,1)} async-done(((bf16[2,2048,128]{2,1,0:T(8,128)(2,1)}), bf16[2,2048,512]{2,1,0:T(8,128)(2,1)}) %all-gather.5.cloned.1.call-update) | async-done | bytes 4194320 | tf_op jit(solution)/shard_map/all_gather | solution.py:75
  85.6 319.9 %while.21 = (s32[]{:T(128)}, f32[2,128,16,128]{3,2,0,1:T(8,128)}, f32[128,640]{1,0:T(8,128)S(1)}, s32[]{:T(128)}, bf16[128,768]{1,0:T(8,128)(2,1)}, /*index=5*/b...) while((s32[]{:T(128)}, f32[2,128,16,128]{3,2,0,1:T(8,128)}, ...), condition=%wide.region_6.7_spmd, body=%wide.region_0.6_spmd.sunk | while | flops 407355392 | bytes 212464352 | solution.py:91
  85.6 62.8 %conditional.4 = (f32[2,128,16,128]{3,2,0,1:T(8,128)}) conditional(s32[]{:T(128)} %convert_element_type.28, f32[2,128,16,128]{3,2,0,1:T(8,128)} %get-tuple-element.312, (s32[]{:T(128)}, s32[]{:T(128)}, bf16[128,768]{1,0:T(8,128)(2,1)}, bf16[2,2048,512]{2,1,0:T(8,128)(2,1)}, s32[]{:T(128)}, /*index=5*/f32[2,128,16,128]{3,2,0,1:T(8,128)}) %tuple.59), branch_computations={%region_1.1_spmd, %region_2.2_spmd} | conditional | flops 134742016 | bytes 70450520 | solution.py:58
  86.6 3.8 broadcast_in_dim.1
  90.4 12.3 %copy.14 = bf16[16,8,128,256]{3,1,2,0:T(8,128)(2,1)} copy(bf16[16,8,128,256]{3,2,1,0:T(8,128)(2,1)} %bitcast.21) | data formatting | bytes 16777216 | tf_op jit(solution)/shard_map/while/body/eval_jaxpr/cond
  102.8 7.1 %slice.16 = bf16[128,32640]{1,0:T(8,128)(2,1)} slice(bf16[128,32768]{1,0:T(8,128)(2,1)} %bitcast.22), slice={[0:128], [0:32640]} | slice | bytes 16711680 | tf_op jit(solution)/shard_map/while/body/eval_jaxpr/cond/branch_1_fun/slice | solution.py:12
  109.9 29.5 %reshape.38 = bf16[128,128,255]{2,1,0:T(8,128)(2,1)} reshape(bf16[128,32640]{1,0:T(8,128)(2,1)} %slice.16) | data formatting | bytes 16711680 | tf_op jit(solution)/shard_map/while/body/eval_jaxpr/cond/branch_1_fun/reshape | solution.py:15
  140.7 7.7 %bitcast_add_fusion = f32[2,128,16,128]{3,2,0,1:T(8,128)} fusion(f32[2,128,16,128]{3,2,0,1:T(8,128)} %get-tuple-element.199, bf16[128,128,255]{2,1,0:T(8,128)(2,1)} %reshape.38, bf16[2,128,16,128]{3,2,1,0:T(8,128)(2,1)S(1)} %bitcast.23), kind=kOutput, calls=%fused_computation.2 | convolution fusion | flops 134742016 | bytes 9437184 | tf_op jit(solution)/shard_map/while/body/eval_jaxpr/cond/branch_1_fun/bgct,gst->bgcs/dot_general | solution.py:41
  148.4 68.8 %conditional.5 = (f32[128,640]{1,0:T(8,128)S(1)}) conditional(s32[]{:T(128)} %convert_element_type.29, f32[128,640]{1,0:T(8,128)S(1)} %get-tuple-element.313, (s32[]{:T(128)}, s32[]{:T(128)}, f32[128,640]{1,0:T(8,128)S(1)}, bf16[2,2048,512]{2,1,0:T(8,128)(2,1)}, s32[]{:T(128)}, /*index=5*/bf16[2,128,16,256]{3,2,0,1:T(8,128)(2,1)S(1)}) %tuple.60), branch_computations={%region_3.3_spmd, %region_4.5_spmd} | conditional | flops 272613376 | bytes 142013536 | solution.py:66
  155.5 11.7 %copy.15 = f32[16,8,128,256]{3,1,2,0:T(8,128)} copy(f32[16,8,128,256]{3,2,1,0:T(8,128)S(1)} %bitcast.19) | data formatting | bytes 33554432 | tf_op jit(solution)/shard_map/while/body/eval_jaxpr/cond
  167.2 11.3 %slice.18 = f32[128,32640]{1,0:T(8,128)} slice(f32[128,32768]{1,0:T(8,128)} %bitcast.20), slice={[0:128], [0:32640]} | slice | bytes 33423360 | tf_op jit(solution)/shard_map/while/body/eval_jaxpr/cond/branch_1_fun/slice | solution.py:21
  178.5 28.9 %reshape.42 = f32[128,128,255]{2,1,0:T(8,128)} reshape(f32[128,32640]{1,0:T(8,128)} %slice.18) | data formatting | bytes 33423360 | tf_op jit(solution)/shard_map/while/body/eval_jaxpr/cond/branch_1_fun/reshape | solution.py:24
  207.4 8.3 %reduce_sum.9 = f32[128,255]{1,0:T(8,128)S(1)} reduce(f32[128,128,255]{2,1,0:T(8,128)} %reshape.42, f32[]{:T(128)} %constant.66.clone), dimensions={1}, to_apply=%region_5.4 | reduce | flops 4145280 | bytes 16842244 | tf_op jit(solution)/shard_map/while/body/eval_jaxpr/cond/branch_1_fun/reduce_sum | solution.py:24
  217.2 62.8 %conditional.4 = (f32[2,128,16,128]{3,2,0,1:T(8,128)}) conditional(s32[]{:T(128)} %convert_element_type.28, f32[2,128,16,128]{3,2,0,1:T(8,128)} %get-tuple-element.312, (s32[]{:T(128)}, s32[]{:T(128)}, bf16[128,768]{1,0:T(8,128)(2,1)}, bf16[2,2048,512]{2,1,0:T(8,128)(2,1)}, s32[]{:T(128)}, /*index=5*/f32[2,128,16,128]{3,2,0,1:T(8,128)}) %tuple.59), branch_computations={%region_1.1_spmd, %region_2.2_spmd} | conditional | flops 134742016 | bytes 70450520 | solution.py:58
  222.0 12.3 %copy.14 = bf16[16,8,128,256]{3,1,2,0:T(8,128)(2,1)} copy(bf16[16,8,128,256]{3,2,1,0:T(8,128)(2,1)} %bitcast.21) | data formatting | bytes 16777216 | tf_op jit(solution)/shard_map/while/body/eval_jaxpr/cond
  234.4 7.1 %slice.16 = bf16[128,32640]{1,0:T(8,128)(2,1)} slice(bf16[128,32768]{1,0:T(8,128)(2,1)} %bitcast.22), slice={[0:128], [0:32640]} | slice | bytes 16711680 | tf_op jit(solution)/shard_map/while/body/eval_jaxpr/cond/branch_1_fun/slice | solution.py:12
  241.5 29.5 %reshape.38 = bf16[128,128,255]{2,1,0:T(8,128)(2,1)} reshape(bf16[128,32640]{1,0:T(8,128)(2,1)} %slice.16) | data formatting | bytes 16711680 | tf_op jit(solution)/shard_map/while/body/eval_jaxpr/cond/branch_1_fun/reshape | solution.py:15
  272.3 7.7 %bitcast_add_fusion = f32[2,128,16,128]{3,2,0,1:T(8,128)} fusion(f32[2,128,16,128]{3,2,0,1:T(8,128)} %get-tuple-element.199, bf16[128,128,255]{2,1,0:T(8,128)(2,1)} %reshape.38, bf16[2,128,16,128]{3,2,1,0:T(8,128)(2,1)S(1)} %bitcast.23), kind=kOutput, calls=%fused_computation.2 | convolution fusion | flops 134742016 | bytes 9437184 | tf_op jit(solution)/shard_map/while/body/eval_jaxpr/cond/branch_1_fun/bgct,gst->bgcs/dot_general | solution.py:41
  280.0 62.7 %conditional.4 = (f32[2,128,16,128]{3,2,0,1:T(8,128)}) conditional(s32[]{:T(128)} %convert_element_type.28, f32[2,128,16,128]{3,2,0,1:T(8,128)} %get-tuple-element.312, (s32[]{:T(128)}, s32[]{:T(128)}, bf16[128,768]{1,0:T(8,128)(2,1)}, bf16[2,2048,512]{2,1,0:T(8,128)(2,1)}, s32[]{:T(128)}, /*index=5*/f32[2,128,16,128]{3,2,0,1:T(8,128)}) %tuple.59), branch_computations={%region_1.1_spmd, %region_2.2_spmd} | conditional | flops 134742016 | bytes 70450520 | solution.py:58
  284.8 12.3 %copy.14 = bf16[16,8,128,256]{3,1,2,0:T(8,128)(2,1)} copy(bf16[16,8,128,256]{3,2,1,0:T(8,128)(2,1)} %bitcast.21) | data formatting | bytes 16777216 | tf_op jit(solution)/shard_map/while/body/eval_jaxpr/cond
  297.1 7.1 %slice.16 = bf16[128,32640]{1,0:T(8,128)(2,1)} slice(bf16[128,32768]{1,0:T(8,128)(2,1)} %bitcast.22), slice={[0:128], [0:32640]} | slice | bytes 16711680 | tf_op jit(solution)/shard_map/while/body/eval_jaxpr/cond/branch_1_fun/slice | solution.py:12
  304.2 29.5 %reshape.38 = bf16[128,128,255]{2,1,0:T(8,128)(2,1)} reshape(bf16[128,32640]{1,0:T(8,128)(2,1)} %slice.16) | data formatting | bytes 16711680 | tf_op jit(solution)/shard_map/while/body/eval_jaxpr/cond/branch_1_fun/reshape | solution.py:15
  335.0 7.7 %bitcast_add_fusion = f32[2,128,16,128]{3,2,0,1:T(8,128)} fusion(f32[2,128,16,128]{3,2,0,1:T(8,128)} %get-tuple-element.199, bf16[128,128,255]{2,1,0:T(8,128)(2,1)} %reshape.38, bf16[2,128,16,128]{3,2,1,0:T(8,128)(2,1)S(1)} %bitcast.23), kind=kOutput, calls=%fused_computation.2 | convolution fusion | flops 134742016 | bytes 9437184 | tf_op jit(solution)/shard_map/while/body/eval_jaxpr/cond/branch_1_fun/bgct,gst->bgcs/dot_general | solution.py:41
  342.7 62.7 %conditional.4 = (f32[2,128,16,128]{3,2,0,1:T(8,128)}) conditional(s32[]{:T(128)} %convert_element_type.28, f32[2,128,16,128]{3,2,0,1:T(8,128)} %get-tuple-element.312, (s32[]{:T(128)}, s32[]{:T(128)}, bf16[128,768]{1,0:T(8,128)(2,1)}, bf16[2,2048,512]{2,1,0:T(8,128)(2,1)}, s32[]{:T(128)}, /*index=5*/f32[2,128,16,128]{3,2,0,1:T(8,128)}) %tuple.59), branch_computations={%region_1.1_spmd, %region_2.2_spmd} | conditional | flops 134742016 | bytes 70450520 | solution.py:58
  347.5 12.3 %copy.14 = bf16[16,8,128,256]{3,1,2,0:T(8,128)(2,1)} copy(bf16[16,8,128,256]{3,2,1,0:T(8,128)(2,1)} %bitcast.21) | data formatting | bytes 16777216 | tf_op jit(solution)/shard_map/while/body/eval_jaxpr/cond
  359.9 7.1 %slice.16 = bf16[128,32640]{1,0:T(8,128)(2,1)} slice(bf16[128,32768]{1,0:T(8,128)(2,1)} %bitcast.22), slice={[0:128], [0:32640]} | slice | bytes 16711680 | tf_op jit(solution)/shard_map/while/body/eval_jaxpr/cond/branch_1_fun/slice | solution.py:12
  367.0 29.5 %reshape.38 = bf16[128,128,255]{2,1,0:T(8,128)(2,1)} reshape(bf16[128,32640]{1,0:T(8,128)(2,1)} %slice.16) | data formatting | bytes 16711680 | tf_op jit(solution)/shard_map/while/body/eval_jaxpr/cond/branch_1_fun/reshape | solution.py:15
  397.8 7.7 %bitcast_add_fusion = f32[2,128,16,128]{3,2,0,1:T(8,128)} fusion(f32[2,128,16,128]{3,2,0,1:T(8,128)} %get-tuple-element.199, bf16[128,128,255]{2,1,0:T(8,128)(2,1)} %reshape.38, bf16[2,128,16,128]{3,2,1,0:T(8,128)(2,1)S(1)} %bitcast.23), kind=kOutput, calls=%fused_computation.2 | convolution fusion | flops 134742016 | bytes 9437184 | tf_op jit(solution)/shard_map/while/body/eval_jaxpr/cond/branch_1_fun/bgct,gst->bgcs/dot_general | solution.py:41
  406.3 37.8 %reduce-scatter.2.cloned.1.call-done = f32[128,128]{1,0:T(8,128)} async-done(((f32[128,512]{1,0:T(8,128)}), f32[128,128]{1,0:T(8,128)}) %reduce-scatter.2.cloned.1.call-update) | async-done | bytes 65552 | tf_op jit(solution)/shard_map/reduce_scatter | solution.py:93
  447.0 33.3 %all-reduce.5.cloned.1.call-done = f32[128,128]{1,0:T(8,128)} async-done(((f32[128,128]{1,0:T(8,128)}), f32[128,128]{1,0:T(8,128)}) %all-reduce.5.cloned.1.call-update) | async-done | bytes 65552 | tf_op jit(solution)/shard_map/psum | solution.py:94
  (42 shorter events, 39.8 us)
Async XLA Ops:
  7.2 3.3 copy-start
  7.2 40.1 %all-gather.3.cloned.1.call-start = ((), (), s32[]{:S(2)}) async-start(), calls=%async_computation.1 | async-start | bytes 5242880 | tf_op jit(solution)/shard_map/all_gather | solution.py:76
  7.9 76.0 %all-gather.5.cloned.1.call-start = ((), (), s32[]{:S(2)}) async-start(), calls=%async_computation.2 | async-start | bytes 5242880 | tf_op jit(solution)/shard_map/all_gather | solution.py:75
  8.7 435.4 %reduce-scatter.2.cloned.1.call-start = ((), (), s32[]{:S(2)}) async-start(), calls=%async_computation.3 | async-start | bytes 327680 | tf_op jit(solution)/shard_map/reduce_scatter | solution.py:93
  406.2 74.1 %all-reduce.5.cloned.1.call-start = ((), (), s32[]{:S(2)}) async-start(), calls=%async_computation.4 | async-start | bytes 131072 | tf_op jit(solution)/shard_map/psum | solution.py:94
Sparse Core Ops, SparseCore 0:
  9.6 37.7 all-gather.2
  48.9 35.0 all-gather.4
  406.3 37.6 reduce-scatter.1
  446.3 33.9 all-reduce.4
where the time goes:
time: 489 us; the launch traced here: 488 us
  local copies, waits for them, and re-layouts  286 us (58%)
  waiting for transfers between devices  139 us (28%)
  matrix products  33.2 us (7%)
  between operations  13.8 us (3%)
  other arithmetic  10.2 us (2%)
  blocking collectives  6.54 us (1%)
    reshape x4, local copies, waits for them, and re-layouts, toeplitz_block(): skewed = flattened.reshape(leading, positions, 2 * positions - 1)  118 us
    cond x5, local copies, waits for them, and re-layouts  61.1 us
    reduce_scatter x1, waiting for transfers between devices, per_device(): shares = lax.psum_scatter(lag_terms, 'seq', scatter_dimension=1, tiled=True)  37.8 us
    all_gather x1, waiting for transfers between devices, per_device(): input_piece = lax.all_gather(inputs, 'seq', axis=2, tiled=True)  36.6 us
    psum x1, waiting for transfers between devices, per_device(): filter_grad = lax.psum(shares, 'dp')  33.3 us
    dot_general x4, matrix products, input_term(): jnp.einsum('bgct,gst->bgcs', grad_block, matrix, preferred_element_type=j...  30.8 us
    all_gather x1, waiting for transfers between devices, per_device(): grad_piece = lax.all_gather(output_grad, 'seq', axis=2, tiled=True)  29.6 us
    reshape x1, local copies, waits for them, and re-layouts, diagonal_sums(): flattened.reshape(leading, positions, 2 * positions - 1)  28.9 us
  transfers between devices with their start and end apart: 4, of which 4 were waited for; matrix products, arithmetic and copies ran while one was open for 1% of the time, Pallas kernels for 0%

commit v1 on v0

v1 whole, which is shorter than its diff:
```python
import functools

import jax
import jax.numpy as jnp
from jax import lax
from jax.experimental import pallas as pl
from jax.experimental.pallas import tpu as pltpu
from jax.sharding import PartitionSpec as P

GROUP_SIZE = 16
CORES = 2
VMEM_BYTES = 40 << 20


def pick(condition, first, second):
    return jnp.where(condition, first, second)


def group_rows(ref, index):
    sequences, _, positions = ref.shape
    start = pl.multiple_of(index * GROUP_SIZE, GROUP_SIZE)
    return ref[:, pl.ds(start, GROUP_SIZE), :].reshape(sequences * GROUP_SIZE, positions)


def input_grad_kernel(chips, place, *refs):
    lag_blocks = CORES * chips
    filter_refs, refs = refs[:lag_blocks], refs[lag_blocks:]
    own_grad, peer_grad, refs = refs[0], refs[1], refs[2:]
    round_refs, (mine, theirs, taps) = refs[: 2 * (chips - 1)], refs[2 * (chips - 1) :]
    first_core = place[0] == 0
    chip = place[1]
    sequences, channels, positions = own_grad.shape
    rows = sequences * GROUP_SIZE
    width = lag_blocks * positions
    taps[...] = jnp.concatenate([ref[...] for ref in filter_refs], axis=1).astype(jnp.float32)
    row = lax.broadcasted_iota(jnp.int32, (positions, width), 0)
    column = lax.broadcasted_iota(jnp.int32, (positions, width), 1)
    causal = column >= row

    def one_group(index, carry):
        strip = jnp.broadcast_to(taps[pl.ds(index, 1), :], (positions, width))
        strip = pltpu.roll(strip, 0, 1, stride=1, stride_axis=0)
        strip = jnp.where(causal, strip, 0.0).astype(jnp.bfloat16)
        zeros = jnp.zeros((rows, positions), jnp.bfloat16)
        own, peer = group_rows(own_grad, index), group_rows(peer_grad, index)
        blocks = [pick(first_core, own, peer), pick(first_core, peer, own)]
        for distance in range(1, chips):
            received = [group_rows(ref, index) for ref in round_refs[2 * distance - 2 : 2 * distance]]
            lower = chip + distance < chips
            blocks.append(pick(lower, pick(first_core, *received), zeros))
            blocks.append(pick(lower, pick(first_core, *received[::-1]), zeros))
        grads = jnp.concatenate(
            [jnp.concatenate(blocks, axis=1), jnp.concatenate(blocks[1:] + [zeros], axis=1)], axis=0
        )
        sums = lax.dot_general(
            grads, strip, (((1,), (1,)), ((), ())), preferred_element_type=jnp.float32
        ).astype(jnp.bfloat16)
        start = pl.multiple_of(index * GROUP_SIZE, GROUP_SIZE)
        shape = (sequences, GROUP_SIZE, positions)
        early, late = sums[:rows], sums[rows:]
        mine[:, pl.ds(start, GROUP_SIZE), :] = pick(first_core, early, late).reshape(shape)
        theirs[:, pl.ds(start, GROUP_SIZE), :] = pick(first_core, late, early).reshape(shape)
        return carry

    lax.fori_loop(0, channels // GROUP_SIZE, one_group, 0, unroll=4)


def reversal(positions):
    row = lax.broadcasted_iota(jnp.int32, (positions, positions), 0)
    column = lax.broadcasted_iota(jnp.int32, (positions, positions), 1)
    return (row + column == positions - 1).astype(jnp.float32).astype(jnp.bfloat16)


def lag_sums(values, grads, flip, keep):
    positions, width = flip.shape[0], grads.shape[1]
    flipped = jnp.dot(values, flip, preferred_element_type=jnp.float32).astype(jnp.bfloat16)
    products = lax.dot_general(
        flipped, grads, (((0,), (0,)), ((), ())), preferred_element_type=jnp.float32
    )
    if keep is not None:
        products = jnp.where(keep, products, 0.0)
    products = pltpu.roll(products, width - positions + 1, 1, stride=1, stride_axis=0)
    return jnp.sum(products, axis=0, keepdims=True)


def own_lags_kernel(place, own_input, peer_input, own_grad, peer_grad, out):
    first_core = place[0] == 0
    sequences, channels, positions = own_input.shape
    rows, width = sequences * GROUP_SIZE, CORES * positions
    flip = reversal(positions)
    row = lax.broadcasted_iota(jnp.int32, (positions, width), 0)
    column = lax.broadcasted_iota(jnp.int32, (positions, width), 1)
    keep = column + row >= positions - 1

    def one_group(index, carry):
        own, peer = group_rows(own_input, index), group_rows(peer_input, index)
        values = jnp.concatenate([pick(first_core, own, peer), pick(first_core, peer, own)], axis=0)
        own, peer = group_rows(own_grad, index), group_rows(peer_grad, index)
        early, late = pick(first_core, own, peer), pick(first_core, peer, own)
        grads = jnp.concatenate(
            [
                jnp.concatenate([early, late], axis=1),
                jnp.concatenate([late, jnp.zeros((rows, positions), jnp.bfloat16)], axis=1),
            ],
            axis=0,
        )
        out[pl.ds(index, 1), :] = lag_sums(values, grads, flip, keep)
        return carry

    lax.fori_loop(0, channels // GROUP_SIZE, one_group, 0, unroll=4)


def round_lags_kernel(
    chips, distance, place, own_input, peer_input, own_grad, peer_grad, own_got, peer_got, running, out
):
    first_core = place[0] == 0
    lower = place[1] + distance < chips
    sequences, channels, positions = own_input.shape
    rows = sequences * GROUP_SIZE
    flip = reversal(positions)
    out[...] = running[...]
    if 2 * distance == chips:
        first_lag = (2 * distance - 2) * positions
    else:
        first_lag = pl.multiple_of(
            jnp.where(lower, 2 * distance - 2, 2 * (chips - distance) - 2) * positions, positions
        )

    def one_group(index, carry):
        got = group_rows(own_got, index), group_rows(peer_got, index)
        inputs = group_rows(own_input, index), group_rows(peer_input, index)
        grads = group_rows(own_grad, index), group_rows(peer_grad, index)
        left = [pick(lower, a, b) for a, b in zip(inputs, got)]
        right = [pick(lower, b, a) for a, b in zip(grads, got)]
        values = jnp.concatenate([pick(first_core, *left), pick(first_core, *left[::-1])], axis=0)
        early, late = pick(first_core, *right), pick(first_core, *right[::-1])
        zeros = jnp.zeros((rows, positions), jnp.bfloat16)
        pairs = jnp.concatenate(
            [
                jnp.concatenate([zeros, zeros, early, late], axis=1),
                jnp.concatenate([zeros, early, late, zeros], axis=1),
            ],
            axis=0,
        )
        where = (pl.ds(index, 1), pl.ds(first_lag, 2 * CORES * positions))
        out[where] = out[where] + lag_sums(values, pairs, flip, None)
        return carry

    lax.fori_loop(0, channels // GROUP_SIZE, one_group, 0, unroll=4)


def per_device(inputs, output_grad, filters):
    sequences, channels, positions = inputs.shape
    shard_count = lax.axis_size("seq")
    chips = shard_count // CORES
    own_index = lax.axis_index("seq")
    chip, core = own_index // CORES, own_index % CORES
    place = jnp.stack([core, chip]).astype(jnp.int32)
    half = channels // CORES
    part = half // 2
    groups, part_groups = half // GROUP_SIZE, part // GROUP_SIZE
    length = shard_count * positions

    def swap_cores(value):
        return lax.ppermute(value, "seq", [(i, i ^ 1) for i in range(shard_count)])

    def half_of(value, which):
        return lax.dynamic_slice_in_dim(value, which * half, half, 1)

    def from_chip(value, distance, wrap):
        pairs = [
            (i, (i - distance * CORES) % shard_count)
            for i in range(shard_count)
            if wrap or i >= distance * CORES
        ]
        return lax.ppermute(value, "seq", pairs)

    grad_own, input_own = half_of(output_grad, core), half_of(inputs, core)
    grad_peer = swap_cores(half_of(output_grad, 1 - core))
    input_peer = swap_cores(half_of(inputs, 1 - core))

    rounds = range(1, chips)
    first, second = {}, {}
    for k in rounds:
        sends_grad = chip >= k
        first[k] = (
            from_chip(jnp.where(sends_grad, grad_own[:, :part], input_own[:, part:]), k, True),
            from_chip(jnp.where(sends_grad, grad_peer[:, :part], input_peer[:, part:]), k, True),
        )
    for k in rounds:
        second[k] = (
            from_chip(grad_own[:, part:], k, False),
            from_chip(grad_peer[:, part:], k, False),
        )

    taps = jnp.stack([filters, swap_cores(filters)])
    taps = jnp.stack([taps] + [from_chip(taps, k, True) for k in rounds])

    step = min(16, part_groups)
    block = (sequences, step * GROUP_SIZE, positions)
    steps = part_groups // step

    def whole_spec(part_of=None):
        if part_of is None:
            return pl.BlockSpec(block, lambda i, place: (0, place[0] * 2 * steps + i, 0))
        return pl.BlockSpec(block, lambda i, place: (0, (place[0] * 2 + part_of(place)) * steps + i, 0))

    def half_spec(part_of=None):
        if part_of is None:
            return pl.BlockSpec(block, lambda i, place: (0, i, 0))
        return pl.BlockSpec(block, lambda i, place: (0, part_of(place) * steps + i, 0))

    part_spec = pl.BlockSpec(block, lambda i, place: (0, i, 0))
    params = pltpu.CompilerParams(vmem_limit_bytes=VMEM_BYTES)

    lags = pl.pallas_call(
        own_lags_kernel,
        grid_spec=pltpu.PrefetchScalarGridSpec(
            num_scalar_prefetch=1,
            grid=(2 * steps,),
            in_specs=[whole_spec(), half_spec(), whole_spec(), half_spec()],
            out_specs=pl.BlockSpec((step, CORES * positions), lambda i, place: (i, 0)),
        ),
        out_shape=jax.ShapeDtypeStruct((groups, CORES * positions), jnp.float32),
        compiler_params=params,
    )(place, inputs, input_peer, output_grad, grad_peer)
    lags = jnp.pad(lags, ((0, 0), (0, length - CORES * positions)))

    for k in rounds:
        def part_of(place, k=k):
            return jnp.where(place[1] + k < chips, 0, 1)

        lag_spec = pl.BlockSpec((step, length), lambda i, place, part_of=part_of: (part_of(place) * steps + i, 0))
        lags = pl.pallas_call(
            functools.partial(round_lags_kernel, chips, k),
            grid_spec=pltpu.PrefetchScalarGridSpec(
                num_scalar_prefetch=1,
                grid=(steps,),
                in_specs=[
                    whole_spec(part_of), half_spec(part_of), whole_spec(part_of), half_spec(part_of),
                    part_spec, part_spec, lag_spec,
                ],
                out_specs=lag_spec,
            ),
            out_shape=jax.ShapeDtypeStruct((groups, length), jnp.float32),
            input_output_aliases={7: 0},
            compiler_params=params,
        )(place, inputs, input_peer, output_grad, grad_peer, *first[k], lags)

    def input_part(which, received):
        def fixed(place):
            return which

        def filter_spec(block_index):
            def index(i, place):
                rotation = lax.rem(block_index // CORES - place[1] + chips, chips)
                other = jnp.where(place[0] == block_index % CORES, 0, 1)
                return (rotation, other, (place[0] * 2 + which) * steps + i, 0)

            return pl.BlockSpec((None, None, step, positions), index)

        arrays = [ref for k in rounds for ref in received[k]]
        return pl.pallas_call(
            functools.partial(input_grad_kernel, chips),
            grid_spec=pltpu.PrefetchScalarGridSpec(
                num_scalar_prefetch=1,
                grid=(steps,),
                in_specs=[filter_spec(q) for q in range(shard_count)]
                + [whole_spec(fixed), half_spec(fixed)]
                + [part_spec] * len(arrays),
                out_specs=[part_spec, part_spec],
                scratch_shapes=[pltpu.VMEM((step, length), jnp.float32)],
            ),
            out_shape=[jax.ShapeDtypeStruct((sequences, part, positions), jnp.bfloat16)] * 2,
            compiler_params=params,
        )(place, *([taps] * shard_count), output_grad, grad_peer, *arrays)

    parts = []
    for which, received in ((0, first), (1, second)):
        mine, theirs = input_part(which, received)
        parts.append((mine, swap_cores(theirs)))
    mine = jnp.concatenate([p[0] for p in parts], axis=1)
    got = jnp.concatenate([p[1] for p in parts], axis=1)
    input_grad = jnp.where(
        core == 0, jnp.concatenate([mine, got], axis=1), jnp.concatenate([got, mine], axis=1)
    )

    def chip_lags(which):
        return lax.dynamic_slice_in_dim(lags, which * CORES * positions, CORES * positions, 1)

    sums = chip_lags(chip)
    for k in rounds:
        sums = sums + from_chip(chip_lags((chip - k) % chips), k, True)
    keep = lax.dynamic_slice_in_dim(sums, core * positions, positions, 1)
    got = swap_cores(lax.dynamic_slice_in_dim(sums, (1 - core) * positions, positions, 1))
    own = jnp.where(core == 0, jnp.concatenate([keep, got], axis=0), jnp.concatenate([got, keep], axis=0))
    copies = lax.axis_size("dp")
    terms = [own]
    for k in range(1, copies):
        terms.append(lax.ppermute(own, "dp", [(i, i ^ k) for i in range(copies)]))
    while len(terms) > 1:
        terms = [a + b for a, b in zip(terms[::2], terms[1::2])]
    filter_grad = terms[0]
    return (input_grad, filter_grad)


def solution(mesh):
    in_specs = (P("dp", "chan", "seq"), P("dp", "chan", "seq"), P("chan", "seq"))
    out_specs = (P("dp", "chan", "seq"), P("chan", "seq"))
    return jax.shard_map(
        per_device, mesh=mesh, in_specs=in_specs, out_specs=out_specs, check_vma=False
    )
```

time: 489 us -> 67.2 us (0.14)
  local copies, waits for them, and re-layouts: 286 us -> 2.91 us
  waiting for transfers between devices: 139 us -> 8.19 us
  matrix products: 33.2 us -> 0 us
  Pallas kernels: 0 us -> 31.4 us
  starting transfers between devices: 0.16 us -> 19.1 us
  between operations: 13.8 us -> 0.85 us
  blocking collectives: 6.54 us -> 0 us
  other arithmetic: 10.2 us -> 4.45 us
    reshape x5 -> x0, local copies, waits for them, and re-layouts: 147 us -> none  [the longest x4 118 us: toeplitz_block(): skewed = flattened.reshape(leading, positions, 2 * positions - 1)]
    all_gather x2 -> x0, waiting for transfers between devices: 66.2 us -> none  [the longest x1 36.6 us: per_device(): input_piece = lax.all_gather(inputs, 'seq', axis=2, tiled=True)]
    cond x5 -> x0, local copies, waits for them, and re-layouts: 61.1 us -> none
    slice x6 -> x0, local copies, waits for them, and re-layouts: 40.5 us -> none  [the longest x4 28.5 us: toeplitz_block(): repeated.reshape(leading, 2 * positions * positions)]
    reduce_scatter x1 -> x0, waiting for transfers between devices: 37.8 us -> none  [per_device(): shares = lax.psum_scatter(lag_terms, 'seq', scatter_dimension=1, tiled=True)]
    psum x1 -> x0, waiting for transfers between devices: 33.3 us -> none  [per_device(): filter_grad = lax.psum(shares, 'dp')]
    dot_general x5 -> x0, matrix products: 33.2 us -> none  [the longest x4 30.8 us: input_term(): jnp.einsum('bgct,gst->bgcs', grad_block, matrix, preferred_element_type=j...]
    pallas_call x0 -> x4, Pallas kernels: none -> 31.4 us  [the longest x1 11.8 us: per_device(): pl.pallas_call(own_lags_kernel, grid_spec=pltpu.PrefetchScalarGridSpec(nu...]
  transfers between devices with their start and end apart: 4 -> 15, of which waited for: 4 -> 3; matrix products, arithmetic and copies ran while one was open for 1% -> 6% of each run, Pallas kernels for 0% -> 31%
where the time goes in v1:
time: 67.2 us; the launch traced here: 66.9 us
  Pallas kernels  31.4 us (47%)
  starting transfers between devices  19.1 us (28%)
  waiting for transfers between devices  8.19 us (12%)
  other arithmetic  4.45 us (7%)
  local copies, waits for them, and re-layouts  2.91 us (4%)
  between operations  0.85 us (1%)
    pallas_call x1, Pallas kernels, per_device(): pl.pallas_call(own_lags_kernel, grid_spec=pltpu.PrefetchScalarGridSpec(nu...  11.8 us
    pallas_call x1, Pallas kernels, per_device(): pl.pallas_call(functools.partial(round_lags_kernel, chips, k), grid_spec=...  10.7 us
    ppermute x6, starting transfers between devices, from_chip(): return lax.ppermute(value, 'seq', pairs)  10.1 us
    pallas_call x2, Pallas kernels, input_part(): pl.pallas_call(functools.partial(input_grad_kernel, chips), grid_spec=plt...  8.98 us
    ppermute x3, starting transfers between devices, per_device(): terms.append(lax.ppermute(own, 'dp', [(i, i ^ k) for i in range(copies)]))  7.82 us
    ppermute x6, waiting for transfers between devices, from_chip(): return lax.ppermute(value, 'seq', pairs)  7.67 us
    dynamic_slice x2, local copies, waits for them, and re-layouts, half_of(): return lax.dynamic_slice_in_dim(value, which * half, half, 1)  2.86 us
  transfers between devices with their start and end apart: 15, of which 3 were waited for; matrix products, arithmetic and copies ran while one was open for 6% of the time, Pallas kernels for 31%

profile of v1, /device:TPU:0, one launch (start us, length us, event | category | flops | bytes accessed | tf_op | source)
XLA Modules:
  0.0 66.9 jit_solution(16001912337317100021)
XLA Ops:
  0.7 2.0 %constant_dynamic-slice_fusion.5 = bf16[2,1024,128]{2,1,0:T(8,128)(2,1)} fusion(bf16[2,2048,128]{2,1,0:T(8,128)(2,1)} %own_grad.3, s32[]{:T(128)S(6)} %select_n.66), kind=kLoop, calls=%fused_computation.13 | loop fusion | bytes 1048580 | tf_op jit(solution)/shard_map/dynamic_slice | solution.py:168
  2.7 0.5 collective-permute-start.2
  3.1 0.8 %constant_dynamic-slice_fusion.3 = bf16[2,1024,128]{2,1,0:T(8,128)(2,1)} fusion(bf16[2,2048,128]{2,1,0:T(8,128)(2,1)S(1)} %copy-done.1, s32[]{:T(128)S(6)} %select_n.66), kind=kLoop, calls=%fused_computation.11 | loop fusion | bytes 1048580 | tf_op jit(solution)/shard_map/dynamic_slice | solution.py:168
  4.0 0.1 collective-permute-start.4
  4.0 0.8 %dynamic-slice_select_fusion = (bf16[2,512,128]{2,1,0:T(8,128)(2,1)}, bf16[2,512,128]{2,1,0:T(8,128)(2,1)}) fusion(bf16[2,2048,128]{2,1,0:T(8,128)(2,1)S(1)} %copy-done.1, s32[]{:T(128)S(6)} %add.56, bf16[2,2048,128]{2,1,0:T(8,128)(2,1)S(1)} %copy-done, s32[]{:T(128)S(6)} %select_n.68, pred[]{:T(512)S(6)} %ge.3), kind=kLoop, calls=%fused_computation.2 | loop fusion | flops 131072 | bytes 1310729 | tf_op jit(solution)/shard_map/jit(_where)/select_n | solution.py:187
  4.9 3.0 %collective-permute-start.3 = (bf16[2,512,128]{2,1,0:T(8,128)(2,1)}, bf16[2,512,128]{2,1,0:T(8,128)(2,1)S(1)}, u32[]{:S(2)}, u32[]{:S(2)}) collective-permute-start(bf16[2,512,128]{2,1,0:T(8,128)(2,1)} %get-tuple-element.10), channel_id=1, source_target_pairs={{0,16},{8,24},{16,0},{24,8},{1,17},{9,25},{17,1},{25,9},{2,18},{10... | collective-permute-start | bytes 786440 | tf_op jit(solution)/shard_map/ppermute | solution.py:176
  7.9 0.0 collective-permute-done.2.refs_5_.peer_grad
  7.9 0.0 collective-permute-done.4.peer_input
  7.9 0.9 %slice_select_fusion = (bf16[2,512,128]{2,1,0:T(8,128)(2,1)}, bf16[2,512,128]{2,1,0:T(8,128)(2,1)}) fusion(bf16[2,1024,128]{2,1,0:T(8,128)(2,1)S(1)} %collective-permute-done.4.peer_input, bf16[2,1024,128]{2,1,0:T(8,128)(2,1)S(1)} %collective-permute-done.2.refs_5_.peer_grad, pred[]{:T(512)S(6)} %ge.3), kind=kLoop, calls=%fused_computation.1 | loop fusion | flops 131072 | bytes 1310721 | tf_op jit(solution)/shard_map/jit(_where)/select_n | solution.py:188
  8.7 0.9 %collective-permute-start.5 = (bf16[2,512,128]{2,1,0:T(8,128)(2,1)}, bf16[2,512,128]{2,1,0:T(8,128)(2,1)}, u32[]{:S(2)}, u32[]{:S(2)}) collective-permute-start(bf16[2,512,128]{2,1,0:T(8,128)(2,1)} %get-tuple-element.12), channel_id=1, source_target_pairs={{0,16},{8,24},{16,0},{24,8},{1,17},{9,25},{17,1},{25,9},{2,18},{10... | collective-permute-start | bytes 786440 | tf_op jit(solution)/shard_map/ppermute | solution.py:176
  9.6 0.1 pad_add_fusion.place
  9.7 11.8 %shard_map.52 = f32[64,256]{1,0:T(8,128)S(1)} custom-call(s32[2]{0:T(128)S(1)} %pad_add_fusion.place, bf16[2,2048,128]{2,1,0:T(8,128)(2,1)S(1)} %copy-done.1, bf16[2,1024,128]{2,1,0:T(8,128)(2,1)S(1)} %collective-permute-done.4.peer_input, bf16[2,2048,128]{2,1,0:T(8,128)(2,1)S(1)} %copy-done, bf16[2,1024,128]{2,1,0:T(8,128)(2,1)S(1)} %collective-permute-done.2.refs_5_.peer_grad), custom_call_target="tpu_custom_call" | custom-call | tf_op jit(solution)/shard_map/pallas_call | solution.py:216
  21.5 10.7 %shard_map.53 = f32[64,512]{1,0:T(8,128)S(1)} custom-call(s32[2]{0:T(128)S(1)} %pad_add_fusion.place, bf16[2,2048,128]{2,1,0:T(8,128)(2,1)S(1)} %copy-done.1, bf16[2,1024,128]{2,1,0:T(8,128)(2,1)S(1)} %collective-permute-done.4.peer_input, bf16[2,2048,128]{2,1,0:T(8,128)(2,1)S(1)} %copy-done, ...), custom_call_target="tpu_custom_call", output_to_operand_aliasing={{}: (7, {})} | custom-call | tf_op jit(solution)/shard_map/pallas_call | solution.py:234
  32.2 1.2 %collective-permute-start.10 = (f32[64,256]{1,0:T(8,128)S(1)}, f32[64,256]{1,0:T(8,128)S(1)}, u32[]{:S(2)}, u32[]{:S(2)}) collective-permute-start(f32[64,256]{1,0:T(8,128)S(1)} %constant_dynamic-slice_fusion.2), channel_id=1, source_target_pairs={{0,16},{8,24},{16,0},{24,8},{1,17},{9,25},{17,1},{25,9},{2,18},{10... | collective-permute-start | bytes 196616 | tf_op jit(solution)/shard_map/ppermute | solution.py:176
  33.4 0.0 collective-permute-start
  33.4 1.3 %collective-permute-start.6 = (bf16[2,512,128]{2,1,0:T(8,128)(2,1)}, bf16[2,512,128]{2,1,0:T(8,128)(2,1)S(1)}, u32[]{:S(2)}, u32[]{:S(2)}) collective-permute-start(bf16[2,512,128]{2,1,0:T(8,128)(2,1)} %get-tuple-element.11), channel_id=1, source_target_pairs={{16,0},{24,8},{17,1},{25,9},{18,2},{26,10},{19,3},{27,11},{20,4},{... | collective-permute-start | bytes 786440 | tf_op jit(solution)/shard_map/ppermute | solution.py:176
  34.7 1.3 %collective-permute-start.7 = (bf16[2,512,128]{2,1,0:T(8,128)(2,1)}, bf16[2,512,128]{2,1,0:T(8,128)(2,1)S(1)}, u32[]{:S(2)}, u32[]{:S(2)}) collective-permute-start(bf16[2,512,128]{2,1,0:T(8,128)(2,1)} %get-tuple-element.13), channel_id=1, source_target_pairs={{16,0},{24,8},{17,1},{25,9},{18,2},{26,10},{19,3},{27,11},{20,4},{... | collective-permute-start | bytes 786440 | tf_op jit(solution)/shard_map/ppermute | solution.py:176
  36.0 0.5 collective-permute-done.10
  36.6 0.1 collective-permute-start.11
  36.7 0.8 %fusion = (bf16[1,2,128,128]{3,2,1,0:T(8,128)(2,1)S(1)}, bf16[2,128,128]{2,1,0:T(8,128)(2,1)S(1)}) fusion(bf16[1,128,128]{2,1,0:T(8,128)(2,1)S(1)} %bitcast.8, bf16[1,128,128]{2,1,0:T(8,128)(2,1)} %bitcast.2), kind=kLoop, calls=%fused_computation.15 | loop fusion | flops 32768 | bytes 196608 | tf_op jit(solution)/shard_map/stack | solution.py:197
  37.5 2.4 %collective-permute-start.1 = (bf16[2,128,128]{2,1,0:T(8,128)(2,1)S(1)}, bf16[2,128,128]{2,1,0:T(8,128)(2,1)S(1)}, u32[]{:S(2)}, u32[]{:S(2)}) collective-permute-start(bf16[2,128,128]{2,1,0:T(8,128)(2,1)S(1)} %get-tuple-element.17), channel_id=1, source_target_pairs={{0,16},{8,24},{16,0},{24,8},{1,17},{9,25},{17,1},{25,9},{2,18},{10... | collective-permute-start | bytes 196616 | tf_op jit(solution)/shard_map/ppermute | solution.py:176
  39.9 1.6 %collective-permute-start.12 = (f32[128,128]{1,0:T(8,128)S(1)}, f32[128,128]{1,0:T(8,128)S(1)}, u32[]{:S(2)}, u32[]{:S(2)}) collective-permute-start(f32[128,128]{1,0:T(8,128)S(1)} %maximum_select_fusion.1), channel_id=1, source_target_pairs={{0,1},{1,0},{2,3},{3,2},{4,5},{5,4},{6,7},{7,6},{8,9},{9,8},{10,11... | collective-permute-start | bytes 196616 | tf_op jit(solution)/shard_map/ppermute | solution.py:300
  41.5 2.6 %collective-permute-start.13 = (f32[128,128]{1,0:T(8,128)S(1)}, f32[128,128]{1,0:T(8,128)S(1)}, u32[]{:S(2)}, u32[]{:S(2)}) collective-permute-start(f32[128,128]{1,0:T(8,128)S(1)} %maximum_select_fusion.1), channel_id=1, source_target_pairs={{0,2},{1,3},{2,0},{3,1},{4,6},{5,7},{6,4},{7,5},{8,10},{9,11},{10,... | collective-permute-start | bytes 196616 | tf_op jit(solution)/shard_map/ppermute | solution.py:300
  44.1 7.1 %collective-permute-done.1 = bf16[2,128,128]{2,1,0:T(8,128)(2,1)S(1)} collective-permute-done((bf16[2,128,128]{2,1,0:T(8,128)(2,1)S(1)}, bf16[2,128,128]{2,1,0:T(8,128)(2,1)S(1)}, u32[]{:S(2)}, u32[]{:S(2)}) %collective-permute-start.1) | collective-permute-done | bytes 65568 | tf_op jit(solution)/shard_map/ppermute | solution.py:176
  51.3 3.6 %collective-permute-start.14 = (f32[128,128]{1,0:T(8,128)S(1)}, f32[128,128]{1,0:T(8,128)S(1)}, u32[]{:S(2)}, u32[]{:S(2)}) collective-permute-start(f32[128,128]{1,0:T(8,128)S(1)} %maximum_select_fusion.1), channel_id=1, source_target_pairs={{0,3},{1,2},{2,1},{3,0},{4,7},{5,6},{6,5},{7,4},{8,11},{9,10},{10,... | collective-permute-start | bytes 196616 | tf_op jit(solution)/shard_map/ppermute | solution.py:300
  54.9 4.9 %shard_map.50 = (bf16[2,512,128]{2,1,0:T(8,128)(2,1)S(1)}, bf16[2,512,128]{2,1,0:T(8,128)(2,1)S(1)}) custom-call(s32[2]{0:T(128)S(1)} %pad_add_fusion.place, bf16[2,2,128,128]{3,2,1,0:T(8,128)(2,1)S(1)} %pad_maximum_fusion.refs_0_.refs_1_.refs_2_.refs_3_, bf16[2,2,128,128]{3,2,1,0:T(8,128)(2,1)S(1)} %pad_maximum_fusion.refs_0_.refs_1_.refs_2_.refs_3_, ...), custom_call_target="tpu_custom_call" | custom-call | tf_op jit(solution)/shard_map/pallas_call | solution.py:263
  59.8 0.1 collective-permute-start.8
  59.9 4.1 %shard_map.51 = (bf16[2,512,128]{2,1,0:T(8,128)(2,1)S(1)}, bf16[2,512,128]{2,1,0:T(8,128)(2,1)S(1)}) custom-call(s32[2]{0:T(128)S(1)} %pad_add_fusion.place, bf16[2,2,128,128]{3,2,1,0:T(8,128)(2,1)S(1)} %pad_maximum_fusion.refs_0_.refs_1_.refs_2_.refs_3_, bf16[2,2,128,128]{3,2,1,0:T(8,128)(2,1)S(1)} %pad_maximum_fusion.refs_0_.refs_1_.refs_2_.refs_3_, ...), custom_call_target="tpu_custom_call" | custom-call | tf_op jit(solution)/shard_map/pallas_call | solution.py:263
  64.0 0.5 collective-permute-start.9
  64.5 0.6 add_add_fusion
  65.2 0.5 collective-permute-done.9
  65.7 1.2 %maximum_select_fusion = bf16[2,2048,128]{2,1,0:T(8,128)(2,1)} fusion(bf16[2,512,128]{2,1,0:T(8,128)(2,1)S(1)} %collective-permute-done.9, bf16[2,512,128]{2,1,0:T(8,128)(2,1)S(1)} %collective-permute-done.8, bf16[2,512,128]{2,1,0:T(8,128)(2,1)S(1)} %get-tuple-element.7, bf16[2,512,128]{2,1,0:T(8,128)(2,1)S(1)} %get-tuple-element.6, pred[]{:T(512)S(6)} %eq.7), kind=kLoop, calls=%fused_computation | loop fusion | flops 8912896 | bytes 2097153 | tf_op jit(solution)/shard_map/jit(_where)/select_n | solution.py:284
  (20 shorter events, 0.1 us)
Async XLA Ops:
  0.6 2.5 %copy-start.1 = (bf16[2,2048,128]{2,1,0:T(8,128)(2,1)S(1)}, bf16[2,2048,128]{2,1,0:T(8,128)(2,1)}, u32[]{:S(2)}) copy-start(bf16[2,2048,128]{2,1,0:T(8,128)(2,1)} %own_input.3) | copy-start | bytes 3145732
  0.7 3.4 %copy-start = (bf16[2,2048,128]{2,1,0:T(8,128)(2,1)S(1)}, bf16[2,2048,128]{2,1,0:T(8,128)(2,1)}, u32[]{:S(2)}) copy-start(bf16[2,2048,128]{2,1,0:T(8,128)(2,1)} %own_grad.3) | copy-start | bytes 3145732
  2.7 5.2 %collective-permute-start.2 = (bf16[2,1024,128]{2,1,0:T(8,128)(2,1)}, bf16[2,1024,128]{2,1,0:T(8,128)(2,1)S(1)}, u32[]{:S(2)}, u32[]{:S(2)}) collective-permute-start(bf16[2,1024,128]{2,1,0:T(8,128)(2,1)} %constant_dynamic-slice_fusion.5), channel_id=1, source_target_pairs={{0,8},{8,0},{16,24},{24,16},{1,9},{9,1},{17,25},{25,17},{2,10},{10... | collective-permute-start | bytes 1572872 | tf_op jit(solution)/shard_map/ppermute | solution.py:165
  4.0 3.9 %collective-permute-start.4 = (bf16[2,1024,128]{2,1,0:T(8,128)(2,1)}, bf16[2,1024,128]{2,1,0:T(8,128)(2,1)S(1)}, u32[]{:S(2)}, u32[]{:S(2)}) collective-permute-start(bf16[2,1024,128]{2,1,0:T(8,128)(2,1)} %constant_dynamic-slice_fusion.3), channel_id=1, source_target_pairs={{0,8},{8,0},{16,24},{24,16},{1,9},{9,1},{17,25},{25,17},{2,10},{10... | collective-permute-start | bytes 1572872 | tf_op jit(solution)/shard_map/ppermute | solution.py:165
  4.9 16.6 %collective-permute-start.3 = (bf16[2,512,128]{2,1,0:T(8,128)(2,1)}, bf16[2,512,128]{2,1,0:T(8,128)(2,1)S(1)}, u32[]{:S(2)}, u32[]{:S(2)}) collective-permute-start(bf16[2,512,128]{2,1,0:T(8,128)(2,1)} %get-tuple-element.10), channel_id=1, source_target_pairs={{0,16},{8,24},{16,0},{24,8},{1,17},{9,25},{17,1},{25,9},{2,18},{10... | collective-permute-start | bytes 786440 | tf_op jit(solution)/shard_map/ppermute | solution.py:176
  8.7 12.8 %collective-permute-start.5 = (bf16[2,512,128]{2,1,0:T(8,128)(2,1)}, bf16[2,512,128]{2,1,0:T(8,128)(2,1)}, u32[]{:S(2)}, u32[]{:S(2)}) collective-permute-start(bf16[2,512,128]{2,1,0:T(8,128)(2,1)} %get-tuple-element.12), channel_id=1, source_target_pairs={{0,16},{8,24},{16,0},{24,8},{1,17},{9,25},{17,1},{25,9},{2,18},{10... | collective-permute-start | bytes 786440 | tf_op jit(solution)/shard_map/ppermute | solution.py:176
  32.2 4.3 %collective-permute-start.10 = (f32[64,256]{1,0:T(8,128)S(1)}, f32[64,256]{1,0:T(8,128)S(1)}, u32[]{:S(2)}, u32[]{:S(2)}) collective-permute-start(f32[64,256]{1,0:T(8,128)S(1)} %constant_dynamic-slice_fusion.2), channel_id=1, source_target_pairs={{0,16},{8,24},{16,0},{24,8},{1,17},{9,25},{17,1},{25,9},{2,18},{10... | collective-permute-start | bytes 196616 | tf_op jit(solution)/shard_map/ppermute | solution.py:176
  33.4 3.3 %collective-permute-start = (bf16[128,128]{1,0:T(8,128)(2,1)}, bf16[128,128]{1,0:T(8,128)(2,1)S(1)}, u32[]{:S(2)}, u32[]{:S(2)}) collective-permute-start(bf16[128,128]{1,0:T(8,128)(2,1)} %param.5), channel_id=1, source_target_pairs={{0,8},{8,0},{16,24},{24,16},{1,9},{9,1},{17,25},{25,17},{2,10},{10... | collective-permute-start | bytes 98312 | tf_op jit(solution)/shard_map/ppermute | solution.py:165
  33.4 26.3 %collective-permute-start.6 = (bf16[2,512,128]{2,1,0:T(8,128)(2,1)}, bf16[2,512,128]{2,1,0:T(8,128)(2,1)S(1)}, u32[]{:S(2)}, u32[]{:S(2)}) collective-permute-start(bf16[2,512,128]{2,1,0:T(8,128)(2,1)} %get-tuple-element.11), channel_id=1, source_target_pairs={{16,0},{24,8},{17,1},{25,9},{18,2},{26,10},{19,3},{27,11},{20,4},{... | collective-permute-start | bytes 786440 | tf_op jit(solution)/shard_map/ppermute | solution.py:176
  34.7 25.1 %collective-permute-start.7 = (bf16[2,512,128]{2,1,0:T(8,128)(2,1)}, bf16[2,512,128]{2,1,0:T(8,128)(2,1)S(1)}, u32[]{:S(2)}, u32[]{:S(2)}) collective-permute-start(bf16[2,512,128]{2,1,0:T(8,128)(2,1)} %get-tuple-element.13), channel_id=1, source_target_pairs={{16,0},{24,8},{17,1},{25,9},{18,2},{26,10},{19,3},{27,11},{20,4},{... | collective-permute-start | bytes 786440 | tf_op jit(solution)/shard_map/ppermute | solution.py:176
  36.6 3.3 %collective-permute-start.11 = (f32[64,128]{1,0:T(8,128)S(1)}, f32[64,128]{1,0:T(8,128)S(1)}, u32[]{:S(2)}, u32[]{:S(2)}) collective-permute-start(f32[64,128]{1,0:T(8,128)S(1)} %get-tuple-element.15), channel_id=1, source_target_pairs={{0,8},{8,0},{16,24},{24,16},{1,9},{9,1},{17,25},{25,17},{2,10},{10... | collective-permute-start | bytes 98312 | tf_op jit(solution)/shard_map/ppermute | solution.py:165
  37.5 13.8 %collective-permute-start.1 = (bf16[2,128,128]{2,1,0:T(8,128)(2,1)S(1)}, bf16[2,128,128]{2,1,0:T(8,128)(2,1)S(1)}, u32[]{:S(2)}, u32[]{:S(2)}) collective-permute-start(bf16[2,128,128]{2,1,0:T(8,128)(2,1)S(1)} %get-tuple-element.17), channel_id=1, source_target_pairs={{0,16},{8,24},{16,0},{24,8},{1,17},{9,25},{17,1},{25,9},{2,18},{10... | collective-permute-start | bytes 196616 | tf_op jit(solution)/shard_map/ppermute | solution.py:176
  39.9 24.6 %collective-permute-start.12 = (f32[128,128]{1,0:T(8,128)S(1)}, f32[128,128]{1,0:T(8,128)S(1)}, u32[]{:S(2)}, u32[]{:S(2)}) collective-permute-start(f32[128,128]{1,0:T(8,128)S(1)} %maximum_select_fusion.1), channel_id=1, source_target_pairs={{0,1},{1,0},{2,3},{3,2},{4,5},{5,4},{6,7},{7,6},{8,9},{9,8},{10,11... | collective-permute-start | bytes 196616 | tf_op jit(solution)/shard_map/ppermute | solution.py:300
  41.5 23.0 %collective-permute-start.13 = (f32[128,128]{1,0:T(8,128)S(1)}, f32[128,128]{1,0:T(8,128)S(1)}, u32[]{:S(2)}, u32[]{:S(2)}) collective-permute-start(f32[128,128]{1,0:T(8,128)S(1)} %maximum_select_fusion.1), channel_id=1, source_target_pairs={{0,2},{1,3},{2,0},{3,1},{4,6},{5,7},{6,4},{7,5},{8,10},{9,11},{10,... | collective-permute-start | bytes 196616 | tf_op jit(solution)/shard_map/ppermute | solution.py:300
  51.3 13.3 %collective-permute-start.14 = (f32[128,128]{1,0:T(8,128)S(1)}, f32[128,128]{1,0:T(8,128)S(1)}, u32[]{:S(2)}, u32[]{:S(2)}) collective-permute-start(f32[128,128]{1,0:T(8,128)S(1)} %maximum_select_fusion.1), channel_id=1, source_target_pairs={{0,3},{1,2},{2,1},{3,0},{4,7},{5,6},{6,5},{7,4},{8,11},{9,10},{10,... | collective-permute-start | bytes 196616 | tf_op jit(solution)/shard_map/ppermute | solution.py:300
  59.8 5.4 %collective-permute-start.8 = (bf16[2,512,128]{2,1,0:T(8,128)(2,1)S(1)}, bf16[2,512,128]{2,1,0:T(8,128)(2,1)S(1)}, u32[]{:S(2)}, u32[]{:S(2)}) collective-permute-start(bf16[2,512,128]{2,1,0:T(8,128)(2,1)S(1)} %get-tuple-element.8), channel_id=1, source_target_pairs={{0,8},{8,0},{16,24},{24,16},{1,9},{9,1},{17,25},{25,17},{2,10},{10... | collective-permute-start | bytes 786440 | tf_op jit(solution)/shard_map/ppermute | solution.py:165
  64.0 1.7 %collective-permute-start.9 = (bf16[2,512,128]{2,1,0:T(8,128)(2,1)S(1)}, bf16[2,512,128]{2,1,0:T(8,128)(2,1)S(1)}, u32[]{:S(2)}, u32[]{:S(2)}) collective-permute-start(bf16[2,512,128]{2,1,0:T(8,128)(2,1)S(1)} %get-tuple-element.9), channel_id=1, source_target_pairs={{0,8},{8,0},{16,24},{24,16},{1,9},{9,1},{17,25},{25,17},{2,10},{10... | collective-permute-start | bytes 786440 | tf_op jit(solution)/shard_map/ppermute | solution.py:165

commit v2 on v1

--- a/solution.py
+++ b/solution.py
@@ -10,6 +10,7 @@
 GROUP_SIZE = 16
 CORES = 2
 VMEM_BYTES = 40 << 20
+UNROLL = 16
 
 
 def pick(condition, first, second):
@@ -62,7 +63,7 @@
         theirs[:, pl.ds(start, GROUP_SIZE), :] = pick(first_core, late, early).reshape(shape)
         return carry
 
-    lax.fori_loop(0, channels // GROUP_SIZE, one_group, 0, unroll=4)
+    lax.fori_loop(0, channels // GROUP_SIZE, one_group, 0, unroll=UNROLL)
 
 
 def reversal(positions):
@@ -71,53 +72,77 @@
     return (row + column == positions - 1).astype(jnp.float32).astype(jnp.bfloat16)
 
 
-def lag_sums(values, grads, flip, keep):
-    positions, width = flip.shape[0], grads.shape[1]
-    flipped = jnp.dot(values, flip, preferred_element_type=jnp.float32).astype(jnp.bfloat16)
+def flip_rows(out, core, values, flip):
+    sequences, channels, positions = values.shape
+    flat = values.reshape(sequences * channels, positions)
+    flat = jnp.dot(flat, flip, preferred_element_type=jnp.float32).astype(jnp.bfloat16)
+    out[core] = flat.reshape(sequences, channels, positions)
+
+
+def lag_sums(flipped, grads, keep, lead):
     products = lax.dot_general(
         flipped, grads, (((0,), (0,)), ((), ())), preferred_element_type=jnp.float32
     )
+    positions = products.shape[0]
     if keep is not None:
         products = jnp.where(keep, products, 0.0)
-    products = pltpu.roll(products, width - positions + 1, 1, stride=1, stride_axis=0)
+    if lead:
+        products = jnp.concatenate([jnp.zeros((positions, lead), jnp.float32), products], axis=1)
+    products = pltpu.roll(products, products.shape[1] - positions + 1, 1, stride=1, stride_axis=0)
     return jnp.sum(products, axis=0, keepdims=True)
 
 
-def own_lags_kernel(place, own_input, peer_input, own_grad, peer_grad, out):
+def own_lags_kernel(place, own_input, peer_input, own_grad, peer_grad, out, flipped):
     first_core = place[0] == 0
     sequences, channels, positions = own_input.shape
     rows, width = sequences * GROUP_SIZE, CORES * positions
     flip = reversal(positions)
+    own, peer = own_input[...], peer_input[...]
+    flip_rows(flipped, 0, pick(first_core, own, peer), flip)
+    flip_rows(flipped, 1, pick(first_core, peer, own), flip)
     row = lax.broadcasted_iota(jnp.int32, (positions, width), 0)
     column = lax.broadcasted_iota(jnp.int32, (positions, width), 1)
     keep = column + row >= positions - 1
 
     def one_group(index, carry):
-        own, peer = group_rows(own_input, index), group_rows(peer_input, index)
-        values = jnp.concatenate([pick(first_core, own, peer), pick(first_core, peer, own)], axis=0)
+        values = jnp.concatenate([group_rows(flipped.at[core], index) for core in range(CORES)], axis=0)
         own, peer = group_rows(own_grad, index), group_rows(peer_grad, index)
         early, late = pick(first_core, own, peer), pick(first_core, peer, own)
+        zeros = jnp.zeros((rows, positions), jnp.bfloat16)
         grads = jnp.concatenate(
-            [
-                jnp.concatenate([early, late], axis=1),
-                jnp.concatenate([late, jnp.zeros((rows, positions), jnp.bfloat16)], axis=1),
-            ],
-            axis=0,
-        )
-        out[pl.ds(index, 1), :] = lag_sums(values, grads, flip, keep)
+            [jnp.concatenate([early, late], axis=1), jnp.concatenate([late, zeros], axis=1)], axis=0
+        )
+        out[pl.ds(index, 1), :] = lag_sums(values, grads, keep, 0)
         return carry
 
-    lax.fori_loop(0, channels // GROUP_SIZE, one_group, 0, unroll=4)
+    lax.fori_loop(0, channels // GROUP_SIZE, one_group, 0, unroll=UNROLL)
 
 
 def round_lags_kernel(
-    chips, distance, place, own_input, peer_input, own_grad, peer_grad, own_got, peer_got, running, out
+    chips,
+    distance,
+    place,
+    own_input,
+    peer_input,
+    own_grad,
+    peer_grad,
+    own_got,
+    peer_got,
+    running,
+    out,
+    flipped,
 ):
     first_core = place[0] == 0
     lower = place[1] + distance < chips
     sequences, channels, positions = own_input.shape
     rows = sequences * GROUP_SIZE
     flip = reversal(positions)
+    own, peer = (
+        pick(lower, own_input[...], own_got[...]),
+        pick(lower, peer_input[...], peer_got[...]),
+    )
+    flip_rows(flipped, 0, pick(first_core, own, peer), flip)
+    flip_rows(flipped, 1, pick(first_core, peer, own), flip)
     out[...] = running[...]
     if 2 * distance == chips:
         first_lag = (2 * distance - 2) * positions
@@ -128,25 +153,23 @@
 
     def one_group(index, carry):
         got = group_rows(own_got, index), group_rows(peer_got, index)
-        inputs = group_rows(own_input, index), group_rows(peer_input, index)
         grads = group_rows(own_grad, index), group_rows(peer_grad, index)
-        left = [pick(lower, a, b) for a, b in zip(inputs, got)]
         right = [pick(lower, b, a) for a, b in zip(grads, got)]
-        values = jnp.concatenate([pick(first_core, *left), pick(first_core, *left[::-1])], axis=0)
+        values = jnp.concatenate([group_rows(flipped.at[core], index) for core in range(CORES)], axis=0)
         early, late = pick(first_core, *right), pick(first_core, *right[::-1])
         zeros = jnp.zeros((rows, positions), jnp.bfloat16)
         pairs = jnp.concatenate(
             [
-                jnp.concatenate([zeros, zeros, early, late], axis=1),
-                jnp.concatenate([zeros, early, late, zeros], axis=1),
+                jnp.concatenate([zeros, early, late], axis=1),
+                jnp.concatenate([early, late, zeros], axis=1),
             ],
             axis=0,
         )
         where = (pl.ds(index, 1), pl.ds(first_lag, 2 * CORES * positions))
-        out[where] = out[where] + lag_sums(values, pairs, flip, None)
+        out[where] = out[where] + lag_sums(values, pairs, None, positions)
         return carry
 
-    lax.fori_loop(0, channels // GROUP_SIZE, one_group, 0, unroll=4)
+    lax.fori_loop(0, channels // GROUP_SIZE, one_group, 0, unroll=UNROLL)
 
 
 def per_device(inputs, output_grad, filters):
@@ -212,6 +235,15 @@
 
     part_spec = pl.BlockSpec(block, lambda i, place: (0, i, 0))
     params = pltpu.CompilerParams(vmem_limit_bytes=VMEM_BYTES)
+    flip_scratch = [pltpu.VMEM((CORES,) + block, jnp.bfloat16)]
+    rows = sequences * GROUP_SIZE
+
+    def cost(group_count, depth, width, arrays):
+        return pl.CostEstimate(
+            flops=2 * group_count * depth * positions * width,
+            bytes_accessed=arrays * group_count * rows * positions * 2,
+            transcendentals=0,
+        )
 
     lags = pl.pallas_call(
         own_lags_kernel,
@@ -220,8 +252,10 @@
             grid=(2 * steps,),
             in_specs=[whole_spec(), half_spec(), whole_spec(), half_spec()],
             out_specs=pl.BlockSpec((step, CORES * positions), lambda i, place: (i, 0)),
+            scratch_shapes=flip_scratch,
         ),
         out_shape=jax.ShapeDtypeStruct((groups, CORES * positions), jnp.float32),
+        cost_estimate=cost(groups, CORES * rows, CORES * positions, 4),
         compiler_params=params,
     )(place, inputs, input_peer, output_grad, grad_peer)
     lags = jnp.pad(lags, ((0, 0), (0, length - CORES * positions)))
@@ -241,9 +275,11 @@
                     part_spec, part_spec, lag_spec,
                 ],
                 out_specs=lag_spec,
+                scratch_shapes=flip_scratch,
             ),
             out_shape=jax.ShapeDtypeStruct((groups, length), jnp.float32),
             input_output_aliases={7: 0},
+            cost_estimate=cost(part_groups, CORES * rows, 3 * positions, 6),
             compiler_params=params,
         )(place, inputs, input_peer, output_grad, grad_peer, *first[k], lags)
 
@@ -272,6 +308,7 @@
                 scratch_shapes=[pltpu.VMEM((step, length), jnp.float32)],
             ),
             out_shape=[jax.ShapeDtypeStruct((sequences, part, positions), jnp.bfloat16)] * 2,
+            cost_estimate=cost(part_groups, CORES * rows, length, 4 + len(arrays)),
             compiler_params=params,
         )(place, *([taps] * shard_count), output_grad, grad_peer, *arrays)
 

time: 67.2 us -> 46.4 us (0.69)
  Pallas kernels: 31.4 us -> 16.4 us
  starting transfers between devices: 19.1 us -> 14.4 us
  other arithmetic: 4.45 us -> 3.71 us
    pallas_call x1, Pallas kernels: 11.8 us -> 4.9 us  [per_device(): pl.pallas_call(own_lags_kernel, grid_spec=pltpu.PrefetchScalarGridSpec(nu...]
    pallas_call x1, Pallas kernels: 10.7 us -> 4.33 us  [per_device(): pl.pallas_call(functools.partial(round_lags_kernel, chips, k), grid_spec=...]
    ppermute x3, starting transfers between devices: 7.82 us -> 4.5 us  [per_device(): terms.append(lax.ppermute(own, 'dp', [(i, i ^ k) for i in range(copies)]))]
    pallas_call x2, Pallas kernels: 8.98 us -> 7.18 us  [input_part(): pl.pallas_call(functools.partial(input_grad_kernel, chips), grid_spec=plt...]
    ppermute x6, starting transfers between devices: 10.1 us -> 8.58 us  [from_chip(): return lax.ppermute(value, 'seq', pairs)]
    another operation x2, other arithmetic: 0.79 us -> 0.02 us  [per_device(): taps = jnp.stack([taps] + [from_chip(taps, k, True) for k in rounds])]
  transfers between devices with their start and end apart: 15 -> 15, of which waited for: 3 -> 4; matrix products, arithmetic and copies ran while one was open for 6% -> 7% of each run, Pallas kernels for 31% -> 36%
where the time goes in v2:
time: 46.4 us; the launch traced here: 46.2 us
  Pallas kernels  16.4 us (35%)
  starting transfers between devices  14.4 us (31%)
  waiting for transfers between devices  7.91 us (17%)
  other arithmetic  3.71 us (8%)
  local copies, waits for them, and re-layouts  2.92 us (6%)
  between operations  0.88 us (2%)
    ppermute x6, starting transfers between devices, from_chip(): return lax.ppermute(value, 'seq', pairs)  8.58 us
    ppermute x6, waiting for transfers between devices, from_chip(): return lax.ppermute(value, 'seq', pairs)  7.39 us
    pallas_call x2, Pallas kernels, input_part(): pl.pallas_call(functools.partial(input_grad_kernel, chips), grid_spec=plt...  7.18 us
    pallas_call x1, Pallas kernels, per_device(): pl.pallas_call(own_lags_kernel, grid_spec=pltpu.PrefetchScalarGridSpec(nu...  4.9 us
    ppermute x3, starting transfers between devices, per_device(): terms.append(lax.ppermute(own, 'dp', [(i, i ^ k) for i in range(copies)]))  4.5 us
    pallas_call x1, Pallas kernels, per_device(): pl.pallas_call(functools.partial(round_lags_kernel, chips, k), grid_spec=...  4.33 us
    dynamic_slice x2, local copies, waits for them, and re-layouts, half_of(): return lax.dynamic_slice_in_dim(value, which * half, half, 1)  2.86 us
    ppermute x6, starting transfers between devices, swap_cores(): return lax.ppermute(value, 'seq', [(i, i ^ 1) for i in range(shard_count)])  1.28 us
  transfers between devices with their start and end apart: 15, of which 4 were waited for; matrix products, arithmetic and copies ran while one was open for 7% of the time, Pallas kernels for 36%

profile of v2, /device:TPU:0, one launch (start us, length us, event | category | flops | bytes accessed | tf_op | source)
XLA Modules:
  0.0 46.2 jit_solution(6076540629312631055)
XLA Ops:
  0.7 2.0 %constant_dynamic-slice_fusion.5 = bf16[2,1024,128]{2,1,0:T(8,128)(2,1)} fusion(bf16[2,2048,128]{2,1,0:T(8,128)(2,1)} %own_grad.3, s32[]{:T(128)S(6)} %select_n.66), kind=kLoop, calls=%fused_computation.13 | loop fusion | bytes 1048580 | tf_op jit(solution)/shard_map/dynamic_slice | solution.py:191
  2.7 0.5 collective-permute-start.2
  3.1 0.8 %constant_dynamic-slice_fusion.3 = bf16[2,1024,128]{2,1,0:T(8,128)(2,1)} fusion(bf16[2,2048,128]{2,1,0:T(8,128)(2,1)S(1)} %copy-done.1, s32[]{:T(128)S(6)} %select_n.66), kind=kLoop, calls=%fused_computation.11 | loop fusion | bytes 1048580 | tf_op jit(solution)/shard_map/dynamic_slice | solution.py:191
  4.0 0.1 collective-permute-start.4
  4.0 0.8 %dynamic-slice_select_fusion = (bf16[2,512,128]{2,1,0:T(8,128)(2,1)}, bf16[2,512,128]{2,1,0:T(8,128)(2,1)}) fusion(bf16[2,2048,128]{2,1,0:T(8,128)(2,1)S(1)} %copy-done.1, s32[]{:T(128)S(6)} %add.56, bf16[2,2048,128]{2,1,0:T(8,128)(2,1)S(1)} %copy-done, s32[]{:T(128)S(6)} %select_n.68, pred[]{:T(512)S(6)} %ge.3), kind=kLoop, calls=%fused_computation.2 | loop fusion | flops 131072 | bytes 1310729 | tf_op jit(solution)/shard_map/jit(_where)/select_n | solution.py:210
  4.9 3.0 %collective-permute-start.3 = (bf16[2,512,128]{2,1,0:T(8,128)(2,1)}, bf16[2,512,128]{2,1,0:T(8,128)(2,1)S(1)}, u32[]{:S(2)}, u32[]{:S(2)}) collective-permute-start(bf16[2,512,128]{2,1,0:T(8,128)(2,1)} %get-tuple-element.10), channel_id=1, source_target_pairs={{0,16},{8,24},{16,0},{24,8},{1,17},{9,25},{17,1},{25,9},{2,18},{10... | collective-permute-start | bytes 786440 | tf_op jit(solution)/shard_map/ppermute | solution.py:199
  7.9 0.0 collective-permute-done.2.refs_5_.peer_grad
  7.9 0.8 %slice_select_fusion = (bf16[2,512,128]{2,1,0:T(8,128)(2,1)}, bf16[2,512,128]{2,1,0:T(8,128)(2,1)}) fusion(bf16[2,1024,128]{2,1,0:T(8,128)(2,1)S(1)} %collective-permute-done.4.peer_input, bf16[2,1024,128]{2,1,0:T(8,128)(2,1)S(1)} %collective-permute-done.2.refs_5_.peer_grad, pred[]{:T(512)S(6)} %ge.3), kind=kLoop, calls=%fused_computation.1 | loop fusion | flops 131072 | bytes 1310721 | tf_op jit(solution)/shard_map/jit(_where)/select_n | solution.py:211
  8.7 0.9 %collective-permute-start.5 = (bf16[2,512,128]{2,1,0:T(8,128)(2,1)}, bf16[2,512,128]{2,1,0:T(8,128)(2,1)}, u32[]{:S(2)}, u32[]{:S(2)}) collective-permute-start(bf16[2,512,128]{2,1,0:T(8,128)(2,1)} %get-tuple-element.12), channel_id=1, source_target_pairs={{0,16},{8,24},{16,0},{24,8},{1,17},{9,25},{17,1},{25,9},{2,18},{10... | collective-permute-start | bytes 786440 | tf_op jit(solution)/shard_map/ppermute | solution.py:199
  9.6 0.1 collective-permute-start
  9.7 1.3 %collective-permute-start.6 = (bf16[2,512,128]{2,1,0:T(8,128)(2,1)}, bf16[2,512,128]{2,1,0:T(8,128)(2,1)}, u32[]{:S(2)}, u32[]{:S(2)}) collective-permute-start(bf16[2,512,128]{2,1,0:T(8,128)(2,1)} %get-tuple-element.11), channel_id=1, source_target_pairs={{16,0},{24,8},{17,1},{25,9},{18,2},{26,10},{19,3},{27,11},{20,4},{... | collective-permute-start | bytes 786440 | tf_op jit(solution)/shard_map/ppermute | solution.py:199
  11.0 0.1 pad_add_fusion.place
  11.1 4.9 %shard_map.52 = f32[64,256]{1,0:T(8,128)S(1)} custom-call(s32[2]{0:T(128)S(1)} %pad_add_fusion.place, bf16[2,2048,128]{2,1,0:T(8,128)(2,1)S(1)} %copy-done.1, bf16[2,1024,128]{2,1,0:T(8,128)(2,1)S(1)} %collective-permute-done.4.peer_input, bf16[2,2048,128]{2,1,0:T(8,128)(2,1)S(1)} %copy-done, bf16[2,1024,128]{2,1,0:T(8,128)(2,1)S(1)} %collective-permute-done.2.refs_5_.peer_grad), custom_call_target="tpu_custom_call" | custom-call | flops 268435456 | bytes 2097152 | tf_op jit(solution)/shard_map/pallas_call | solution.py:248
  16.0 0.0 collective-permute-done.3.refs_6_.own_got
  16.1 4.9 %collective-permute-done.5.refs_7_.peer_got = bf16[2,512,128]{2,1,0:T(8,128)(2,1)} collective-permute-done((bf16[2,512,128]{2,1,0:T(8,128)(2,1)}, bf16[2,512,128]{2,1,0:T(8,128)(2,1)}, u32[]{:S(2)}, u32[]{:S(2)}) %collective-permute-start.5) | collective-permute-done | bytes 262176 | tf_op jit(solution)/shard_map/ppermute | solution.py:199
  20.9 4.3 %shard_map.53 = f32[64,512]{1,0:T(8,128)S(1)} custom-call(s32[2]{0:T(128)S(1)} %pad_add_fusion.place, bf16[2,2048,128]{2,1,0:T(8,128)(2,1)S(1)} %copy-done.1, bf16[2,1024,128]{2,1,0:T(8,128)(2,1)S(1)} %collective-permute-done.4.peer_input, bf16[2,2048,128]{2,1,0:T(8,128)(2,1)S(1)} %copy-done, ...), custom_call_target="tpu_custom_call", output_to_operand_aliasing={{}: (7, {})} | custom-call | flops 201326592 | bytes 1572864 | tf_op jit(solution)/shard_map/pallas_call | solution.py:268
  25.3 1.2 %collective-permute-start.10 = (f32[64,256]{1,0:T(8,128)S(1)}, f32[64,256]{1,0:T(8,128)S(1)}, u32[]{:S(2)}, u32[]{:S(2)}) collective-permute-start(f32[64,256]{1,0:T(8,128)S(1)} %constant_dynamic-slice_fusion.2), channel_id=1, source_target_pairs={{0,16},{8,24},{16,0},{24,8},{1,17},{9,25},{17,1},{25,9},{2,18},{10... | collective-permute-start | bytes 196616 | tf_op jit(solution)/shard_map/ppermute | solution.py:199
  26.5 1.0 %collective-permute-start.1 = (bf16[2,128,128]{2,1,0:T(8,128)(2,1)S(1)}, bf16[2,128,128]{2,1,0:T(8,128)(2,1)S(1)}, u32[]{:S(2)}, u32[]{:S(2)}) collective-permute-start(bf16[2,128,128]{2,1,0:T(8,128)(2,1)S(1)} %get-tuple-element.17), channel_id=1, source_target_pairs={{0,16},{8,24},{16,0},{24,8},{1,17},{9,25},{17,1},{25,9},{2,18},{10... | collective-permute-start | bytes 196616 | tf_op jit(solution)/shard_map/ppermute | solution.py:199
  27.5 1.3 %collective-permute-start.7 = (bf16[2,512,128]{2,1,0:T(8,128)(2,1)S(1)}, bf16[2,512,128]{2,1,0:T(8,128)(2,1)S(1)}, u32[]{:S(2)}, u32[]{:S(2)}) collective-permute-start(bf16[2,512,128]{2,1,0:T(8,128)(2,1)S(1)} %copy-done.2), channel_id=1, source_target_pairs={{16,0},{24,8},{17,1},{25,9},{18,2},{26,10},{19,3},{27,11},{20,4},{... | collective-permute-start | bytes 786440 | tf_op jit(solution)/shard_map/ppermute | solution.py:199
  28.7 0.9 %collective-permute-done.10 = f32[64,256]{1,0:T(8,128)S(1)} collective-permute-done((f32[64,256]{1,0:T(8,128)S(1)}, f32[64,256]{1,0:T(8,128)S(1)}, u32[]{:S(2)}, u32[]{:S(2)}) %collective-permute-start.10) | collective-permute-done | bytes 65568 | tf_op jit(solution)/shard_map/ppermute | solution.py:199
  29.6 0.1 collective-permute-start.11
  29.7 1.7 %collective-permute-done.1 = bf16[2,128,128]{2,1,0:T(8,128)(2,1)S(1)} collective-permute-done((bf16[2,128,128]{2,1,0:T(8,128)(2,1)S(1)}, bf16[2,128,128]{2,1,0:T(8,128)(2,1)S(1)}, u32[]{:S(2)}, u32[]{:S(2)}) %collective-permute-start.1) | collective-permute-done | bytes 65568 | tf_op jit(solution)/shard_map/ppermute | solution.py:199
  31.4 0.0 collective-permute-done.11
  31.4 1.9 %collective-permute-start.12 = (f32[128,128]{1,0:T(8,128)S(1)}, f32[128,128]{1,0:T(8,128)S(1)}, u32[]{:S(2)}, u32[]{:S(2)}) collective-permute-start(f32[128,128]{1,0:T(8,128)S(1)} %maximum_select_fusion.1), channel_id=1, source_target_pairs={{0,1},{1,0},{2,3},{3,2},{4,5},{5,4},{6,7},{7,6},{8,9},{9,8},{10,11... | collective-permute-start | bytes 196616 | tf_op jit(solution)/shard_map/ppermute | solution.py:337
  33.3 2.6 %collective-permute-start.13 = (f32[128,128]{1,0:T(8,128)S(1)}, f32[128,128]{1,0:T(8,128)S(1)}, u32[]{:S(2)}, u32[]{:S(2)}) collective-permute-start(f32[128,128]{1,0:T(8,128)S(1)} %maximum_select_fusion.1), channel_id=1, source_target_pairs={{0,2},{1,3},{2,0},{3,1},{4,6},{5,7},{6,4},{7,5},{8,10},{9,11},{10,... | collective-permute-start | bytes 196616 | tf_op jit(solution)/shard_map/ppermute | solution.py:337
  35.9 3.6 %shard_map.50 = (bf16[2,512,128]{2,1,0:T(8,128)(2,1)S(1)}, bf16[2,512,128]{2,1,0:T(8,128)(2,1)S(1)}) custom-call(s32[2]{0:T(128)S(1)} %pad_add_fusion.place, bf16[2,2,128,128]{3,2,1,0:T(8,128)(2,1)S(1)} %pad_maximum_fusion.refs_0_.refs_1_.refs_2_.refs_3_, bf16[2,2,128,128]{3,2,1,0:T(8,128)(2,1)S(1)} %pad_maximum_fusion.refs_0_.refs_1_.refs_2_.refs_3_, ...), custom_call_target="tpu_custom_call" | custom-call | flops 268435456 | bytes 1572864 | tf_op jit(solution)/shard_map/pallas_call | solution.py:299
  39.5 0.1 collective-permute-start.8
  39.6 3.6 %shard_map.51 = (bf16[2,512,128]{2,1,0:T(8,128)(2,1)S(1)}, bf16[2,512,128]{2,1,0:T(8,128)(2,1)S(1)}) custom-call(s32[2]{0:T(128)S(1)} %pad_add_fusion.place, bf16[2,2,128,128]{3,2,1,0:T(8,128)(2,1)S(1)} %pad_maximum_fusion.refs_0_.refs_1_.refs_2_.refs_3_, bf16[2,2,128,128]{3,2,1,0:T(8,128)(2,1)S(1)} %pad_maximum_fusion.refs_0_.refs_1_.refs_2_.refs_3_, ...), custom_call_target="tpu_custom_call" | custom-call | flops 268435456 | bytes 1572864 | tf_op jit(solution)/shard_map/pallas_call | solution.py:299
  43.2 0.5 %collective-permute-start.9 = (bf16[2,512,128]{2,1,0:T(8,128)(2,1)S(1)}, bf16[2,512,128]{2,1,0:T(8,128)(2,1)S(1)}, u32[]{:S(2)}, u32[]{:S(2)}) collective-permute-start(bf16[2,512,128]{2,1,0:T(8,128)(2,1)S(1)} %get-tuple-element.9), channel_id=1, source_target_pairs={{0,8},{8,0},{16,24},{24,16},{1,9},{9,1},{17,25},{25,17},{2,10},{10... | collective-permute-start | bytes 786440 | tf_op jit(solution)/shard_map/ppermute | solution.py:188
  43.8 0.6 %add_add_fusion = f32[128,128]{1,0:T(8,128)} fusion(f32[128,128]{1,0:T(8,128)S(1)} %collective-permute-done.13, f32[128,128]{1,0:T(8,128)S(1)} %collective-permute-done.14, f32[128,128]{1,0:T(8,128)S(1)} %maximum_select_fusion.1, f32[128,128]{1,0:T(8,128)S(1)} %collective-permute-done.12), kind=kLoop, calls=%fused_computation.6 | loop fusion | flops 49152 | bytes 327680 | tf_op jit(solution)/shard_map/add | solution.py:339
  44.4 0.5 %collective-permute-done.9 = bf16[2,512,128]{2,1,0:T(8,128)(2,1)S(1)} collective-permute-done((bf16[2,512,128]{2,1,0:T(8,128)(2,1)S(1)}, bf16[2,512,128]{2,1,0:T(8,128)(2,1)S(1)}, u32[]{:S(2)}, u32[]{:S(2)}) %collective-permute-start.9) | collective-permute-done | bytes 262176 | tf_op jit(solution)/shard_map/ppermute | solution.py:188
  44.9 1.3 %maximum_select_fusion = bf16[2,2048,128]{2,1,0:T(8,128)(2,1)} fusion(bf16[2,512,128]{2,1,0:T(8,128)(2,1)S(1)} %collective-permute-done.9, bf16[2,512,128]{2,1,0:T(8,128)(2,1)S(1)} %collective-permute-done.8, bf16[2,512,128]{2,1,0:T(8,128)(2,1)S(1)} %get-tuple-element.7, bf16[2,512,128]{2,1,0:T(8,128)(2,1)S(1)} %get-tuple-element.6, pred[]{:T(512)S(6)} %eq.7), kind=kLoop, calls=%fused_computation | loop fusion | flops 8912896 | bytes 2097153 | tf_op jit(solution)/shard_map/jit(_where)/select_n | solution.py:321
  (24 shorter events, 0.1 us)
Async XLA Ops:
  0.6 2.5 %copy-start.1 = (bf16[2,2048,128]{2,1,0:T(8,128)(2,1)S(1)}, bf16[2,2048,128]{2,1,0:T(8,128)(2,1)}, u32[]{:S(2)}) copy-start(bf16[2,2048,128]{2,1,0:T(8,128)(2,1)} %own_input.3) | copy-start | bytes 3145732
  0.7 3.4 %copy-start = (bf16[2,2048,128]{2,1,0:T(8,128)(2,1)S(1)}, bf16[2,2048,128]{2,1,0:T(8,128)(2,1)}, u32[]{:S(2)}) copy-start(bf16[2,2048,128]{2,1,0:T(8,128)(2,1)} %own_grad.3) | copy-start | bytes 3145732
  2.7 5.2 %collective-permute-start.2 = (bf16[2,1024,128]{2,1,0:T(8,128)(2,1)}, bf16[2,1024,128]{2,1,0:T(8,128)(2,1)S(1)}, u32[]{:S(2)}, u32[]{:S(2)}) collective-permute-start(bf16[2,1024,128]{2,1,0:T(8,128)(2,1)} %constant_dynamic-slice_fusion.5), channel_id=1, source_target_pairs={{0,8},{8,0},{16,24},{24,16},{1,9},{9,1},{17,25},{25,17},{2,10},{10... | collective-permute-start | bytes 1572872 | tf_op jit(solution)/shard_map/ppermute | solution.py:188
  4.0 3.9 %collective-permute-start.4 = (bf16[2,1024,128]{2,1,0:T(8,128)(2,1)}, bf16[2,1024,128]{2,1,0:T(8,128)(2,1)S(1)}, u32[]{:S(2)}, u32[]{:S(2)}) collective-permute-start(bf16[2,1024,128]{2,1,0:T(8,128)(2,1)} %constant_dynamic-slice_fusion.3), channel_id=1, source_target_pairs={{0,8},{8,0},{16,24},{24,16},{1,9},{9,1},{17,25},{25,17},{2,10},{10... | collective-permute-start | bytes 1572872 | tf_op jit(solution)/shard_map/ppermute | solution.py:188
  4.0 5.6 %copy-start.3 = (bf16[128,128]{1,0:T(8,128)(2,1)S(1)}, bf16[128,128]{1,0:T(8,128)(2,1)}, u32[]{:S(2)}) copy-start(bf16[128,128]{1,0:T(8,128)(2,1)} %param.5) | copy-start | bytes 98308
  4.9 11.2 %collective-permute-start.3 = (bf16[2,512,128]{2,1,0:T(8,128)(2,1)}, bf16[2,512,128]{2,1,0:T(8,128)(2,1)S(1)}, u32[]{:S(2)}, u32[]{:S(2)}) collective-permute-start(bf16[2,512,128]{2,1,0:T(8,128)(2,1)} %get-tuple-element.10), channel_id=1, source_target_pairs={{0,16},{8,24},{16,0},{24,8},{1,17},{9,25},{17,1},{25,9},{2,18},{10... | collective-permute-start | bytes 786440 | tf_op jit(solution)/shard_map/ppermute | solution.py:199
  8.7 12.2 %collective-permute-start.5 = (bf16[2,512,128]{2,1,0:T(8,128)(2,1)}, bf16[2,512,128]{2,1,0:T(8,128)(2,1)}, u32[]{:S(2)}, u32[]{:S(2)}) collective-permute-start(bf16[2,512,128]{2,1,0:T(8,128)(2,1)} %get-tuple-element.12), channel_id=1, source_target_pairs={{0,16},{8,24},{16,0},{24,8},{1,17},{9,25},{17,1},{25,9},{2,18},{10... | collective-permute-start | bytes 786440 | tf_op jit(solution)/shard_map/ppermute | solution.py:199
  9.6 16.8 %collective-permute-start = (bf16[128,128]{1,0:T(8,128)(2,1)S(1)}, bf16[128,128]{1,0:T(8,128)(2,1)S(1)}, u32[]{:S(2)}, u32[]{:S(2)}) collective-permute-start(bf16[128,128]{1,0:T(8,128)(2,1)S(1)} %copy-done.3), channel_id=1, source_target_pairs={{0,8},{8,0},{16,24},{24,16},{1,9},{9,1},{17,25},{25,17},{2,10},{10... | collective-permute-start | bytes 98312 | tf_op jit(solution)/shard_map/ppermute | solution.py:188
  9.7 29.8 %collective-permute-start.6 = (bf16[2,512,128]{2,1,0:T(8,128)(2,1)}, bf16[2,512,128]{2,1,0:T(8,128)(2,1)}, u32[]{:S(2)}, u32[]{:S(2)}) collective-permute-start(bf16[2,512,128]{2,1,0:T(8,128)(2,1)} %get-tuple-element.11), channel_id=1, source_target_pairs={{16,0},{24,8},{17,1},{25,9},{18,2},{26,10},{19,3},{27,11},{20,4},{... | collective-permute-start | bytes 786440 | tf_op jit(solution)/shard_map/ppermute | solution.py:199
  16.0 11.4 %copy-start.2 = (bf16[2,512,128]{2,1,0:T(8,128)(2,1)S(1)}, bf16[2,512,128]{2,1,0:T(8,128)(2,1)}, u32[]{:S(2)}) copy-start(bf16[2,512,128]{2,1,0:T(8,128)(2,1)} %get-tuple-element.13) | copy-start | bytes 786436
  25.3 4.3 %collective-permute-start.10 = (f32[64,256]{1,0:T(8,128)S(1)}, f32[64,256]{1,0:T(8,128)S(1)}, u32[]{:S(2)}, u32[]{:S(2)}) collective-permute-start(f32[64,256]{1,0:T(8,128)S(1)} %constant_dynamic-slice_fusion.2), channel_id=1, source_target_pairs={{0,16},{8,24},{16,0},{24,8},{1,17},{9,25},{17,1},{25,9},{2,18},{10... | collective-permute-start | bytes 196616 | tf_op jit(solution)/shard_map/ppermute | solution.py:199
  26.5 4.9 %collective-permute-start.1 = (bf16[2,128,128]{2,1,0:T(8,128)(2,1)S(1)}, bf16[2,128,128]{2,1,0:T(8,128)(2,1)S(1)}, u32[]{:S(2)}, u32[]{:S(2)}) collective-permute-start(bf16[2,128,128]{2,1,0:T(8,128)(2,1)S(1)} %get-tuple-element.17), channel_id=1, source_target_pairs={{0,16},{8,24},{16,0},{24,8},{1,17},{9,25},{17,1},{25,9},{2,18},{10... | collective-permute-start | bytes 196616 | tf_op jit(solution)/shard_map/ppermute | solution.py:199
  27.5 12.2 %collective-permute-start.7 = (bf16[2,512,128]{2,1,0:T(8,128)(2,1)S(1)}, bf16[2,512,128]{2,1,0:T(8,128)(2,1)S(1)}, u32[]{:S(2)}, u32[]{:S(2)}) collective-permute-start(bf16[2,512,128]{2,1,0:T(8,128)(2,1)S(1)} %copy-done.2), channel_id=1, source_target_pairs={{16,0},{24,8},{17,1},{25,9},{18,2},{26,10},{19,3},{27,11},{20,4},{... | collective-permute-start | bytes 786440 | tf_op jit(solution)/shard_map/ppermute | solution.py:199
  29.6 1.8 %collective-permute-start.11 = (f32[64,128]{1,0:T(8,128)S(1)}, f32[64,128]{1,0:T(8,128)S(1)}, u32[]{:S(2)}, u32[]{:S(2)}) collective-permute-start(f32[64,128]{1,0:T(8,128)S(1)} %get-tuple-element.15), channel_id=1, source_target_pairs={{0,8},{8,0},{16,24},{24,16},{1,9},{9,1},{17,25},{25,17},{2,10},{10... | collective-permute-start | bytes 98312 | tf_op jit(solution)/shard_map/ppermute | solution.py:188
  31.4 12.3 %collective-permute-start.12 = (f32[128,128]{1,0:T(8,128)S(1)}, f32[128,128]{1,0:T(8,128)S(1)}, u32[]{:S(2)}, u32[]{:S(2)}) collective-permute-start(f32[128,128]{1,0:T(8,128)S(1)} %maximum_select_fusion.1), channel_id=1, source_target_pairs={{0,1},{1,0},{2,3},{3,2},{4,5},{5,4},{6,7},{7,6},{8,9},{9,8},{10,11... | collective-permute-start | bytes 196616 | tf_op jit(solution)/shard_map/ppermute | solution.py:337
  33.3 10.4 %collective-permute-start.13 = (f32[128,128]{1,0:T(8,128)S(1)}, f32[128,128]{1,0:T(8,128)S(1)}, u32[]{:S(2)}, u32[]{:S(2)}) collective-permute-start(f32[128,128]{1,0:T(8,128)S(1)} %maximum_select_fusion.1), channel_id=1, source_target_pairs={{0,2},{1,3},{2,0},{3,1},{4,6},{5,7},{6,4},{7,5},{8,10},{9,11},{10,... | collective-permute-start | bytes 196616 | tf_op jit(solution)/shard_map/ppermute | solution.py:337
  35.9 7.9 %collective-permute-start.14 = (f32[128,128]{1,0:T(8,128)S(1)}, f32[128,128]{1,0:T(8,128)S(1)}, u32[]{:S(2)}, u32[]{:S(2)}) collective-permute-start(f32[128,128]{1,0:T(8,128)S(1)} %maximum_select_fusion.1), channel_id=1, source_target_pairs={{0,3},{1,2},{2,1},{3,0},{4,7},{5,6},{6,5},{7,4},{8,11},{9,10},{10,... | collective-permute-start | bytes 196616 | tf_op jit(solution)/shard_map/ppermute | solution.py:337
  39.5 4.9 %collective-permute-start.8 = (bf16[2,512,128]{2,1,0:T(8,128)(2,1)S(1)}, bf16[2,512,128]{2,1,0:T(8,128)(2,1)S(1)}, u32[]{:S(2)}, u32[]{:S(2)}) collective-permute-start(bf16[2,512,128]{2,1,0:T(8,128)(2,1)S(1)} %get-tuple-element.8), channel_id=1, source_target_pairs={{0,8},{8,0},{16,24},{24,16},{1,9},{9,1},{17,25},{25,17},{2,10},{10... | collective-permute-start | bytes 786440 | tf_op jit(solution)/shard_map/ppermute | solution.py:188
  43.2 1.7 %collective-permute-start.9 = (bf16[2,512,128]{2,1,0:T(8,128)(2,1)S(1)}, bf16[2,512,128]{2,1,0:T(8,128)(2,1)S(1)}, u32[]{:S(2)}, u32[]{:S(2)}) collective-permute-start(bf16[2,512,128]{2,1,0:T(8,128)(2,1)S(1)} %get-tuple-element.9), channel_id=1, source_target_pairs={{0,8},{8,0},{16,24},{24,16},{1,9},{9,1},{17,25},{25,17},{2,10},{10... | collective-permute-start | bytes 786440 | tf_op jit(solution)/shard_map/ppermute | solution.py:188

commit v3 on v1

v3 whole, which is shorter than its diff:
```python
import functools

import jax
import jax.numpy as jnp
from jax import lax
from jax.experimental import pallas as pl
from jax.experimental.pallas import tpu as pltpu
from jax.sharding import PartitionSpec as P

GROUP_SIZE = 16
CORES = 2
VMEM_BYTES = 16 << 20
UNROLL = 16
OWN_WEIGHT = 100
EARLY = 12
C1 = True
C2 = True


def pick(condition, first, second):
    return jnp.where(condition, first, second)


def group_rows(ref, index, first_row=0):
    sequences, _, positions = ref.shape
    start = pl.multiple_of(first_row + index * GROUP_SIZE, GROUP_SIZE)
    return ref[:, pl.ds(start, GROUP_SIZE), :].reshape(sequences * GROUP_SIZE, positions)


def chunked(groups, body):
    count = max(size for size in range(1, UNROLL + 1) if groups % size == 0)

    def chunk(number, carry):
        body(number * count, count)
        return carry

    lax.fori_loop(0, groups // count, chunk, 0)


def input_grad_kernel(chips, which, offset, slot_rows, place, *refs):
    filter_refs, refs = refs[: CORES * chips], refs[CORES * chips :]
    own_grad, peer_grad, refs = refs[0], refs[1], refs[2:]
    round_refs, (mine, theirs, taps) = list(refs[:-3]), refs[-3:]
    core, chip = place[0], place[1]
    first_core = core == 0
    sequences, size, positions = mine.shape
    part = own_grad.shape[1] // CORES // 2
    if len(round_refs) < CORES * (chips - 1):
        round_refs = [
            ref.at[pl.ds(core_of * sequences, sequences)] for ref in round_refs for core_of in range(CORES)
        ]
    groups = size // GROUP_SIZE
    first_taps = which * (part // GROUP_SIZE) + offset
    rows = sequences * GROUP_SIZE
    width = CORES * chips * positions
    own_row = pl.multiple_of((core * 2 + which) * part + offset * GROUP_SIZE, GROUP_SIZE)
    all_groups = taps.shape[0]
    own_taps = pl.ds(pl.multiple_of(core * all_groups, all_groups), all_groups)
    holders = range(all_groups // slot_rows)
    for rotation in range(chips):
        start = lax.rem(chip + rotation, chips) * (CORES * positions)
        pair = filter_refs[CORES * rotation : CORES * (rotation + 1)]
        if rotation == 0:
            pair = [ref[own_taps, :] for ref in pair]
        else:
            pair = [
                jnp.concatenate([ref[holder, part : part + slot_rows, :] for holder in holders], axis=0)
                for ref in pair
            ]
        pair = jnp.concatenate([pick(first_core, *pair), pick(first_core, *pair[::-1])], axis=1)
        taps[:, pl.ds(pl.multiple_of(start, positions), CORES * positions)] = pair.astype(jnp.float32)
    row = lax.broadcasted_iota(jnp.int32, (positions, width), 0)
    column = lax.broadcasted_iota(jnp.int32, (positions, width), 1)
    causal = column >= row
    zeros = jnp.zeros((rows, positions), jnp.bfloat16)

    def one_group(index):
        strip = jnp.broadcast_to(taps[pl.ds(first_taps + index, 1), :], (positions, width))
        strip = pltpu.roll(strip, 0, 1, stride=1, stride_axis=0)
        strip = jnp.where(causal, strip, 0.0).astype(jnp.bfloat16)
        own, peer = group_rows(own_grad, index, own_row), group_rows(peer_grad, index, own_row)
        blocks = [pick(first_core, own, peer), pick(first_core, peer, own)]
        for distance in range(1, chips):
            received = [group_rows(ref, index) for ref in round_refs[2 * distance - 2 : 2 * distance]]
            lower = chip + distance < chips
            blocks.append(pick(lower, pick(first_core, *received), zeros))
            blocks.append(pick(lower, pick(first_core, *received[::-1]), zeros))
        grads = jnp.concatenate(
            [jnp.concatenate(blocks, axis=1), jnp.concatenate(blocks[1:] + [zeros], axis=1)], axis=0
        )
        sums = lax.dot_general(
            grads, strip, (((1,), (1,)), ((), ())), preferred_element_type=jnp.float32
        ).astype(jnp.bfloat16)
        start = pl.multiple_of(index * GROUP_SIZE, GROUP_SIZE)
        shape = (sequences, GROUP_SIZE, positions)
        early, late = sums[:rows], sums[rows:]
        mine[:, pl.ds(start, GROUP_SIZE), :] = pick(first_core, early, late).reshape(shape)
        theirs[:, pl.ds(start, GROUP_SIZE), :] = pick(first_core, late, early).reshape(shape)

    def body(first, count):
        for index in range(count):
            one_group(first + index)

    chunked(groups, body)


def reversal(positions):
    row = lax.broadcasted_iota(jnp.int32, (positions, positions), 0)
    column = lax.broadcasted_iota(jnp.int32, (positions, positions), 1)
    return (row + column == positions - 1).astype(jnp.float32).astype(jnp.bfloat16)


def flip_rows(out, core, values, flip):
    sequences, channels, positions = values.shape
    flat = values.reshape(sequences * channels, positions)
    flat = jnp.dot(flat, flip, preferred_element_type=jnp.float32).astype(jnp.bfloat16)
    out[core, :, :channels, :] = flat.reshape(sequences, channels, positions)


def lag_sums(flipped, grads, keep, lead):
    products = lax.dot_general(
        flipped, grads, (((0,), (0,)), ((), ())), preferred_element_type=jnp.float32
    )
    positions = products.shape[0]
    if keep is not None:
        products = jnp.where(keep, products, 0.0)
    if lead:
        products = jnp.concatenate([jnp.zeros((positions, lead), jnp.float32), products], axis=1)
    products = pltpu.roll(products, products.shape[1] - positions + 1, 1, stride=1, stride_axis=0)
    return jnp.sum(products, axis=0, keepdims=True)


def own_lags_kernel(place, own_input, peer_input, own_grad, peer_grad, out, flipped):
    first_core = place[0] == 0
    sequences, channels, positions = own_input.shape
    half = channels // CORES
    own_row = pl.multiple_of(place[0] * half, half)
    rows, width = sequences * GROUP_SIZE, CORES * positions
    flip = reversal(positions)
    row = lax.broadcasted_iota(jnp.int32, (positions, width), 0)
    column = lax.broadcasted_iota(jnp.int32, (positions, width), 1)
    keep = column + row >= positions - 1
    zeros = jnp.zeros((rows, positions), jnp.bfloat16)
    out[...] = jnp.zeros_like(out)

    def body(first, count):
        start = pl.multiple_of(own_row + first * GROUP_SIZE, GROUP_SIZE)
        own = own_input[:, pl.ds(start, count * GROUP_SIZE), :]
        peer = peer_input[:, pl.ds(start, count * GROUP_SIZE), :]
        flip_rows(flipped, 0, pick(first_core, own, peer), flip)
        flip_rows(flipped, 1, pick(first_core, peer, own), flip)
        for index in range(count):
            values = jnp.concatenate(
                [group_rows(flipped.at[core], index) for core in range(CORES)], axis=0
            )
            own = group_rows(own_grad, index, start)
            peer = group_rows(peer_grad, index, start)
            early, late = pick(first_core, own, peer), pick(first_core, peer, own)
            grads = jnp.concatenate(
                [jnp.concatenate([early, late], axis=1), jnp.concatenate([late, zeros], axis=1)], axis=0
            )
            out[pl.ds(first + index, 1), :width] = lag_sums(values, grads, keep, 0)

    chunked(half // GROUP_SIZE, body)


def round_lags_kernel(
    chips, distance, place, own_input, peer_input, own_grad, peer_grad, own_got, peer_got, running, out, flipped
):
    first_core = place[0] == 0
    lower = place[1] + distance < chips
    sequences, channels, positions = own_input.shape
    part = channels // CORES // 2
    rows = sequences * GROUP_SIZE
    flip = reversal(positions)
    part_row = pl.multiple_of((place[0] * 2 + jnp.where(lower, 0, 1)) * part, part)
    part_group = pl.multiple_of(jnp.where(lower, 0, part // GROUP_SIZE), part // GROUP_SIZE)
    if 2 * distance == chips:
        first_lag = (2 * distance - 2) * positions
    else:
        first_lag = pl.multiple_of(
            jnp.where(lower, 2 * distance - 2, 2 * (chips - distance) - 2) * positions, positions
        )
    zeros = jnp.zeros((rows, positions), jnp.bfloat16)
    out[...] = running[...]

    def body(first, count):
        start = pl.multiple_of(first * GROUP_SIZE, GROUP_SIZE)
        own_rows = pl.ds(pl.multiple_of(part_row + start, GROUP_SIZE), count * GROUP_SIZE)
        got_rows = pl.ds(start, count * GROUP_SIZE)
        own = pick(lower, own_input[:, own_rows, :], own_got[:, got_rows, :])
        peer = pick(lower, peer_input[:, own_rows, :], peer_got[:, got_rows, :])
        flip_rows(flipped, 0, pick(first_core, own, peer), flip)
        flip_rows(flipped, 1, pick(first_core, peer, own), flip)
        for index in range(count):
            got = group_rows(own_got, index, start), group_rows(peer_got, index, start)
            grads = (
                group_rows(own_grad, index, part_row + start),
                group_rows(peer_grad, index, part_row + start),
            )
            right = [pick(lower, b, a) for a, b in zip(grads, got)]
            values = jnp.concatenate(
                [group_rows(flipped.at[core], index) for core in range(CORES)], axis=0
            )
            early, late = pick(first_core, *right), pick(first_core, *right[::-1])
            pairs = jnp.concatenate(
                [
                    jnp.concatenate([zeros, early, late], axis=1),
                    jnp.concatenate([early, late, zeros], axis=1),
                ],
                axis=0,
            )
            where = (pl.ds(part_group + first + index, 1), pl.ds(first_lag, 2 * CORES * positions))
            out[where] = out[where] + lag_sums(values, pairs, None, positions)

    chunked(part // GROUP_SIZE, body)


def assemble_kernel(out_place, *refs):
    parts, out, sems = refs[:-2], refs[-2], refs[-1]
    half = out.shape[1] // CORES
    core = out_place[0]
    copies = []
    start = core * half
    for number, ref in enumerate(parts):
        if number == len(parts) // 2:
            start = (1 - core) * half
        rows = pl.ds(pl.multiple_of(start, GROUP_SIZE), ref.shape[1])
        copies.append(pltpu.make_async_copy(ref, out.at[:, rows, :], sems.at[number]))
        start = start + ref.shape[1]
    for copy in copies:
        copy.start()
    for copy in copies:
        copy.wait()


def parts_kernel(chips, slot_rows, inputs, output_grad, filters, *refs):
    count = CORES * (chips - 1)
    outs, stages, in_sems, out_sems = refs[:count], refs[count : 2 * count], refs[-2], refs[-1]
    sequences = inputs.shape[0]
    half = inputs.shape[1] // CORES
    part = half // 2
    groups = filters.shape[0] // CORES
    own_index = lax.axis_index("seq")
    chip, core = lax.div(own_index, CORES), lax.rem(own_index, CORES)

    def arrival(source, start, target, number):
        return pltpu.make_async_copy(
            source.at[:, pl.ds(pl.multiple_of(start, GROUP_SIZE), part), :],
            target.at[:, pl.ds(0, part), :],
            in_sems.at[number],
        )

    for number in range(count):
        distance, other = number // CORES + 1, number % CORES
        whose = core if other == 0 else 1 - core
        start = whose * half
        target = stages[number]
        for sequence in range(sequences):
            slot = sequence if slot_rows < groups else 0
            row = pl.multiple_of(whose * groups + slot * slot_rows, GROUP_SIZE)
            pltpu.make_async_copy(
                filters.at[pl.ds(row, slot_rows), :],
                target.at[sequence, pl.ds(part, slot_rows), :],
                in_sems.at[number],
            ).start()
        lax.cond(
            chip >= distance,
            lambda: arrival(output_grad, start, target, number).start(),
            lambda: arrival(inputs, start + part, target, number).start(),
        )
    for number in range(count):
        pltpu.make_async_copy(stages[number], stages[number], in_sems.at[number]).wait()
        pltpu.make_async_copy(stages[number], outs[number], out_sems.at[number]).start()
    for number in range(count):
        pltpu.make_async_copy(stages[number], outs[number], out_sems.at[number]).wait()


def second_kernel(own_grad, peer_grad, *refs):
    outs, sems = refs[:-1], refs[-1]
    sequences = own_grad.shape[0]
    half = own_grad.shape[1] // CORES
    core = lax.rem(lax.axis_index("seq"), CORES)
    start = core * half + half // 2
    copies = []
    for out in outs:
        for number, ref in enumerate((own_grad, peer_grad)):
            copies.append(
                pltpu.make_async_copy(
                    ref.at[:, pl.ds(pl.multiple_of(start, GROUP_SIZE), out.shape[1]), :],
                    out.at[pl.ds(number * sequences, sequences)],
                    sems.at[len(copies)],
                )
            )
        start = start + out.shape[1]
    for copy in copies:
        copy.start()
    for copy in copies:
        copy.wait()


def per_device(inputs, output_grad, filters):
    sequences, channels, positions = inputs.shape
    shard_count = lax.axis_size("seq")
    chips = shard_count // CORES
    own_index = lax.axis_index("seq")
    chip, core = own_index // CORES, own_index % CORES
    place = jnp.stack([core, chip]).astype(jnp.int32)
    half = channels // CORES
    part = half // 2
    groups = half // GROUP_SIZE
    slot_rows = groups // 2 if sequences == 2 and groups % (2 * GROUP_SIZE) == 0 else groups
    length = shard_count * positions
    rows = sequences * GROUP_SIZE
    rounds = range(1, chips)

    def swap_cores(value):
        return lax.ppermute(value, "seq", [(i, i ^ 1) for i in range(shard_count)])

    def from_chip(value, distance, wrap, other=0):
        pairs = [
            (i, (i - distance * CORES) % shard_count ^ other)
            for i in range(shard_count)
            if wrap or i >= distance * CORES
        ]
        return lax.ppermute(value, "seq", pairs)

    in_hbm = pl.BlockSpec(memory_space=pltpu.HBM)
    params = pltpu.CompilerParams(vmem_limit_bytes=VMEM_BYTES)

    filters_peer = swap_cores(filters)
    grad_peer, input_peer = swap_cores(output_grad), swap_cores(inputs)

    heights = [part + slot_rows] * (CORES * (chips - 1))
    outgoing = pl.pallas_call(
        functools.partial(parts_kernel, chips, slot_rows),
        in_specs=[in_hbm] * 3,
        out_specs=[in_hbm] * len(heights),
        out_shape=[jax.ShapeDtypeStruct((sequences, height, positions), inputs.dtype) for height in heights],
        scratch_shapes=[pltpu.VMEM((sequences, height, positions), inputs.dtype) for height in heights]
        + [pltpu.SemaphoreType.DMA((len(heights),))] * 2,
    )(inputs, output_grad, filters)

    first = {
        k: [from_chip(outgoing[CORES * (k - 1) + other], k, True, other) for other in range(CORES)]
        for k in rounds
    }

    in_smem, in_vmem = pl.BlockSpec(memory_space=pltpu.SMEM), pl.BlockSpec(memory_space=pltpu.VMEM)
    flip_scratch = pltpu.VMEM((CORES, sequences, UNROLL * GROUP_SIZE, positions), jnp.bfloat16)

    def vmem(value):
        return pltpu.with_memory_space_constraint(value, pltpu.VMEM)

    def cost(group_count, depth, width, arrays):
        return pl.CostEstimate(
            flops=2 * group_count * depth * positions * width,
            bytes_accessed=arrays * group_count * rows * positions * 2,
            transcendentals=0,
        )

    input_here, grad_here = vmem(inputs), vmem(output_grad)
    input_peer, grad_peer = vmem(input_peer), vmem(grad_peer)
    both = (input_here, input_peer, grad_here, grad_peer)
    part_groups = groups // 2
    early_groups = part_groups * EARLY // 32
    sizes = [early_groups, part_groups - early_groups]
    outgoing = pl.pallas_call(
        second_kernel,
        in_specs=[in_vmem] * 2,
        out_specs=[in_hbm] * len(sizes),
        out_shape=[
            jax.ShapeDtypeStruct((CORES * sequences, size * GROUP_SIZE, positions), inputs.dtype) for size in sizes
        ],
        scratch_shapes=[pltpu.SemaphoreType.DMA((CORES * len(sizes),))],
    )(grad_here, grad_peer)
    second = [{k: [from_chip(value, k, False)] for k in rounds} for value in outgoing]

    lags = pl.pallas_call(
        own_lags_kernel,
        in_specs=[in_smem] + [in_vmem] * 4,
        out_specs=in_vmem,
        out_shape=pltpu.VMEM((groups, length), jnp.float32),
        scratch_shapes=[flip_scratch],
        cost_estimate=cost(groups * OWN_WEIGHT, CORES * rows, CORES * positions, 4),
        compiler_params=params,
    )(place, *both)

    for k in rounds:
        lags = pl.pallas_call(
            functools.partial(round_lags_kernel, chips, k),
            in_specs=[in_smem] + [in_vmem] * 7,
            out_specs=in_vmem,
            out_shape=pltpu.VMEM((groups, length), jnp.float32),
            scratch_shapes=[flip_scratch],
            cost_estimate=cost(groups // 2, CORES * rows, 3 * positions, 6),
            compiler_params=params,
        )(place, *both, *[vmem(ref) for ref in first[k]], vmem(lags))

    if C1:
        for k in rounds:
            lags, second[0][k][0] = lax.optimization_barrier((lags, second[0][k][0]))

    def chip_lags(which):
        return lax.dynamic_slice_in_dim(lags, which * CORES * positions, CORES * positions, 1)

    sums = chip_lags(chip)
    for k in rounds:
        sums = sums + from_chip(chip_lags((chip - k) % chips), k, True)
    def input_part(which, offset, count, received):
        come = [ref for k in rounds for ref in first[k]]
        arrays = [ref for k in rounds for ref in received[k]]
        values = [filters, filters_peer, *come, grad_here, grad_peer, *arrays]
        return pl.pallas_call(
            functools.partial(input_grad_kernel, chips, which, offset, slot_rows),
            in_specs=[in_smem] + [in_vmem] * len(values),
            out_specs=[in_vmem] * 2,
            out_shape=[jax.ShapeDtypeStruct((sequences, count * GROUP_SIZE, positions), jnp.bfloat16)] * 2,
            scratch_shapes=[pltpu.VMEM((groups, length), jnp.float32)],
            cost_estimate=cost(count, CORES * rows, length, 4 + len(arrays)),
            compiler_params=params,
        )(place, *[vmem(value) for value in values])

    results = [
        input_part(0, 0, part_groups, first),
        input_part(1, 0, sizes[0], second[0]),
        input_part(1, sizes[0], sizes[1], second[1]),
    ]
    mine = jnp.concatenate([result[0] for result in results], axis=1)
    got = jnp.concatenate([swap_cores(result[1]) for result in results], axis=1)
    input_grad = jnp.where(
        core == 0, jnp.concatenate([mine, got], axis=1), jnp.concatenate([got, mine], axis=1)
    )

    if C2:
        sums, _ = lax.optimization_barrier((sums, results[0][0]))
    keep = lax.dynamic_slice_in_dim(sums, core * positions, positions, 1)
    got = swap_cores(lax.dynamic_slice_in_dim(sums, (1 - core) * positions, positions, 1))
    own = jnp.where(core == 0, jnp.concatenate([keep, got], axis=0), jnp.concatenate([got, keep], axis=0))
    copies = lax.axis_size("dp")
    terms = [own]
    for k in range(1, copies):
        terms.append(lax.ppermute(own, "dp", [(i, i ^ k) for i in range(copies)]))
    while len(terms) > 1:
        terms = [a + b for a, b in zip(terms[::2], terms[1::2])]
    filter_grad = terms[0]
    return (input_grad, filter_grad)


def solution(mesh):
    in_specs = (P("dp", "chan", "seq"), P("dp", "chan", "seq"), P("chan", "seq"))
    out_specs = (P("dp", "chan", "seq"), P("chan", "seq"))
    return jax.shard_map(
        per_device, mesh=mesh, in_specs=in_specs, out_specs=out_specs, check_vma=False
    )
```

time: 67.2 us -> 44 us (0.65)
  Pallas kernels: 31.4 us -> 17.7 us
  starting transfers between devices: 19.1 us -> 12.8 us
  other arithmetic: 4.45 us -> 1.82 us
  local copies, waits for them, and re-layouts: 2.91 us -> 1.58 us
  waiting for transfers between devices: 8.19 us -> 8.98 us
    pallas_call x4 -> x7, Pallas kernels: 31.4 us -> 17.7 us  [the longest x3 5.81 us: input_part(): pl.pallas_call(functools.partial(input_grad_kernel, chips, which, offset,...]
    ppermute x6 -> x5, starting transfers between devices: 10.1 us -> 6.49 us  [from_chip(): return lax.ppermute(value, 'seq', pairs)]
    ppermute x3, starting transfers between devices: 7.82 us -> 4.45 us  [per_device(): terms.append(lax.ppermute(own, 'dp', [(i, i ^ k) for i in range(copies)]))]
    ppermute x3, waiting for transfers between devices: 0.01 us -> 3.04 us  [per_device(): terms.append(lax.ppermute(own, 'dp', [(i, i ^ k) for i in range(copies)]))]
    ppermute x6 -> x5, waiting for transfers between devices: 7.67 us -> 4.77 us  [from_chip(): return lax.ppermute(value, 'seq', pairs)]
    dynamic_slice x2 -> x0, local copies, waits for them, and re-layouts: 2.86 us -> none  [half_of(): return lax.dynamic_slice_in_dim(value, which * half, half, 1)]
    select_n x2 -> x0, other arithmetic: 1.69 us -> none  [the longest x1 0.85 us: per_device(): jnp.where(sends_grad, grad_peer[:, :part], input_peer[:, part:])]
    unnamed x4 -> x15, local copies, waits for them, and re-layouts: 0.01 us -> 1.47 us
  transfers between devices with their start and end apart: 15 -> 15, of which waited for: 3 -> 4; matrix products, arithmetic and copies ran while one was open for 6% -> 2% of each run, Pallas kernels for 31% -> 41%
where the time goes in v3:
time: 44 us; the launch traced here: 43.8 us
  Pallas kernels  17.7 us (40%)
  starting transfers between devices  12.8 us (29%)
  waiting for transfers between devices  8.98 us (20%)
  other arithmetic  1.82 us (4%)
  local copies, waits for them, and re-layouts  1.58 us (4%)
  between operations  0.86 us (2%)
    ppermute x5, starting transfers between devices, from_chip(): return lax.ppermute(value, 'seq', pairs)  6.49 us
    pallas_call x3, Pallas kernels, input_part(): pl.pallas_call(functools.partial(input_grad_kernel, chips, which, offset,...  5.81 us
    pallas_call x1, Pallas kernels, per_device(): pl.pallas_call(own_lags_kernel, in_specs=[in_smem] + [in_vmem] * 4, out_s...  5.33 us
    ppermute x5, waiting for transfers between devices, from_chip(): return lax.ppermute(value, 'seq', pairs)  4.77 us
    ppermute x3, starting transfers between devices, per_device(): terms.append(lax.ppermute(own, 'dp', [(i, i ^ k) for i in range(copies)]))  4.45 us
    pallas_call x1, Pallas kernels, per_device(): pl.pallas_call(functools.partial(round_lags_kernel, chips, k), in_specs=[...  3.94 us
    ppermute x3, waiting for transfers between devices, per_device(): terms.append(lax.ppermute(own, 'dp', [(i, i ^ k) for i in range(copies)]))  3.04 us
    pallas_call x1, Pallas kernels, per_device(): pl.pallas_call(functools.partial(parts_kernel, chips, slot_rows), in_spec...  1.84 us
  transfers between devices with their start and end apart: 15, of which 4 were waited for; matrix products, arithmetic and copies ran while one was open for 2% of the time, Pallas kernels for 41%

profile of v3, /device:TPU:0, one launch (start us, length us, event | category | flops | bytes accessed | tf_op | source)
XLA Modules:
  0.0 43.8 jit_solution(3299096921768403220)
XLA Ops:
  0.6 0.5 %collective-permute-start.3 = (bf16[2,2048,128]{2,1,0:T(8,128)(2,1)}, bf16[2,2048,128]{2,1,0:T(8,128)(2,1)S(1)}, u32[]{:S(2)}, u32[]{:S(2)}) collective-permute-start(bf16[2,2048,128]{2,1,0:T(8,128)(2,1)} %refs_4_.5), channel_id=1, source_target_pairs={{0,8},{8,0},{16,24},{24,16},{1,9},{9,1},{17,25},{25,17},{2,10},{10... | collective-permute-start | bytes 3145736 | tf_op jit(solution)/shard_map/ppermute | solution.py:318
  1.2 0.1 collective-permute-start.4
  1.2 0.4 collective-permute-start
  1.7 1.8 %shard_map.50 = (bf16[2,544,128]{2,1,0:T(8,128)(2,1)}, bf16[2,544,128]{2,1,0:T(8,128)(2,1)}) custom-call(bf16[2,2048,128]{2,1,0:T(8,128)(2,1)} %own_input.3, bf16[2,2048,128]{2,1,0:T(8,128)(2,1)} %refs_4_.5, bf16[128,128]{1,0:T(8,128)(2,1)} %refs_0_.5), custom_call_target="tpu_custom_call" | custom-call | tf_op jit(solution)/shard_map/pallas_call | solution.py:335
  3.5 2.7 %collective-permute-start.1 = (bf16[2,544,128]{2,1,0:T(8,128)(2,1)}, bf16[2,544,128]{2,1,0:T(8,128)(2,1)S(1)}, u32[]{:S(2)}, u32[]{:S(2)}) collective-permute-start(bf16[2,544,128]{2,1,0:T(8,128)(2,1)} %get-tuple-element.15), channel_id=1, source_target_pairs={{0,16},{8,24},{16,0},{24,8},{1,17},{9,25},{17,1},{25,9},{2,18},{10... | collective-permute-start | bytes 835592 | tf_op jit(solution)/shard_map/ppermute | solution.py:326
  6.2 0.1 collective-permute-start.2
  6.3 0.1 pad_add_fusion.place
  6.4 0.8 %shard_map.54 = (bf16[4,192,128]{2,1,0:T(8,128)(2,1)}, bf16[4,320,128]{2,1,0:T(8,128)(2,1)}) custom-call(bf16[2,2048,128]{2,1,0:T(8,128)(2,1)S(1)} %copy-done, bf16[2,2048,128]{2,1,0:T(8,128)(2,1)S(1)} %collective-permute-done.3.refs_5_.peer_grad), custom_call_target="tpu_custom_call" | custom-call | tf_op jit(solution)/shard_map/pallas_call | solution.py:368
  7.2 1.3 %collective-permute-start.5 = (bf16[4,192,128]{2,1,0:T(8,128)(2,1)}, bf16[4,192,128]{2,1,0:T(8,128)(2,1)S(1)}, u32[]{:S(2)}, u32[]{:S(2)}) collective-permute-start(bf16[4,192,128]{2,1,0:T(8,128)(2,1)} %get-tuple-element.18), channel_id=1, source_target_pairs={{16,0},{24,8},{17,1},{25,9},{18,2},{26,10},{19,3},{27,11},{20,4},{... | collective-permute-start | bytes 589832 | tf_op jit(solution)/shard_map/ppermute | solution.py:326
  8.5 1.2 %copy-done.1 = bf16[2,2048,128]{2,1,0:T(8,128)(2,1)S(1)} copy-done((bf16[2,2048,128]{2,1,0:T(8,128)(2,1)S(1)}, bf16[2,2048,128]{2,1,0:T(8,128)(2,1)}, u32[]{:S(2)}) %copy-start.1) | copy-done | bytes 1048600
  9.8 5.3 %shard_map.52.running = f32[64,512]{1,0:T(8,128)S(1)} custom-call(s32[2]{0:T(128)S(1)} %pad_add_fusion.place, bf16[2,2048,128]{2,1,0:T(8,128)(2,1)S(1)} %copy-done.1, bf16[2,2048,128]{2,1,0:T(8,128)(2,1)} %collective-permute-done.4.peer_input, bf16[2,2048,128]{2,1,0:T(8,128)(2,1)S(1)} %copy-done, ...), custom_call_target="tpu_custom_call" | custom-call | flops 26843545600 | bytes 209715200 | tf_op jit(solution)/shard_map/pallas_call | solution.py:379
  15.1 0.0 copy-start.3
  15.1 4.2 %collective-permute-done.2.refs_3_.refs_7_.peer_got = bf16[2,544,128]{2,1,0:T(8,128)(2,1)S(1)} collective-permute-done((bf16[2,544,128]{2,1,0:T(8,128)(2,1)}, bf16[2,544,128]{2,1,0:T(8,128)(2,1)S(1)}, u32[]{:S(2)}, u32[]{:S(2)}) %collective-permute-start.2) | collective-permute-done | bytes 278560 | tf_op jit(solution)/shard_map/ppermute | solution.py:326
  19.3 3.9 %shard_map.53 = f32[64,512]{1,0:T(8,128)S(1)} custom-call(s32[2]{0:T(128)S(1)} %pad_add_fusion.place, bf16[2,2048,128]{2,1,0:T(8,128)(2,1)S(1)} %copy-done.1, bf16[2,2048,128]{2,1,0:T(8,128)(2,1)} %collective-permute-done.4.peer_input, bf16[2,2048,128]{2,1,0:T(8,128)(2,1)S(1)} %copy-done, bf16[2,2048,128]{2,1,0:T(8,128)(2,1)S(1)} %collective-permute-done.3.refs_5_.peer_grad, ...), custom_call_target="tpu_custom_call" | custom-call | flops 201326592 | bytes 1572864 | tf_op jit(solution)/shard_map/pallas_call | solution.py:390
  23.3 0.5 %collective-permute-done.5.refs_6_ = bf16[4,192,128]{2,1,0:T(8,128)(2,1)S(1)} collective-permute-done((bf16[4,192,128]{2,1,0:T(8,128)(2,1)}, bf16[4,192,128]{2,1,0:T(8,128)(2,1)S(1)}, u32[]{:S(2)}, u32[]{:S(2)}) %collective-permute-start.5) | collective-permute-done | bytes 196640 | tf_op jit(solution)/shard_map/ppermute | solution.py:326
  23.8 1.1 %collective-permute-start.10 = (f32[64,256]{1,0:T(8,128)S(1)}, f32[64,256]{1,0:T(8,128)S(1)}, u32[]{:S(2)}, u32[]{:S(2)}) collective-permute-start(f32[64,256]{1,0:T(8,128)S(1)} %constant_dynamic-slice_fusion.2), channel_id=1, source_target_pairs={{0,16},{8,24},{16,0},{24,8},{1,17},{9,25},{17,1},{25,9},{2,18},{10... | collective-permute-start | bytes 196616 | tf_op jit(solution)/shard_map/ppermute | solution.py:326
  25.0 1.3 %collective-permute-start.6 = (bf16[4,320,128]{2,1,0:T(8,128)(2,1)S(1)}, bf16[4,320,128]{2,1,0:T(8,128)(2,1)S(1)}, u32[]{:S(2)}, u32[]{:S(2)}) collective-permute-start(bf16[4,320,128]{2,1,0:T(8,128)(2,1)S(1)} %copy-done.3), channel_id=1, source_target_pairs={{16,0},{24,8},{17,1},{25,9},{18,2},{26,10},{19,3},{27,11},{20,4},{... | collective-permute-start | bytes 983048 | tf_op jit(solution)/shard_map/ppermute | solution.py:326
  26.3 2.5 %shard_map.51 = (bf16[2,512,128]{2,1,0:T(8,128)(2,1)S(1)}, bf16[2,512,128]{2,1,0:T(8,128)(2,1)S(1)}) custom-call(s32[2]{0:T(128)S(1)} %pad_add_fusion.place, bf16[128,128]{1,0:T(8,128)(2,1)S(1)} %copy-done.2, bf16[128,128]{1,0:T(8,128)(2,1)S(1)} %collective-permute-done.refs_1_, bf16[2,544,128]{2,1,0:T(8,128)(2,1)S(1)} %collective-permute-done.1.refs_2_.refs_6_.own_got, ...), custom_call_target="tpu_custom_call" | custom-call | flops 268435456 | bytes 1572864 | tf_op jit(solution)/shard_map/pallas_call | solution.py:414
  28.8 0.1 collective-permute-start.7
  28.9 1.4 %shard_map.55 = (bf16[2,192,128]{2,1,0:T(8,128)(2,1)S(1)}, bf16[2,192,128]{2,1,0:T(8,128)(2,1)S(1)}) custom-call(s32[2]{0:T(128)S(1)} %pad_add_fusion.place, bf16[128,128]{1,0:T(8,128)(2,1)S(1)} %copy-done.2, bf16[128,128]{1,0:T(8,128)(2,1)S(1)} %collective-permute-done.refs_1_, bf16[2,544,128]{2,1,0:T(8,128)(2,1)S(1)} %collective-permute-done.1.refs_2_.refs_6_.own_got, ...), custom_call_target="tpu_custom_call" | custom-call | flops 100663296 | bytes 491520 | tf_op jit(solution)/shard_map/pallas_call | solution.py:414
  30.2 0.6 %collective-permute-start.8 = (bf16[2,192,128]{2,1,0:T(8,128)(2,1)S(1)}, bf16[2,192,128]{2,1,0:T(8,128)(2,1)S(1)}, u32[]{:S(2)}, u32[]{:S(2)}) collective-permute-start(bf16[2,192,128]{2,1,0:T(8,128)(2,1)S(1)} %get-tuple-element.24), channel_id=1, source_target_pairs={{0,8},{8,0},{16,24},{24,16},{1,9},{9,1},{17,25},{25,17},{2,10},{10... | collective-permute-start | bytes 294920 | tf_op jit(solution)/shard_map/ppermute | solution.py:318
  30.8 0.1 collective-permute-start.11
  31.0 1.2 %collective-permute-done.11 = f32[64,128]{1,0:T(8,128)S(1)} collective-permute-done((f32[64,128]{1,0:T(8,128)S(1)}, f32[64,128]{1,0:T(8,128)S(1)}, u32[]{:S(2)}, u32[]{:S(2)}) %collective-permute-start.11) | collective-permute-done | bytes 32800 | tf_op jit(solution)/shard_map/ppermute | solution.py:318
  32.1 3.7 %collective-permute-start.14 = (f32[128,128]{1,0:T(8,128)S(1)}, f32[128,128]{1,0:T(8,128)S(1)}, u32[]{:S(2)}, u32[]{:S(2)}) collective-permute-start(f32[128,128]{1,0:T(8,128)S(1)} %maximum_select_fusion), channel_id=1, source_target_pairs={{0,3},{1,2},{2,1},{3,0},{4,7},{5,6},{6,5},{7,4},{8,11},{9,10},{10,... | collective-permute-start | bytes 196616 | tf_op jit(solution)/shard_map/ppermute | solution.py:443
  35.8 0.8 %collective-permute-start.12 = (f32[128,128]{1,0:T(8,128)S(1)}, f32[128,128]{1,0:T(8,128)S(1)}, u32[]{:S(2)}, u32[]{:S(2)}) collective-permute-start(f32[128,128]{1,0:T(8,128)S(1)} %maximum_select_fusion), channel_id=1, source_target_pairs={{0,1},{1,0},{2,3},{3,2},{4,5},{5,4},{6,7},{7,6},{8,9},{9,8},{10,11... | collective-permute-start | bytes 196616 | tf_op jit(solution)/shard_map/ppermute | solution.py:443
  36.6 1.9 %shard_map.56 = (bf16[2,320,128]{2,1,0:T(8,128)(2,1)S(1)}, bf16[2,320,128]{2,1,0:T(8,128)(2,1)S(1)}) custom-call(s32[2]{0:T(128)S(1)} %pad_add_fusion.place, bf16[128,128]{1,0:T(8,128)(2,1)S(1)} %copy-done.2, bf16[128,128]{1,0:T(8,128)(2,1)S(1)} %collective-permute-done.refs_1_, bf16[2,544,128]{2,1,0:T(8,128)(2,1)S(1)} %collective-permute-done.1.refs_2_.refs_6_.own_got, ...), custom_call_target="tpu_custom_call" | custom-call | flops 167772160 | bytes 819200 | tf_op jit(solution)/shard_map/pallas_call | solution.py:414
  38.6 0.1 collective-permute-start.9
  38.6 3.0 %collective-permute-done.13 = f32[128,128]{1,0:T(8,128)S(1)} collective-permute-done((f32[128,128]{1,0:T(8,128)S(1)}, f32[128,128]{1,0:T(8,128)S(1)}, u32[]{:S(2)}, u32[]{:S(2)}) %collective-permute-start.13) | collective-permute-done | bytes 65568 | tf_op jit(solution)/shard_map/ppermute | solution.py:443
  41.7 0.6 %add_add_fusion = f32[128,128]{1,0:T(8,128)} fusion(f32[128,128]{1,0:T(8,128)S(1)} %collective-permute-done.13, f32[128,128]{1,0:T(8,128)S(1)} %collective-permute-done.14, f32[128,128]{1,0:T(8,128)S(1)} %maximum_select_fusion, f32[128,128]{1,0:T(8,128)S(1)} %collective-permute-done.12), kind=kLoop, calls=%fused_computation.2 | loop fusion | flops 49152 | bytes 327680 | tf_op jit(solution)/shard_map/add | solution.py:445
  42.4 0.1 constant_dynamic-update-slice_fusion.8
  42.5 0.1 constant_dynamic-update-slice_fusion.6
  42.7 1.1 %broadcast_select_fusion = bf16[2,2048,128]{2,1,0:T(8,128)(2,1)} fusion(bf16[2,2048,128]{2,1,0:T(8,128)(2,1)S(1)} %constant_dynamic-update-slice_fusion, bf16[2,2048,128]{2,1,0:T(8,128)(2,1)S(1)} %get-tuple-element.30, pred[]{:T(512)S(6)} %eq.7), kind=kLoop, calls=%fused_computation | loop fusion | flops 524288 | bytes 3145729 | tf_op jit(solution)/shard_map/jit(_where)/select_n | solution.py:431
  (29 shorter events, 0.3 us)
Async XLA Ops:
  0.6 5.8 %copy-start = (bf16[2,2048,128]{2,1,0:T(8,128)(2,1)S(1)}, bf16[2,2048,128]{2,1,0:T(8,128)(2,1)}, u32[]{:S(2)}) copy-start(bf16[2,2048,128]{2,1,0:T(8,128)(2,1)} %refs_4_.5) | copy-start | bytes 3145732
  0.6 5.7 %collective-permute-start.3 = (bf16[2,2048,128]{2,1,0:T(8,128)(2,1)}, bf16[2,2048,128]{2,1,0:T(8,128)(2,1)S(1)}, u32[]{:S(2)}, u32[]{:S(2)}) collective-permute-start(bf16[2,2048,128]{2,1,0:T(8,128)(2,1)} %refs_4_.5), channel_id=1, source_target_pairs={{0,8},{8,0},{16,24},{24,16},{1,9},{9,1},{17,25},{25,17},{2,10},{10... | collective-permute-start | bytes 3145736 | tf_op jit(solution)/shard_map/ppermute | solution.py:318
  1.2 7.4 %collective-permute-start.4 = (bf16[2,2048,128]{2,1,0:T(8,128)(2,1)}, bf16[2,2048,128]{2,1,0:T(8,128)(2,1)}, u32[]{:S(2)}, u32[]{:S(2)}) collective-permute-start(bf16[2,2048,128]{2,1,0:T(8,128)(2,1)} %own_input.3), channel_id=1, source_target_pairs={{0,8},{8,0},{16,24},{24,16},{1,9},{9,1},{17,25},{25,17},{2,10},{10... | collective-permute-start | bytes 3145736 | tf_op jit(solution)/shard_map/ppermute | solution.py:318
  1.2 25.0 %collective-permute-start = (bf16[128,128]{1,0:T(8,128)(2,1)}, bf16[128,128]{1,0:T(8,128)(2,1)S(1)}, u32[]{:S(2)}, u32[]{:S(2)}) collective-permute-start(bf16[128,128]{1,0:T(8,128)(2,1)} %refs_0_.5), channel_id=1, source_target_pairs={{0,8},{8,0},{16,24},{24,16},{1,9},{9,1},{17,25},{25,17},{2,10},{10... | collective-permute-start | bytes 98312 | tf_op jit(solution)/shard_map/ppermute | solution.py:318
  3.5 11.6 %collective-permute-start.1 = (bf16[2,544,128]{2,1,0:T(8,128)(2,1)}, bf16[2,544,128]{2,1,0:T(8,128)(2,1)S(1)}, u32[]{:S(2)}, u32[]{:S(2)}) collective-permute-start(bf16[2,544,128]{2,1,0:T(8,128)(2,1)} %get-tuple-element.15), channel_id=1, source_target_pairs={{0,16},{8,24},{16,0},{24,8},{1,17},{9,25},{17,1},{25,9},{2,18},{10... | collective-permute-start | bytes 835592 | tf_op jit(solution)/shard_map/ppermute | solution.py:326
  6.2 13.2 %collective-permute-start.2 = (bf16[2,544,128]{2,1,0:T(8,128)(2,1)}, bf16[2,544,128]{2,1,0:T(8,128)(2,1)S(1)}, u32[]{:S(2)}, u32[]{:S(2)}) collective-permute-start(bf16[2,544,128]{2,1,0:T(8,128)(2,1)} %get-tuple-element.16), channel_id=1, source_target_pairs={{0,24},{8,16},{16,8},{24,0},{1,25},{9,17},{17,9},{25,1},{2,26},{10... | collective-permute-start | bytes 835592 | tf_op jit(solution)/shard_map/ppermute | solution.py:326
  7.2 16.6 %collective-permute-start.5 = (bf16[4,192,128]{2,1,0:T(8,128)(2,1)}, bf16[4,192,128]{2,1,0:T(8,128)(2,1)S(1)}, u32[]{:S(2)}, u32[]{:S(2)}) collective-permute-start(bf16[4,192,128]{2,1,0:T(8,128)(2,1)} %get-tuple-element.18), channel_id=1, source_target_pairs={{16,0},{24,8},{17,1},{25,9},{18,2},{26,10},{19,3},{27,11},{20,4},{... | collective-permute-start | bytes 589832 | tf_op jit(solution)/shard_map/ppermute | solution.py:326
  8.5 1.2 %copy-start.1 = (bf16[2,2048,128]{2,1,0:T(8,128)(2,1)S(1)}, bf16[2,2048,128]{2,1,0:T(8,128)(2,1)}, u32[]{:S(2)}) copy-start(bf16[2,2048,128]{2,1,0:T(8,128)(2,1)} %own_input.3) | copy-start | bytes 3145732
  15.1 9.9 %copy-start.3 = (bf16[4,320,128]{2,1,0:T(8,128)(2,1)S(1)}, bf16[4,320,128]{2,1,0:T(8,128)(2,1)}, u32[]{:S(2)}) copy-start(bf16[4,320,128]{2,1,0:T(8,128)(2,1)} %get-tuple-element.21) | copy-start | bytes 983044
  23.8 2.4 %copy-start.2 = (bf16[128,128]{1,0:T(8,128)(2,1)S(1)}, bf16[128,128]{1,0:T(8,128)(2,1)}, u32[]{:S(2)}) copy-start(bf16[128,128]{1,0:T(8,128)(2,1)} %refs_0_.5) | copy-start | bytes 98308
  23.8 7.0 %collective-permute-start.10 = (f32[64,256]{1,0:T(8,128)S(1)}, f32[64,256]{1,0:T(8,128)S(1)}, u32[]{:S(2)}, u32[]{:S(2)}) collective-permute-start(f32[64,256]{1,0:T(8,128)S(1)} %constant_dynamic-slice_fusion.2), channel_id=1, source_target_pairs={{0,16},{8,24},{16,0},{24,8},{1,17},{9,25},{17,1},{25,9},{2,18},{10... | collective-permute-start | bytes 196616 | tf_op jit(solution)/shard_map/ppermute | solution.py:326
  25.0 11.6 %collective-permute-start.6 = (bf16[4,320,128]{2,1,0:T(8,128)(2,1)S(1)}, bf16[4,320,128]{2,1,0:T(8,128)(2,1)S(1)}, u32[]{:S(2)}, u32[]{:S(2)}) collective-permute-start(bf16[4,320,128]{2,1,0:T(8,128)(2,1)S(1)} %copy-done.3), channel_id=1, source_target_pairs={{16,0},{24,8},{17,1},{25,9},{18,2},{26,10},{19,3},{27,11},{20,4},{... | collective-permute-start | bytes 983048 | tf_op jit(solution)/shard_map/ppermute | solution.py:326
  28.8 2.1 %collective-permute-start.7 = (bf16[2,512,128]{2,1,0:T(8,128)(2,1)S(1)}, bf16[2,512,128]{2,1,0:T(8,128)(2,1)S(1)}, u32[]{:S(2)}, u32[]{:S(2)}) collective-permute-start(bf16[2,512,128]{2,1,0:T(8,128)(2,1)S(1)} %get-tuple-element.23), channel_id=1, source_target_pairs={{0,8},{8,0},{16,24},{24,16},{1,9},{9,1},{17,25},{25,17},{2,10},{10... | collective-permute-start | bytes 786440 | tf_op jit(solution)/shard_map/ppermute | solution.py:318
  30.2 6.3 %collective-permute-start.8 = (bf16[2,192,128]{2,1,0:T(8,128)(2,1)S(1)}, bf16[2,192,128]{2,1,0:T(8,128)(2,1)S(1)}, u32[]{:S(2)}, u32[]{:S(2)}) collective-permute-start(bf16[2,192,128]{2,1,0:T(8,128)(2,1)S(1)} %get-tuple-element.24), channel_id=1, source_target_pairs={{0,8},{8,0},{16,24},{24,16},{1,9},{9,1},{17,25},{25,17},{2,10},{10... | collective-permute-start | bytes 294920 | tf_op jit(solution)/shard_map/ppermute | solution.py:318
  30.8 1.3 %collective-permute-start.11 = (f32[64,128]{1,0:T(8,128)S(1)}, f32[64,128]{1,0:T(8,128)S(1)}, u32[]{:S(2)}, u32[]{:S(2)}) collective-permute-start(f32[64,128]{1,0:T(8,128)S(1)} %get-tuple-element.35), channel_id=1, source_target_pairs={{0,8},{8,0},{16,24},{24,16},{1,9},{9,1},{17,25},{25,17},{2,10},{10... | collective-permute-start | bytes 98312 | tf_op jit(solution)/shard_map/ppermute | solution.py:318
  32.1 6.5 %collective-permute-start.14 = (f32[128,128]{1,0:T(8,128)S(1)}, f32[128,128]{1,0:T(8,128)S(1)}, u32[]{:S(2)}, u32[]{:S(2)}) collective-permute-start(f32[128,128]{1,0:T(8,128)S(1)} %maximum_select_fusion), channel_id=1, source_target_pairs={{0,3},{1,2},{2,1},{3,0},{4,7},{5,6},{6,5},{7,4},{8,11},{9,10},{10,... | collective-permute-start | bytes 196616 | tf_op jit(solution)/shard_map/ppermute | solution.py:443
  35.8 5.9 %collective-permute-start.13 = (f32[128,128]{1,0:T(8,128)S(1)}, f32[128,128]{1,0:T(8,128)S(1)}, u32[]{:S(2)}, u32[]{:S(2)}) collective-permute-start(f32[128,128]{1,0:T(8,128)S(1)} %maximum_select_fusion), channel_id=1, source_target_pairs={{0,2},{1,3},{2,0},{3,1},{4,6},{5,7},{6,4},{7,5},{8,10},{9,11},{10,... | collective-permute-start | bytes 196616 | tf_op jit(solution)/shard_map/ppermute | solution.py:443
  35.8 5.9 %collective-permute-start.12 = (f32[128,128]{1,0:T(8,128)S(1)}, f32[128,128]{1,0:T(8,128)S(1)}, u32[]{:S(2)}, u32[]{:S(2)}) collective-permute-start(f32[128,128]{1,0:T(8,128)S(1)} %maximum_select_fusion), channel_id=1, source_target_pairs={{0,1},{1,0},{2,3},{3,2},{4,5},{5,4},{6,7},{7,6},{8,9},{9,8},{10,11... | collective-permute-start | bytes 196616 | tf_op jit(solution)/shard_map/ppermute | solution.py:443
  38.6 3.8 %collective-permute-start.9 = (bf16[2,320,128]{2,1,0:T(8,128)(2,1)S(1)}, bf16[2,320,128]{2,1,0:T(8,128)(2,1)S(1)}, u32[]{:S(2)}, u32[]{:S(2)}) collective-permute-start(bf16[2,320,128]{2,1,0:T(8,128)(2,1)S(1)} %get-tuple-element.25), channel_id=1, source_target_pairs={{0,8},{8,0},{16,24},{24,16},{1,9},{9,1},{17,25},{25,17},{2,10},{10... | collective-permute-start | bytes 491528 | tf_op jit(solution)/shard_map/ppermute | solution.py:318

commit v4 on v3

--- a/solution.py
+++ b/solution.py
@@ -11,10 +11,9 @@
 CORES = 2
 VMEM_BYTES = 16 << 20
 UNROLL = 16
-OWN_WEIGHT = 100
-EARLY = 12
-C1 = True
-C2 = True
+EARLY = 14
+PART_WEIGHT = 32
+OWN_WEIGHT = 1000
 
 
 def pick(condition, first, second):
@@ -27,8 +26,8 @@
     return ref[:, pl.ds(start, GROUP_SIZE), :].reshape(sequences * GROUP_SIZE, positions)
 
 
-def chunked(groups, body):
-    count = max(size for size in range(1, UNROLL + 1) if groups % size == 0)
+def chunked(groups, body, most=UNROLL):
+    count = max(size for size in range(1, most + 1) if groups % size == 0)
 
     def chunk(number, carry):
         body(number * count, count)
@@ -213,7 +212,7 @@
             where = (pl.ds(part_group + first + index, 1), pl.ds(first_lag, 2 * CORES * positions))
             out[where] = out[where] + lag_sums(values, pairs, None, positions)
 
-    chunked(part // GROUP_SIZE, body)
+    chunked(part // GROUP_SIZE, body, 2 * UNROLL)
 
 
 def assemble_kernel(out_place, *refs):
@@ -328,9 +327,6 @@
     in_hbm = pl.BlockSpec(memory_space=pltpu.HBM)
     params = pltpu.CompilerParams(vmem_limit_bytes=VMEM_BYTES)
 
-    filters_peer = swap_cores(filters)
-    grad_peer, input_peer = swap_cores(output_grad), swap_cores(inputs)
-
     heights = [part + slot_rows] * (CORES * (chips - 1))
     outgoing = pl.pallas_call(
         functools.partial(parts_kernel, chips, slot_rows),
@@ -341,21 +337,23 @@
         + [pltpu.SemaphoreType.DMA((len(heights),))] * 2,
     )(inputs, output_grad, filters)
 
+    to_swap = (filters, output_grad, inputs)
+    filters_peer, grad_peer, input_peer = (swap_cores(value) for value in to_swap)
     first = {
         k: [from_chip(outgoing[CORES * (k - 1) + other], k, True, other) for other in range(CORES)]
         for k in rounds
     }
 
     in_smem, in_vmem = pl.BlockSpec(memory_space=pltpu.SMEM), pl.BlockSpec(memory_space=pltpu.VMEM)
-    flip_scratch = pltpu.VMEM((CORES, sequences, UNROLL * GROUP_SIZE, positions), jnp.bfloat16)
+    flip_scratch = pltpu.VMEM((CORES, sequences, 2 * UNROLL * GROUP_SIZE, positions), jnp.bfloat16)
 
     def vmem(value):
         return pltpu.with_memory_space_constraint(value, pltpu.VMEM)
 
     def cost(group_count, depth, width, arrays):
         return pl.CostEstimate(
-            flops=2 * group_count * depth * positions * width,
-            bytes_accessed=arrays * group_count * rows * positions * 2,
+            flops=max(1, int(2 * group_count * depth * positions * width)),
+            bytes_accessed=max(1, int(arrays * group_count * rows * positions * 2)),
             transcendentals=0,
         )
 
@@ -374,7 +372,7 @@
         ],
         scratch_shapes=[pltpu.SemaphoreType.DMA((CORES * len(sizes),))],
     )(grad_here, grad_peer)
-    second = [{k: [from_chip(value, k, False)] for k in rounds} for value in outgoing]
+    second = [{k: [from_chip(outgoing[0], k, False)] for k in rounds}]
 
     lags = pl.pallas_call(
         own_lags_kernel,
@@ -397,9 +395,8 @@
             compiler_params=params,
         )(place, *both, *[vmem(ref) for ref in first[k]], vmem(lags))
 
-    if C1:
-        for k in rounds:
-            lags, second[0][k][0] = lax.optimization_barrier((lags, second[0][k][0]))
+    for k in rounds:
+        lags, second[0][k][0] = lax.optimization_barrier((lags, second[0][k][0]))
 
     def chip_lags(which):
         return lax.dynamic_slice_in_dim(lags, which * CORES * positions, CORES * positions, 1)
@@ -407,6 +404,7 @@
     sums = chip_lags(chip)
     for k in rounds:
         sums = sums + from_chip(chip_lags((chip - k) % chips), k, True)
+
     def input_part(which, offset, count, received):
         come = [ref for k in rounds for ref in first[k]]
         arrays = [ref for k in rounds for ref in received[k]]
@@ -417,23 +415,25 @@
             out_specs=[in_vmem] * 2,
             out_shape=[jax.ShapeDtypeStruct((sequences, count * GROUP_SIZE, positions), jnp.bfloat16)] * 2,
             scratch_shapes=[pltpu.VMEM((groups, length), jnp.float32)],
-            cost_estimate=cost(count, CORES * rows, length, 4 + len(arrays)),
+            cost_estimate=cost(count if which and offset else PART_WEIGHT, CORES * rows, length, 4 + len(arrays)),
             compiler_params=params,
         )(place, *[vmem(value) for value in values])
 
+    second.append({k: [from_chip(outgoing[1], k, False)] for k in rounds})
+    for k in rounds:
+        second[1][k][0], second[0][k][0] = lax.optimization_barrier((second[1][k][0], second[0][k][0]))
     results = [
         input_part(0, 0, part_groups, first),
         input_part(1, 0, sizes[0], second[0]),
         input_part(1, sizes[0], sizes[1], second[1]),
     ]
+    sums, _ = lax.optimization_barrier((sums, results[0][0]))
     mine = jnp.concatenate([result[0] for result in results], axis=1)
     got = jnp.concatenate([swap_cores(result[1]) for result in results], axis=1)
     input_grad = jnp.where(
         core == 0, jnp.concatenate([mine, got], axis=1), jnp.concatenate([got, mine], axis=1)
     )
 
-    if C2:
-        sums, _ = lax.optimization_barrier((sums, results[0][0]))
     keep = lax.dynamic_slice_in_dim(sums, core * positions, positions, 1)
     got = swap_cores(lax.dynamic_slice_in_dim(sums, (1 - core) * positions, positions, 1))
     own = jnp.where(core == 0, jnp.concatenate([keep, got], axis=0), jnp.concatenate([got, keep], axis=0))

time: 44 us -> 43.6 us (level)
  Pallas kernels: 17.7 us -> 19.2 us
  local copies, waits for them, and re-layouts: 1.58 us -> 0.36 us
  starting transfers between devices: 12.8 us -> 12.1 us
    ppermute x3, waiting for transfers between devices: 3.04 us -> 0.01 us  [per_device(): terms.append(lax.ppermute(own, 'dp', [(i, i ^ k) for i in range(copies)]))]
    ppermute x5, waiting for transfers between devices: 4.77 us -> 7.4 us  [from_chip(): return lax.ppermute(value, 'seq', pairs)]
    pallas_call x3, Pallas kernels: 5.81 us -> 7.57 us  [input_part(): pl.pallas_call(functools.partial(input_grad_kernel, chips, which, offset,...]
    unnamed x15 -> x13, local copies, waits for them, and re-layouts: 1.47 us -> 0.26 us
    ppermute x5, starting transfers between devices: 6.49 us -> 5.59 us  [from_chip(): return lax.ppermute(value, 'seq', pairs)]
  transfers between devices with their start and end apart: 15 -> 15, of which waited for: 4 -> 6; matrix products, arithmetic and copies ran while one was open for 2% -> 2% of each run, Pallas kernels for 41% -> 44%
where the time goes in v4:
time: 43.6 us; the launch traced here: 43.3 us
  Pallas kernels  19.2 us (44%)
  starting transfers between devices  12.1 us (28%)
  waiting for transfers between devices  8.9 us (20%)
  other arithmetic  1.82 us (4%)
  between operations  0.84 us (2%)
    pallas_call x3, Pallas kernels, input_part(): pl.pallas_call(functools.partial(input_grad_kernel, chips, which, offset,...  7.57 us
    ppermute x5, waiting for transfers between devices, from_chip(): return lax.ppermute(value, 'seq', pairs)  7.4 us
    ppermute x5, starting transfers between devices, from_chip(): return lax.ppermute(value, 'seq', pairs)  5.59 us
    pallas_call x1, Pallas kernels, per_device(): pl.pallas_call(own_lags_kernel, in_specs=[in_smem] + [in_vmem] * 4, out_s...  5.34 us
    ppermute x3, starting transfers between devices, per_device(): terms.append(lax.ppermute(own, 'dp', [(i, i ^ k) for i in range(copies)]))  4.52 us
    pallas_call x1, Pallas kernels, per_device(): pl.pallas_call(functools.partial(round_lags_kernel, chips, k), in_specs=[...  3.66 us
    ppermute x7, starting transfers between devices, swap_cores(): return lax.ppermute(value, 'seq', [(i, i ^ 1) for i in range(shard_count)])  1.99 us
    pallas_call x1, Pallas kernels, per_device(): pl.pallas_call(functools.partial(parts_kernel, chips, slot_rows), in_spec...  1.84 us
  transfers between devices with their start and end apart: 15, of which 6 were waited for; matrix products, arithmetic and copies ran while one was open for 2% of the time, Pallas kernels for 44%

profile of v4, /device:TPU:0, one launch (start us, length us, event | category | flops | bytes accessed | tf_op | source)
XLA Modules:
  0.0 43.3 jit_solution(3037594038105282955)
XLA Ops:
  0.6 0.5 %collective-permute-start.3 = (bf16[2,2048,128]{2,1,0:T(8,128)(2,1)}, bf16[2,2048,128]{2,1,0:T(8,128)(2,1)S(1)}, u32[]{:S(2)}, u32[]{:S(2)}) collective-permute-start(bf16[2,2048,128]{2,1,0:T(8,128)(2,1)} %refs_4_.5), channel_id=1, source_target_pairs={{0,8},{8,0},{16,24},{24,16},{1,9},{9,1},{17,25},{25,17},{2,10},{10... | collective-permute-start | bytes 3145736 | tf_op jit(solution)/shard_map/ppermute | solution.py:317
  1.2 0.1 collective-permute-start.5
  1.2 1.8 %shard_map.50 = (bf16[2,544,128]{2,1,0:T(8,128)(2,1)}, bf16[2,544,128]{2,1,0:T(8,128)(2,1)}) custom-call(bf16[2,2048,128]{2,1,0:T(8,128)(2,1)} %own_input.3, bf16[2,2048,128]{2,1,0:T(8,128)(2,1)} %refs_4_.5, bf16[128,128]{1,0:T(8,128)(2,1)} %refs_0_.5), custom_call_target="tpu_custom_call" | custom-call | tf_op jit(solution)/shard_map/pallas_call | solution.py:331
  3.1 3.0 %collective-permute-start.1 = (bf16[2,544,128]{2,1,0:T(8,128)(2,1)}, bf16[2,544,128]{2,1,0:T(8,128)(2,1)}, u32[]{:S(2)}, u32[]{:S(2)}) collective-permute-start(bf16[2,544,128]{2,1,0:T(8,128)(2,1)} %get-tuple-element.17), channel_id=1, source_target_pairs={{0,16},{8,24},{16,0},{24,8},{1,17},{9,25},{17,1},{25,9},{2,18},{10... | collective-permute-start | bytes 835592 | tf_op jit(solution)/shard_map/ppermute | solution.py:325
  6.1 0.1 pad_add_fusion.place
  6.2 0.0 collective-permute-done.3.refs_5_.peer_grad
  6.2 0.8 %shard_map.52 = (bf16[4,224,128]{2,1,0:T(8,128)(2,1)}, bf16[4,288,128]{2,1,0:T(8,128)(2,1)}) custom-call(bf16[2,2048,128]{2,1,0:T(8,128)(2,1)S(1)} %copy-done, bf16[2,2048,128]{2,1,0:T(8,128)(2,1)S(1)} %collective-permute-done.3.refs_5_.peer_grad), custom_call_target="tpu_custom_call" | custom-call | tf_op jit(solution)/shard_map/pallas_call | solution.py:366
  7.0 1.3 %collective-permute-start.6 = (bf16[4,224,128]{2,1,0:T(8,128)(2,1)}, bf16[4,224,128]{2,1,0:T(8,128)(2,1)}, u32[]{:S(2)}, u32[]{:S(2)}) collective-permute-start(bf16[4,224,128]{2,1,0:T(8,128)(2,1)} %get-tuple-element.21), channel_id=1, source_target_pairs={{16,0},{24,8},{17,1},{25,9},{18,2},{26,10},{19,3},{27,11},{20,4},{... | collective-permute-start | bytes 688136 | tf_op jit(solution)/shard_map/ppermute | solution.py:325
  8.3 5.3 %shard_map.53.running = f32[64,512]{1,0:T(8,128)S(1)} custom-call(s32[2]{0:T(128)S(1)} %pad_add_fusion.place, bf16[2,2048,128]{2,1,0:T(8,128)(2,1)S(1)} %copy-done.1, bf16[2,2048,128]{2,1,0:T(8,128)(2,1)} %collective-permute-done.5.peer_input, bf16[2,2048,128]{2,1,0:T(8,128)(2,1)S(1)} %copy-done, ...), custom_call_target="tpu_custom_call" | custom-call | flops 268435456000 | bytes 2097152000 | tf_op jit(solution)/shard_map/pallas_call | solution.py:377
  13.7 0.2 collective-permute-done.1.refs_2_.refs_6_.own_got
  13.9 4.9 %collective-permute-done.2.refs_3_.refs_7_.peer_got = bf16[2,544,128]{2,1,0:T(8,128)(2,1)} collective-permute-done((bf16[2,544,128]{2,1,0:T(8,128)(2,1)}, bf16[2,544,128]{2,1,0:T(8,128)(2,1)}, u32[]{:S(2)}, u32[]{:S(2)}) %collective-permute-start.2) | collective-permute-done | bytes 278560 | tf_op jit(solution)/shard_map/ppermute | solution.py:325
  18.7 3.7 %shard_map.54 = f32[64,512]{1,0:T(8,128)S(1)} custom-call(s32[2]{0:T(128)S(1)} %pad_add_fusion.place, bf16[2,2048,128]{2,1,0:T(8,128)(2,1)S(1)} %copy-done.1, bf16[2,2048,128]{2,1,0:T(8,128)(2,1)} %collective-permute-done.5.peer_input, bf16[2,2048,128]{2,1,0:T(8,128)(2,1)S(1)} %copy-done, bf16[2,2048,128]{2,1,0:T(8,128)(2,1)S(1)} %collective-permute-done.3.refs_5_.peer_grad, ...), custom_call_target="tpu_custom_call" | custom-call | flops 201326592 | bytes 1572864 | tf_op jit(solution)/shard_map/pallas_call | solution.py:388
  22.4 0.0 copy-start.2
  22.4 1.8 %collective-permute-done.6.refs_6_ = bf16[4,224,128]{2,1,0:T(8,128)(2,1)} collective-permute-done((bf16[4,224,128]{2,1,0:T(8,128)(2,1)}, bf16[4,224,128]{2,1,0:T(8,128)(2,1)}, u32[]{:S(2)}, u32[]{:S(2)}) %collective-permute-start.6) | collective-permute-done | bytes 229408 | tf_op jit(solution)/shard_map/ppermute | solution.py:325
  24.2 0.1 collective-permute-start
  24.3 1.3 %collective-permute-start.4 = (bf16[4,288,128]{2,1,0:T(8,128)(2,1)}, bf16[4,288,128]{2,1,0:T(8,128)(2,1)S(1)}, u32[]{:S(2)}, u32[]{:S(2)}) collective-permute-start(bf16[4,288,128]{2,1,0:T(8,128)(2,1)} %get-tuple-element.20), channel_id=1, source_target_pairs={{16,0},{24,8},{17,1},{25,9},{18,2},{26,10},{19,3},{27,11},{20,4},{... | collective-permute-start | bytes 884744 | tf_op jit(solution)/shard_map/ppermute | solution.py:325
  25.6 3.2 %shard_map.51 = (bf16[2,512,128]{2,1,0:T(8,128)(2,1)S(1)}, bf16[2,512,128]{2,1,0:T(8,128)(2,1)S(1)}) custom-call(s32[2]{0:T(128)S(1)} %pad_add_fusion.place, bf16[128,128]{1,0:T(8,128)(2,1)S(1)} %copy-done.2, bf16[128,128]{1,0:T(8,128)(2,1)S(1)} %collective-permute-done.refs_1_, bf16[2,544,128]{2,1,0:T(8,128)(2,1)} %collective-permute-done.1.refs_2_.refs_6_.own_got, ...), custom_call_target="tpu_custom_call" | custom-call | flops 268435456 | bytes 1572864 | tf_op jit(solution)/shard_map/pallas_call | solution.py:412
  28.8 0.5 %collective-permute-start.7 = (bf16[2,512,128]{2,1,0:T(8,128)(2,1)S(1)}, bf16[2,512,128]{2,1,0:T(8,128)(2,1)S(1)}, u32[]{:S(2)}, u32[]{:S(2)}) collective-permute-start(bf16[2,512,128]{2,1,0:T(8,128)(2,1)S(1)} %get-tuple-element.27), channel_id=1, source_target_pairs={{0,8},{8,0},{16,24},{24,16},{1,9},{9,1},{17,25},{25,17},{2,10},{10... | collective-permute-start | bytes 786440 | tf_op jit(solution)/shard_map/ppermute | solution.py:317
  29.4 0.1 collective-permute-start.11
  29.5 1.2 %collective-permute-done.11 = f32[64,128]{1,0:T(8,128)S(1)} collective-permute-done((f32[64,128]{1,0:T(8,128)S(1)}, f32[64,128]{1,0:T(8,128)S(1)}, u32[]{:S(2)}, u32[]{:S(2)}) %collective-permute-start.11) | collective-permute-done | bytes 32800 | tf_op jit(solution)/shard_map/ppermute | solution.py:317
  30.7 3.9 %collective-permute-start.14 = (f32[128,128]{1,0:T(8,128)S(1)}, f32[128,128]{1,0:T(8,128)S(1)}, u32[]{:S(2)}, u32[]{:S(2)}) collective-permute-start(f32[128,128]{1,0:T(8,128)S(1)} %maximum_select_fusion), channel_id=1, source_target_pairs={{0,3},{1,2},{2,1},{3,0},{4,7},{5,6},{6,5},{7,4},{8,11},{9,10},{10,... | collective-permute-start | bytes 196616 | tf_op jit(solution)/shard_map/ppermute | solution.py:443
  34.6 0.6 %collective-permute-start.12 = (f32[128,128]{1,0:T(8,128)S(1)}, f32[128,128]{1,0:T(8,128)S(1)}, u32[]{:S(2)}, u32[]{:S(2)}) collective-permute-start(f32[128,128]{1,0:T(8,128)S(1)} %maximum_select_fusion), channel_id=1, source_target_pairs={{0,1},{1,0},{2,3},{3,2},{4,5},{5,4},{6,7},{7,6},{8,9},{9,8},{10,11... | collective-permute-start | bytes 196616 | tf_op jit(solution)/shard_map/ppermute | solution.py:443
  35.2 0.6 %collective-permute-done.4.refs_6_ = bf16[4,288,128]{2,1,0:T(8,128)(2,1)S(1)} collective-permute-done((bf16[4,288,128]{2,1,0:T(8,128)(2,1)}, bf16[4,288,128]{2,1,0:T(8,128)(2,1)S(1)}, u32[]{:S(2)}, u32[]{:S(2)}) %collective-permute-start.4) | collective-permute-done | bytes 294944 | tf_op jit(solution)/shard_map/ppermute | solution.py:325
  35.8 2.0 %shard_map.55 = (bf16[2,224,128]{2,1,0:T(8,128)(2,1)S(1)}, bf16[2,224,128]{2,1,0:T(8,128)(2,1)S(1)}) custom-call(s32[2]{0:T(128)S(1)} %pad_add_fusion.place, bf16[128,128]{1,0:T(8,128)(2,1)S(1)} %copy-done.2, bf16[128,128]{1,0:T(8,128)(2,1)S(1)} %collective-permute-done.refs_1_, bf16[2,544,128]{2,1,0:T(8,128)(2,1)} %collective-permute-done.1.refs_2_.refs_6_.own_got, ...), custom_call_target="tpu_custom_call" | custom-call | flops 268435456 | bytes 1310720 | tf_op jit(solution)/shard_map/pallas_call | solution.py:412
  37.8 0.1 collective-permute-start.8
  37.9 2.4 %shard_map.56 = (bf16[2,288,128]{2,1,0:T(8,128)(2,1)S(1)}, bf16[2,288,128]{2,1,0:T(8,128)(2,1)S(1)}) custom-call(s32[2]{0:T(128)S(1)} %pad_add_fusion.place, bf16[128,128]{1,0:T(8,128)(2,1)S(1)} %copy-done.2, bf16[128,128]{1,0:T(8,128)(2,1)S(1)} %collective-permute-done.refs_1_, bf16[2,544,128]{2,1,0:T(8,128)(2,1)} %collective-permute-done.1.refs_2_.refs_6_.own_got, ...), custom_call_target="tpu_custom_call" | custom-call | flops 150994944 | bytes 737280 | tf_op jit(solution)/shard_map/pallas_call | solution.py:412
  40.3 0.6 %collective-permute-start.9 = (bf16[2,288,128]{2,1,0:T(8,128)(2,1)S(1)}, bf16[2,288,128]{2,1,0:T(8,128)(2,1)S(1)}, u32[]{:S(2)}, u32[]{:S(2)}) collective-permute-start(bf16[2,288,128]{2,1,0:T(8,128)(2,1)S(1)} %get-tuple-element.29), channel_id=1, source_target_pairs={{0,8},{8,0},{16,24},{24,16},{1,9},{9,1},{17,25},{25,17},{2,10},{10... | collective-permute-start | bytes 442376 | tf_op jit(solution)/shard_map/ppermute | solution.py:317
  40.8 0.6 %add_add_fusion = f32[128,128]{1,0:T(8,128)} fusion(f32[128,128]{1,0:T(8,128)S(1)} %collective-permute-done.13, f32[128,128]{1,0:T(8,128)S(1)} %collective-permute-done.14, f32[128,128]{1,0:T(8,128)S(1)} %maximum_select_fusion, f32[128,128]{1,0:T(8,128)S(1)} %collective-permute-done.12), kind=kLoop, calls=%fused_computation.2 | loop fusion | flops 49152 | bytes 327680 | tf_op jit(solution)/shard_map/add | solution.py:445
  41.5 0.3 collective-permute-done.9
  41.9 0.1 constant_dynamic-update-slice_fusion.8
  42.0 0.1 constant_dynamic-update-slice_fusion.6
  42.2 1.1 %broadcast_select_fusion = bf16[2,2048,128]{2,1,0:T(8,128)(2,1)} fusion(bf16[2,2048,128]{2,1,0:T(8,128)(2,1)S(1)} %constant_dynamic-update-slice_fusion, bf16[2,2048,128]{2,1,0:T(8,128)(2,1)S(1)} %get-tuple-element.34, pred[]{:T(512)S(6)} %eq.7), kind=kLoop, calls=%fused_computation | loop fusion | flops 524288 | bytes 3145729 | tf_op jit(solution)/shard_map/jit(_where)/select_n | solution.py:433
  (27 shorter events, 0.3 us)
Async XLA Ops:
  0.6 5.5 %copy-start = (bf16[2,2048,128]{2,1,0:T(8,128)(2,1)S(1)}, bf16[2,2048,128]{2,1,0:T(8,128)(2,1)}, u32[]{:S(2)}) copy-start(bf16[2,2048,128]{2,1,0:T(8,128)(2,1)} %refs_4_.5) | copy-start | bytes 3145732
  0.6 5.5 %collective-permute-start.3 = (bf16[2,2048,128]{2,1,0:T(8,128)(2,1)}, bf16[2,2048,128]{2,1,0:T(8,128)(2,1)S(1)}, u32[]{:S(2)}, u32[]{:S(2)}) collective-permute-start(bf16[2,2048,128]{2,1,0:T(8,128)(2,1)} %refs_4_.5), channel_id=1, source_target_pairs={{0,8},{8,0},{16,24},{24,16},{1,9},{9,1},{17,25},{25,17},{2,10},{10... | collective-permute-start | bytes 3145736 | tf_op jit(solution)/shard_map/ppermute | solution.py:317
  1.2 7.2 %collective-permute-start.5 = (bf16[2,2048,128]{2,1,0:T(8,128)(2,1)}, bf16[2,2048,128]{2,1,0:T(8,128)(2,1)}, u32[]{:S(2)}, u32[]{:S(2)}) collective-permute-start(bf16[2,2048,128]{2,1,0:T(8,128)(2,1)} %own_input.3), channel_id=1, source_target_pairs={{0,8},{8,0},{16,24},{24,16},{1,9},{9,1},{17,25},{25,17},{2,10},{10... | collective-permute-start | bytes 3145736 | tf_op jit(solution)/shard_map/ppermute | solution.py:317
  3.1 10.8 %collective-permute-start.1 = (bf16[2,544,128]{2,1,0:T(8,128)(2,1)}, bf16[2,544,128]{2,1,0:T(8,128)(2,1)}, u32[]{:S(2)}, u32[]{:S(2)}) collective-permute-start(bf16[2,544,128]{2,1,0:T(8,128)(2,1)} %get-tuple-element.17), channel_id=1, source_target_pairs={{0,16},{8,24},{16,0},{24,8},{1,17},{9,25},{17,1},{25,9},{2,18},{10... | collective-permute-start | bytes 835592 | tf_op jit(solution)/shard_map/ppermute | solution.py:325
  6.1 12.6 %collective-permute-start.2 = (bf16[2,544,128]{2,1,0:T(8,128)(2,1)}, bf16[2,544,128]{2,1,0:T(8,128)(2,1)}, u32[]{:S(2)}, u32[]{:S(2)}) collective-permute-start(bf16[2,544,128]{2,1,0:T(8,128)(2,1)} %get-tuple-element.18), channel_id=1, source_target_pairs={{0,24},{8,16},{16,8},{24,0},{1,25},{9,17},{17,9},{25,1},{2,26},{10... | collective-permute-start | bytes 835592 | tf_op jit(solution)/shard_map/ppermute | solution.py:325
  6.2 2.2 %copy-start.1 = (bf16[2,2048,128]{2,1,0:T(8,128)(2,1)S(1)}, bf16[2,2048,128]{2,1,0:T(8,128)(2,1)}, u32[]{:S(2)}) copy-start(bf16[2,2048,128]{2,1,0:T(8,128)(2,1)} %own_input.3) | copy-start | bytes 3145732
  7.0 17.2 %collective-permute-start.6 = (bf16[4,224,128]{2,1,0:T(8,128)(2,1)}, bf16[4,224,128]{2,1,0:T(8,128)(2,1)}, u32[]{:S(2)}, u32[]{:S(2)}) collective-permute-start(bf16[4,224,128]{2,1,0:T(8,128)(2,1)} %get-tuple-element.21), channel_id=1, source_target_pairs={{16,0},{24,8},{17,1},{25,9},{18,2},{26,10},{19,3},{27,11},{20,4},{... | collective-permute-start | bytes 688136 | tf_op jit(solution)/shard_map/ppermute | solution.py:325
  22.4 1.8 %copy-start.2 = (bf16[128,128]{1,0:T(8,128)(2,1)S(1)}, bf16[128,128]{1,0:T(8,128)(2,1)}, u32[]{:S(2)}) copy-start(bf16[128,128]{1,0:T(8,128)(2,1)} %refs_0_.5) | copy-start | bytes 98308
  24.2 5.2 %collective-permute-start.10 = (f32[64,256]{1,0:T(8,128)S(1)}, f32[64,256]{1,0:T(8,128)S(1)}, u32[]{:S(2)}, u32[]{:S(2)}) collective-permute-start(f32[64,256]{1,0:T(8,128)S(1)} %constant_dynamic-slice_fusion.2), channel_id=1, source_target_pairs={{0,16},{8,24},{16,0},{24,8},{1,17},{9,25},{17,1},{25,9},{2,18},{10... | collective-permute-start | bytes 196616 | tf_op jit(solution)/shard_map/ppermute | solution.py:325
  24.2 1.4 %collective-permute-start = (bf16[128,128]{1,0:T(8,128)(2,1)S(1)}, bf16[128,128]{1,0:T(8,128)(2,1)S(1)}, u32[]{:S(2)}, u32[]{:S(2)}) collective-permute-start(bf16[128,128]{1,0:T(8,128)(2,1)S(1)} %copy-done.2), channel_id=1, source_target_pairs={{0,8},{8,0},{16,24},{24,16},{1,9},{9,1},{17,25},{25,17},{2,10},{10... | collective-permute-start | bytes 98312 | tf_op jit(solution)/shard_map/ppermute | solution.py:317
  24.3 11.5 %collective-permute-start.4 = (bf16[4,288,128]{2,1,0:T(8,128)(2,1)}, bf16[4,288,128]{2,1,0:T(8,128)(2,1)S(1)}, u32[]{:S(2)}, u32[]{:S(2)}) collective-permute-start(bf16[4,288,128]{2,1,0:T(8,128)(2,1)} %get-tuple-element.20), channel_id=1, source_target_pairs={{16,0},{24,8},{17,1},{25,9},{18,2},{26,10},{19,3},{27,11},{20,4},{... | collective-permute-start | bytes 884744 | tf_op jit(solution)/shard_map/ppermute | solution.py:325
  28.8 6.4 %collective-permute-start.7 = (bf16[2,512,128]{2,1,0:T(8,128)(2,1)S(1)}, bf16[2,512,128]{2,1,0:T(8,128)(2,1)S(1)}, u32[]{:S(2)}, u32[]{:S(2)}) collective-permute-start(bf16[2,512,128]{2,1,0:T(8,128)(2,1)S(1)} %get-tuple-element.27), channel_id=1, source_target_pairs={{0,8},{8,0},{16,24},{24,16},{1,9},{9,1},{17,25},{25,17},{2,10},{10... | collective-permute-start | bytes 786440 | tf_op jit(solution)/shard_map/ppermute | solution.py:317
  29.4 1.3 %collective-permute-start.11 = (f32[64,128]{1,0:T(8,128)S(1)}, f32[64,128]{1,0:T(8,128)S(1)}, u32[]{:S(2)}, u32[]{:S(2)}) collective-permute-start(f32[64,128]{1,0:T(8,128)S(1)} %get-tuple-element.39), channel_id=1, source_target_pairs={{0,8},{8,0},{16,24},{24,16},{1,9},{9,1},{17,25},{25,17},{2,10},{10... | collective-permute-start | bytes 98312 | tf_op jit(solution)/shard_map/ppermute | solution.py:317
  30.7 10.1 %collective-permute-start.14 = (f32[128,128]{1,0:T(8,128)S(1)}, f32[128,128]{1,0:T(8,128)S(1)}, u32[]{:S(2)}, u32[]{:S(2)}) collective-permute-start(f32[128,128]{1,0:T(8,128)S(1)} %maximum_select_fusion), channel_id=1, source_target_pairs={{0,3},{1,2},{2,1},{3,0},{4,7},{5,6},{6,5},{7,4},{8,11},{9,10},{10,... | collective-permute-start | bytes 196616 | tf_op jit(solution)/shard_map/ppermute | solution.py:443
  34.6 6.3 %collective-permute-start.13 = (f32[128,128]{1,0:T(8,128)S(1)}, f32[128,128]{1,0:T(8,128)S(1)}, u32[]{:S(2)}, u32[]{:S(2)}) collective-permute-start(f32[128,128]{1,0:T(8,128)S(1)} %maximum_select_fusion), channel_id=1, source_target_pairs={{0,2},{1,3},{2,0},{3,1},{4,6},{5,7},{6,4},{7,5},{8,10},{9,11},{10,... | collective-permute-start | bytes 196616 | tf_op jit(solution)/shard_map/ppermute | solution.py:443
  34.6 6.3 %collective-permute-start.12 = (f32[128,128]{1,0:T(8,128)S(1)}, f32[128,128]{1,0:T(8,128)S(1)}, u32[]{:S(2)}, u32[]{:S(2)}) collective-permute-start(f32[128,128]{1,0:T(8,128)S(1)} %maximum_select_fusion), channel_id=1, source_target_pairs={{0,1},{1,0},{2,3},{3,2},{4,5},{5,4},{6,7},{7,6},{8,9},{9,8},{10,11... | collective-permute-start | bytes 196616 | tf_op jit(solution)/shard_map/ppermute | solution.py:443
  37.8 3.7 %collective-permute-start.8 = (bf16[2,224,128]{2,1,0:T(8,128)(2,1)S(1)}, bf16[2,224,128]{2,1,0:T(8,128)(2,1)S(1)}, u32[]{:S(2)}, u32[]{:S(2)}) collective-permute-start(bf16[2,224,128]{2,1,0:T(8,128)(2,1)S(1)} %get-tuple-element.28), channel_id=1, source_target_pairs={{0,8},{8,0},{16,24},{24,16},{1,9},{9,1},{17,25},{25,17},{2,10},{10... | collective-permute-start | bytes 344072 | tf_op jit(solution)/shard_map/ppermute | solution.py:317
  40.3 1.6 %collective-permute-start.9 = (bf16[2,288,128]{2,1,0:T(8,128)(2,1)S(1)}, bf16[2,288,128]{2,1,0:T(8,128)(2,1)S(1)}, u32[]{:S(2)}, u32[]{:S(2)}) collective-permute-start(bf16[2,288,128]{2,1,0:T(8,128)(2,1)S(1)} %get-tuple-element.29), channel_id=1, source_target_pairs={{0,8},{8,0},{16,24},{24,16},{1,9},{9,1},{17,25},{25,17},{2,10},{10... | collective-permute-start | bytes 442376 | tf_op jit(solution)/shard_map/ppermute | solution.py:317

commit v5 on v4

--- a/solution.py
+++ b/solution.py
@@ -100,7 +100,7 @@
         for index in range(count):
             one_group(first + index)
 
-    chunked(groups, body)
+    chunked(groups, body, 2 * UNROLL)
 
 
 def reversal(positions):

time: 43.6 us -> 43.4 us (level)
  no operation moved by 1% of the time
where the time goes in v5:
time: 43.4 us; the launch traced here: 43.1 us
  Pallas kernels  18.9 us (44%)
  starting transfers between devices  12.1 us (28%)
  waiting for transfers between devices  9.09 us (21%)
  other arithmetic  1.82 us (4%)
  between operations  0.83 us (2%)
    ppermute x5, waiting for transfers between devices, from_chip(): return lax.ppermute(value, 'seq', pairs)  7.59 us
    pallas_call x3, Pallas kernels, input_part(): pl.pallas_call(functools.partial(input_grad_kernel, chips, which, offset,...  7.18 us
    ppermute x5, starting transfers between devices, from_chip(): return lax.ppermute(value, 'seq', pairs)  5.59 us
    pallas_call x1, Pallas kernels, per_device(): pl.pallas_call(own_lags_kernel, in_specs=[in_smem] + [in_vmem] * 4, out_s...  5.34 us
    ppermute x3, starting transfers between devices, per_device(): terms.append(lax.ppermute(own, 'dp', [(i, i ^ k) for i in range(copies)]))  4.53 us
    pallas_call x1, Pallas kernels, per_device(): pl.pallas_call(functools.partial(round_lags_kernel, chips, k), in_specs=[...  3.66 us
    ppermute x7, starting transfers between devices, swap_cores(): return lax.ppermute(value, 'seq', [(i, i ^ 1) for i in range(shard_count)])  1.99 us
    pallas_call x1, Pallas kernels, per_device(): pl.pallas_call(functools.partial(parts_kernel, chips, slot_rows), in_spec...  1.84 us
  transfers between devices with their start and end apart: 15, of which 6 were waited for; matrix products, arithmetic and copies ran while one was open for 2% of the time, Pallas kernels for 44%

profile of v5, /device:TPU:0, one launch (start us, length us, event | category | flops | bytes accessed | tf_op | source)
XLA Modules:
  0.0 43.1 jit_solution(7236063007063411737)
XLA Ops:
  0.6 0.5 %collective-permute-start.3 = (bf16[2,2048,128]{2,1,0:T(8,128)(2,1)}, bf16[2,2048,128]{2,1,0:T(8,128)(2,1)S(1)}, u32[]{:S(2)}, u32[]{:S(2)}) collective-permute-start(bf16[2,2048,128]{2,1,0:T(8,128)(2,1)} %refs_4_.5), channel_id=1, source_target_pairs={{0,8},{8,0},{16,24},{24,16},{1,9},{9,1},{17,25},{25,17},{2,10},{10... | collective-permute-start | bytes 3145736 | tf_op jit(solution)/shard_map/ppermute | solution.py:317
  1.2 0.1 collective-permute-start.5
  1.2 1.8 %shard_map.50 = (bf16[2,544,128]{2,1,0:T(8,128)(2,1)}, bf16[2,544,128]{2,1,0:T(8,128)(2,1)}) custom-call(bf16[2,2048,128]{2,1,0:T(8,128)(2,1)} %own_input.3, bf16[2,2048,128]{2,1,0:T(8,128)(2,1)} %refs_4_.5, bf16[128,128]{1,0:T(8,128)(2,1)} %refs_0_.5), custom_call_target="tpu_custom_call" | custom-call | tf_op jit(solution)/shard_map/pallas_call | solution.py:331
  3.1 3.0 %collective-permute-start.1 = (bf16[2,544,128]{2,1,0:T(8,128)(2,1)}, bf16[2,544,128]{2,1,0:T(8,128)(2,1)}, u32[]{:S(2)}, u32[]{:S(2)}) collective-permute-start(bf16[2,544,128]{2,1,0:T(8,128)(2,1)} %get-tuple-element.17), channel_id=1, source_target_pairs={{0,16},{8,24},{16,0},{24,8},{1,17},{9,25},{17,1},{25,9},{2,18},{10... | collective-permute-start | bytes 835592 | tf_op jit(solution)/shard_map/ppermute | solution.py:325
  6.1 0.0 collective-permute-start.2
  6.1 0.1 pad_add_fusion.place
  6.2 0.8 %shard_map.52 = (bf16[4,224,128]{2,1,0:T(8,128)(2,1)}, bf16[4,288,128]{2,1,0:T(8,128)(2,1)}) custom-call(bf16[2,2048,128]{2,1,0:T(8,128)(2,1)S(1)} %copy-done, bf16[2,2048,128]{2,1,0:T(8,128)(2,1)S(1)} %collective-permute-done.3.refs_5_.peer_grad), custom_call_target="tpu_custom_call" | custom-call | tf_op jit(solution)/shard_map/pallas_call | solution.py:366
  7.0 1.3 %collective-permute-start.6 = (bf16[4,224,128]{2,1,0:T(8,128)(2,1)}, bf16[4,224,128]{2,1,0:T(8,128)(2,1)}, u32[]{:S(2)}, u32[]{:S(2)}) collective-permute-start(bf16[4,224,128]{2,1,0:T(8,128)(2,1)} %get-tuple-element.21), channel_id=1, source_target_pairs={{16,0},{24,8},{17,1},{25,9},{18,2},{26,10},{19,3},{27,11},{20,4},{... | collective-permute-start | bytes 688136 | tf_op jit(solution)/shard_map/ppermute | solution.py:325
  8.3 5.3 %shard_map.53.running = f32[64,512]{1,0:T(8,128)S(1)} custom-call(s32[2]{0:T(128)S(1)} %pad_add_fusion.place, bf16[2,2048,128]{2,1,0:T(8,128)(2,1)S(1)} %copy-done.1, bf16[2,2048,128]{2,1,0:T(8,128)(2,1)} %collective-permute-done.5.peer_input, bf16[2,2048,128]{2,1,0:T(8,128)(2,1)S(1)} %copy-done, ...), custom_call_target="tpu_custom_call" | custom-call | flops 268435456000 | bytes 2097152000 | tf_op jit(solution)/shard_map/pallas_call | solution.py:377
  13.7 0.2 collective-permute-done.1.refs_2_.refs_6_.own_got
  13.9 4.9 %collective-permute-done.2.refs_3_.refs_7_.peer_got = bf16[2,544,128]{2,1,0:T(8,128)(2,1)} collective-permute-done((bf16[2,544,128]{2,1,0:T(8,128)(2,1)}, bf16[2,544,128]{2,1,0:T(8,128)(2,1)}, u32[]{:S(2)}, u32[]{:S(2)}) %collective-permute-start.2) | collective-permute-done | bytes 278560 | tf_op jit(solution)/shard_map/ppermute | solution.py:325
  18.7 3.7 %shard_map.54 = f32[64,512]{1,0:T(8,128)S(1)} custom-call(s32[2]{0:T(128)S(1)} %pad_add_fusion.place, bf16[2,2048,128]{2,1,0:T(8,128)(2,1)S(1)} %copy-done.1, bf16[2,2048,128]{2,1,0:T(8,128)(2,1)} %collective-permute-done.5.peer_input, bf16[2,2048,128]{2,1,0:T(8,128)(2,1)S(1)} %copy-done, bf16[2,2048,128]{2,1,0:T(8,128)(2,1)S(1)} %collective-permute-done.3.refs_5_.peer_grad, ...), custom_call_target="tpu_custom_call" | custom-call | flops 201326592 | bytes 1572864 | tf_op jit(solution)/shard_map/pallas_call | solution.py:388
  22.4 0.0 copy-start.2
  22.4 1.8 %collective-permute-done.6.refs_6_ = bf16[4,224,128]{2,1,0:T(8,128)(2,1)} collective-permute-done((bf16[4,224,128]{2,1,0:T(8,128)(2,1)}, bf16[4,224,128]{2,1,0:T(8,128)(2,1)}, u32[]{:S(2)}, u32[]{:S(2)}) %collective-permute-start.6) | collective-permute-done | bytes 229408 | tf_op jit(solution)/shard_map/ppermute | solution.py:325
  24.2 0.1 collective-permute-start
  24.3 1.3 %collective-permute-start.4 = (bf16[4,288,128]{2,1,0:T(8,128)(2,1)}, bf16[4,288,128]{2,1,0:T(8,128)(2,1)S(1)}, u32[]{:S(2)}, u32[]{:S(2)}) collective-permute-start(bf16[4,288,128]{2,1,0:T(8,128)(2,1)} %get-tuple-element.20), channel_id=1, source_target_pairs={{16,0},{24,8},{17,1},{25,9},{18,2},{26,10},{19,3},{27,11},{20,4},{... | collective-permute-start | bytes 884744 | tf_op jit(solution)/shard_map/ppermute | solution.py:325
  25.6 3.0 %shard_map.51 = (bf16[2,512,128]{2,1,0:T(8,128)(2,1)S(1)}, bf16[2,512,128]{2,1,0:T(8,128)(2,1)S(1)}) custom-call(s32[2]{0:T(128)S(1)} %pad_add_fusion.place, bf16[128,128]{1,0:T(8,128)(2,1)S(1)} %copy-done.2, bf16[128,128]{1,0:T(8,128)(2,1)S(1)} %collective-permute-done.refs_1_, bf16[2,544,128]{2,1,0:T(8,128)(2,1)} %collective-permute-done.1.refs_2_.refs_6_.own_got, ...), custom_call_target="tpu_custom_call" | custom-call | flops 268435456 | bytes 1572864 | tf_op jit(solution)/shard_map/pallas_call | solution.py:412
  28.6 0.5 %collective-permute-start.7 = (bf16[2,512,128]{2,1,0:T(8,128)(2,1)S(1)}, bf16[2,512,128]{2,1,0:T(8,128)(2,1)S(1)}, u32[]{:S(2)}, u32[]{:S(2)}) collective-permute-start(bf16[2,512,128]{2,1,0:T(8,128)(2,1)S(1)} %get-tuple-element.27), channel_id=1, source_target_pairs={{0,8},{8,0},{16,24},{24,16},{1,9},{9,1},{17,25},{25,17},{2,10},{10... | collective-permute-start | bytes 786440 | tf_op jit(solution)/shard_map/ppermute | solution.py:317
  29.2 0.1 collective-permute-start.11
  29.3 1.1 %collective-permute-done.11 = f32[64,128]{1,0:T(8,128)S(1)} collective-permute-done((f32[64,128]{1,0:T(8,128)S(1)}, f32[64,128]{1,0:T(8,128)S(1)}, u32[]{:S(2)}, u32[]{:S(2)}) %collective-permute-start.11) | collective-permute-done | bytes 32800 | tf_op jit(solution)/shard_map/ppermute | solution.py:317
  30.5 3.9 %collective-permute-start.14 = (f32[128,128]{1,0:T(8,128)S(1)}, f32[128,128]{1,0:T(8,128)S(1)}, u32[]{:S(2)}, u32[]{:S(2)}) collective-permute-start(f32[128,128]{1,0:T(8,128)S(1)} %maximum_select_fusion), channel_id=1, source_target_pairs={{0,3},{1,2},{2,1},{3,0},{4,7},{5,6},{6,5},{7,4},{8,11},{9,10},{10,... | collective-permute-start | bytes 196616 | tf_op jit(solution)/shard_map/ppermute | solution.py:443
  34.4 0.6 %collective-permute-start.12 = (f32[128,128]{1,0:T(8,128)S(1)}, f32[128,128]{1,0:T(8,128)S(1)}, u32[]{:S(2)}, u32[]{:S(2)}) collective-permute-start(f32[128,128]{1,0:T(8,128)S(1)} %maximum_select_fusion), channel_id=1, source_target_pairs={{0,1},{1,0},{2,3},{3,2},{4,5},{5,4},{6,7},{7,6},{8,9},{9,8},{10,11... | collective-permute-start | bytes 196616 | tf_op jit(solution)/shard_map/ppermute | solution.py:443
  35.0 0.8 %collective-permute-done.4.refs_6_ = bf16[4,288,128]{2,1,0:T(8,128)(2,1)S(1)} collective-permute-done((bf16[4,288,128]{2,1,0:T(8,128)(2,1)}, bf16[4,288,128]{2,1,0:T(8,128)(2,1)S(1)}, u32[]{:S(2)}, u32[]{:S(2)}) %collective-permute-start.4) | collective-permute-done | bytes 294944 | tf_op jit(solution)/shard_map/ppermute | solution.py:325
  35.8 2.0 %shard_map.55 = (bf16[2,224,128]{2,1,0:T(8,128)(2,1)S(1)}, bf16[2,224,128]{2,1,0:T(8,128)(2,1)S(1)}) custom-call(s32[2]{0:T(128)S(1)} %pad_add_fusion.place, bf16[128,128]{1,0:T(8,128)(2,1)S(1)} %copy-done.2, bf16[128,128]{1,0:T(8,128)(2,1)S(1)} %collective-permute-done.refs_1_, bf16[2,544,128]{2,1,0:T(8,128)(2,1)} %collective-permute-done.1.refs_2_.refs_6_.own_got, ...), custom_call_target="tpu_custom_call" | custom-call | flops 268435456 | bytes 1310720 | tf_op jit(solution)/shard_map/pallas_call | solution.py:412
  37.8 0.1 collective-permute-start.8
  37.9 2.2 %shard_map.56 = (bf16[2,288,128]{2,1,0:T(8,128)(2,1)S(1)}, bf16[2,288,128]{2,1,0:T(8,128)(2,1)S(1)}) custom-call(s32[2]{0:T(128)S(1)} %pad_add_fusion.place, bf16[128,128]{1,0:T(8,128)(2,1)S(1)} %copy-done.2, bf16[128,128]{1,0:T(8,128)(2,1)S(1)} %collective-permute-done.refs_1_, bf16[2,544,128]{2,1,0:T(8,128)(2,1)} %collective-permute-done.1.refs_2_.refs_6_.own_got, ...), custom_call_target="tpu_custom_call" | custom-call | flops 150994944 | bytes 737280 | tf_op jit(solution)/shard_map/pallas_call | solution.py:412
  40.1 0.6 %collective-permute-start.9 = (bf16[2,288,128]{2,1,0:T(8,128)(2,1)S(1)}, bf16[2,288,128]{2,1,0:T(8,128)(2,1)S(1)}, u32[]{:S(2)}, u32[]{:S(2)}) collective-permute-start(bf16[2,288,128]{2,1,0:T(8,128)(2,1)S(1)} %get-tuple-element.29), channel_id=1, source_target_pairs={{0,8},{8,0},{16,24},{24,16},{1,9},{9,1},{17,25},{25,17},{2,10},{10... | collective-permute-start | bytes 442376 | tf_op jit(solution)/shard_map/ppermute | solution.py:317
  40.6 0.6 %add_add_fusion = f32[128,128]{1,0:T(8,128)} fusion(f32[128,128]{1,0:T(8,128)S(1)} %collective-permute-done.13, f32[128,128]{1,0:T(8,128)S(1)} %collective-permute-done.14, f32[128,128]{1,0:T(8,128)S(1)} %maximum_select_fusion, f32[128,128]{1,0:T(8,128)S(1)} %collective-permute-done.12), kind=kLoop, calls=%fused_computation.2 | loop fusion | flops 49152 | bytes 327680 | tf_op jit(solution)/shard_map/add | solution.py:445
  41.3 0.3 collective-permute-done.9
  41.7 0.1 constant_dynamic-update-slice_fusion.8
  41.8 0.1 constant_dynamic-update-slice_fusion.6
  42.0 1.1 %broadcast_select_fusion = bf16[2,2048,128]{2,1,0:T(8,128)(2,1)} fusion(bf16[2,2048,128]{2,1,0:T(8,128)(2,1)S(1)} %constant_dynamic-update-slice_fusion, bf16[2,2048,128]{2,1,0:T(8,128)(2,1)S(1)} %get-tuple-element.34, pred[]{:T(512)S(6)} %eq.7), kind=kLoop, calls=%fused_computation | loop fusion | flops 524288 | bytes 3145729 | tf_op jit(solution)/shard_map/jit(_where)/select_n | solution.py:433
  (27 shorter events, 0.3 us)
Async XLA Ops:
  0.6 5.5 %copy-start = (bf16[2,2048,128]{2,1,0:T(8,128)(2,1)S(1)}, bf16[2,2048,128]{2,1,0:T(8,128)(2,1)}, u32[]{:S(2)}) copy-start(bf16[2,2048,128]{2,1,0:T(8,128)(2,1)} %refs_4_.5) | copy-start | bytes 3145732
  0.6 5.5 %collective-permute-start.3 = (bf16[2,2048,128]{2,1,0:T(8,128)(2,1)}, bf16[2,2048,128]{2,1,0:T(8,128)(2,1)S(1)}, u32[]{:S(2)}, u32[]{:S(2)}) collective-permute-start(bf16[2,2048,128]{2,1,0:T(8,128)(2,1)} %refs_4_.5), channel_id=1, source_target_pairs={{0,8},{8,0},{16,24},{24,16},{1,9},{9,1},{17,25},{25,17},{2,10},{10... | collective-permute-start | bytes 3145736 | tf_op jit(solution)/shard_map/ppermute | solution.py:317
  1.2 7.2 %collective-permute-start.5 = (bf16[2,2048,128]{2,1,0:T(8,128)(2,1)}, bf16[2,2048,128]{2,1,0:T(8,128)(2,1)}, u32[]{:S(2)}, u32[]{:S(2)}) collective-permute-start(bf16[2,2048,128]{2,1,0:T(8,128)(2,1)} %own_input.3), channel_id=1, source_target_pairs={{0,8},{8,0},{16,24},{24,16},{1,9},{9,1},{17,25},{25,17},{2,10},{10... | collective-permute-start | bytes 3145736 | tf_op jit(solution)/shard_map/ppermute | solution.py:317
  3.1 10.8 %collective-permute-start.1 = (bf16[2,544,128]{2,1,0:T(8,128)(2,1)}, bf16[2,544,128]{2,1,0:T(8,128)(2,1)}, u32[]{:S(2)}, u32[]{:S(2)}) collective-permute-start(bf16[2,544,128]{2,1,0:T(8,128)(2,1)} %get-tuple-element.17), channel_id=1, source_target_pairs={{0,16},{8,24},{16,0},{24,8},{1,17},{9,25},{17,1},{25,9},{2,18},{10... | collective-permute-start | bytes 835592 | tf_op jit(solution)/shard_map/ppermute | solution.py:325
  6.1 12.6 %collective-permute-start.2 = (bf16[2,544,128]{2,1,0:T(8,128)(2,1)}, bf16[2,544,128]{2,1,0:T(8,128)(2,1)}, u32[]{:S(2)}, u32[]{:S(2)}) collective-permute-start(bf16[2,544,128]{2,1,0:T(8,128)(2,1)} %get-tuple-element.18), channel_id=1, source_target_pairs={{0,24},{8,16},{16,8},{24,0},{1,25},{9,17},{17,9},{25,1},{2,26},{10... | collective-permute-start | bytes 835592 | tf_op jit(solution)/shard_map/ppermute | solution.py:325
  6.2 2.2 %copy-start.1 = (bf16[2,2048,128]{2,1,0:T(8,128)(2,1)S(1)}, bf16[2,2048,128]{2,1,0:T(8,128)(2,1)}, u32[]{:S(2)}) copy-start(bf16[2,2048,128]{2,1,0:T(8,128)(2,1)} %own_input.3) | copy-start | bytes 3145732
  7.0 17.2 %collective-permute-start.6 = (bf16[4,224,128]{2,1,0:T(8,128)(2,1)}, bf16[4,224,128]{2,1,0:T(8,128)(2,1)}, u32[]{:S(2)}, u32[]{:S(2)}) collective-permute-start(bf16[4,224,128]{2,1,0:T(8,128)(2,1)} %get-tuple-element.21), channel_id=1, source_target_pairs={{16,0},{24,8},{17,1},{25,9},{18,2},{26,10},{19,3},{27,11},{20,4},{... | collective-permute-start | bytes 688136 | tf_op jit(solution)/shard_map/ppermute | solution.py:325
  22.4 1.8 %copy-start.2 = (bf16[128,128]{1,0:T(8,128)(2,1)S(1)}, bf16[128,128]{1,0:T(8,128)(2,1)}, u32[]{:S(2)}) copy-start(bf16[128,128]{1,0:T(8,128)(2,1)} %refs_0_.5) | copy-start | bytes 98308
  24.2 5.0 %collective-permute-start.10 = (f32[64,256]{1,0:T(8,128)S(1)}, f32[64,256]{1,0:T(8,128)S(1)}, u32[]{:S(2)}, u32[]{:S(2)}) collective-permute-start(f32[64,256]{1,0:T(8,128)S(1)} %constant_dynamic-slice_fusion.2), channel_id=1, source_target_pairs={{0,16},{8,24},{16,0},{24,8},{1,17},{9,25},{17,1},{25,9},{2,18},{10... | collective-permute-start | bytes 196616 | tf_op jit(solution)/shard_map/ppermute | solution.py:325
  24.2 1.4 %collective-permute-start = (bf16[128,128]{1,0:T(8,128)(2,1)S(1)}, bf16[128,128]{1,0:T(8,128)(2,1)S(1)}, u32[]{:S(2)}, u32[]{:S(2)}) collective-permute-start(bf16[128,128]{1,0:T(8,128)(2,1)S(1)} %copy-done.2), channel_id=1, source_target_pairs={{0,8},{8,0},{16,24},{24,16},{1,9},{9,1},{17,25},{25,17},{2,10},{10... | collective-permute-start | bytes 98312 | tf_op jit(solution)/shard_map/ppermute | solution.py:317
  24.3 11.5 %collective-permute-start.4 = (bf16[4,288,128]{2,1,0:T(8,128)(2,1)}, bf16[4,288,128]{2,1,0:T(8,128)(2,1)S(1)}, u32[]{:S(2)}, u32[]{:S(2)}) collective-permute-start(bf16[4,288,128]{2,1,0:T(8,128)(2,1)} %get-tuple-element.20), channel_id=1, source_target_pairs={{16,0},{24,8},{17,1},{25,9},{18,2},{26,10},{19,3},{27,11},{20,4},{... | collective-permute-start | bytes 884744 | tf_op jit(solution)/shard_map/ppermute | solution.py:325
  28.6 6.4 %collective-permute-start.7 = (bf16[2,512,128]{2,1,0:T(8,128)(2,1)S(1)}, bf16[2,512,128]{2,1,0:T(8,128)(2,1)S(1)}, u32[]{:S(2)}, u32[]{:S(2)}) collective-permute-start(bf16[2,512,128]{2,1,0:T(8,128)(2,1)S(1)} %get-tuple-element.27), channel_id=1, source_target_pairs={{0,8},{8,0},{16,24},{24,16},{1,9},{9,1},{17,25},{25,17},{2,10},{10... | collective-permute-start | bytes 786440 | tf_op jit(solution)/shard_map/ppermute | solution.py:317
  29.2 1.3 %collective-permute-start.11 = (f32[64,128]{1,0:T(8,128)S(1)}, f32[64,128]{1,0:T(8,128)S(1)}, u32[]{:S(2)}, u32[]{:S(2)}) collective-permute-start(f32[64,128]{1,0:T(8,128)S(1)} %get-tuple-element.39), channel_id=1, source_target_pairs={{0,8},{8,0},{16,24},{24,16},{1,9},{9,1},{17,25},{25,17},{2,10},{10... | collective-permute-start | bytes 98312 | tf_op jit(solution)/shard_map/ppermute | solution.py:317
  30.5 10.2 %collective-permute-start.14 = (f32[128,128]{1,0:T(8,128)S(1)}, f32[128,128]{1,0:T(8,128)S(1)}, u32[]{:S(2)}, u32[]{:S(2)}) collective-permute-start(f32[128,128]{1,0:T(8,128)S(1)} %maximum_select_fusion), channel_id=1, source_target_pairs={{0,3},{1,2},{2,1},{3,0},{4,7},{5,6},{6,5},{7,4},{8,11},{9,10},{10,... | collective-permute-start | bytes 196616 | tf_op jit(solution)/shard_map/ppermute | solution.py:443
  34.4 6.3 %collective-permute-start.13 = (f32[128,128]{1,0:T(8,128)S(1)}, f32[128,128]{1,0:T(8,128)S(1)}, u32[]{:S(2)}, u32[]{:S(2)}) collective-permute-start(f32[128,128]{1,0:T(8,128)S(1)} %maximum_select_fusion), channel_id=1, source_target_pairs={{0,2},{1,3},{2,0},{3,1},{4,6},{5,7},{6,4},{7,5},{8,10},{9,11},{10,... | collective-permute-start | bytes 196616 | tf_op jit(solution)/shard_map/ppermute | solution.py:443
  34.4 6.3 %collective-permute-start.12 = (f32[128,128]{1,0:T(8,128)S(1)}, f32[128,128]{1,0:T(8,128)S(1)}, u32[]{:S(2)}, u32[]{:S(2)}) collective-permute-start(f32[128,128]{1,0:T(8,128)S(1)} %maximum_select_fusion), channel_id=1, source_target_pairs={{0,1},{1,0},{2,3},{3,2},{4,5},{5,4},{6,7},{7,6},{8,9},{9,8},{10,11... | collective-permute-start | bytes 196616 | tf_op jit(solution)/shard_map/ppermute | solution.py:443
  37.8 3.5 %collective-permute-start.8 = (bf16[2,224,128]{2,1,0:T(8,128)(2,1)S(1)}, bf16[2,224,128]{2,1,0:T(8,128)(2,1)S(1)}, u32[]{:S(2)}, u32[]{:S(2)}) collective-permute-start(bf16[2,224,128]{2,1,0:T(8,128)(2,1)S(1)} %get-tuple-element.28), channel_id=1, source_target_pairs={{0,8},{8,0},{16,24},{24,16},{1,9},{9,1},{17,25},{25,17},{2,10},{10... | collective-permute-start | bytes 344072 | tf_op jit(solution)/shard_map/ppermute | solution.py:317
  40.1 1.6 %collective-permute-start.9 = (bf16[2,288,128]{2,1,0:T(8,128)(2,1)S(1)}, bf16[2,288,128]{2,1,0:T(8,128)(2,1)S(1)}, u32[]{:S(2)}, u32[]{:S(2)}) collective-permute-start(bf16[2,288,128]{2,1,0:T(8,128)(2,1)S(1)} %get-tuple-element.29), channel_id=1, source_target_pairs={{0,8},{8,0},{16,24},{24,16},{1,9},{9,1},{17,25},{25,17},{2,10},{10... | collective-permute-start | bytes 442376 | tf_op jit(solution)/shard_map/ppermute | solution.py:317

commit v6 on v4

--- a/solution.py
+++ b/solution.py
@@ -243,12 +243,12 @@
     own_index = lax.axis_index("seq")
     chip, core = lax.div(own_index, CORES), lax.rem(own_index, CORES)
 
-    def arrival(source, start, target, number):
-        return pltpu.make_async_copy(
-            source.at[:, pl.ds(pl.multiple_of(start, GROUP_SIZE), part), :],
-            target.at[:, pl.ds(0, part), :],
-            in_sems.at[number],
-        )
+    def arrivals(source, start, target, number):
+        rows = pl.ds(pl.multiple_of(start, GROUP_SIZE), part)
+        for sequence in range(sequences):
+            pltpu.make_async_copy(
+                source.at[sequence, rows, :], target.at[sequence, pl.ds(0, part), :], in_sems.at[number]
+            ).start()
 
     for number in range(count):
         distance, other = number // CORES + 1, number % CORES
@@ -265,12 +265,13 @@
             ).start()
         lax.cond(
             chip >= distance,
-            lambda: arrival(output_grad, start, target, number).start(),
-            lambda: arrival(inputs, start + part, target, number).start(),
+            lambda: arrivals(output_grad, start, target, number),
+            lambda: arrivals(inputs, start + part, target, number),
         )
     for number in range(count):
         pltpu.make_async_copy(stages[number], stages[number], in_sems.at[number]).wait()
-        pltpu.make_async_copy(stages[number], outs[number], out_sems.at[number]).start()
+        for sequence in range(sequences):
+            pltpu.make_async_copy(stages[number].at[sequence], outs[number].at[sequence], out_sems.at[number]).start()
     for number in range(count):
         pltpu.make_async_copy(stages[number], outs[number], out_sems.at[number]).wait()
 

time: 43.6 us -> 43.7 us (level)
  transfers between devices with their start and end apart: 15 -> 15, of which waited for: 6 -> 6; matrix products, arithmetic and copies ran while one was open for 2% -> 2% of each run, Pallas kernels for 44% -> 45%
where the time goes in v6:
time: 43.7 us; the launch traced here: 43.3 us
  Pallas kernels  19.3 us (44%)
  starting transfers between devices  12.1 us (28%)
  waiting for transfers between devices  8.91 us (20%)
  other arithmetic  1.82 us (4%)
  between operations  0.84 us (2%)
    pallas_call x3, Pallas kernels, input_part(): pl.pallas_call(functools.partial(input_grad_kernel, chips, which, offset,...  7.56 us
    ppermute x5, waiting for transfers between devices, from_chip(): return lax.ppermute(value, 'seq', pairs)  7.4 us
    ppermute x5, starting transfers between devices, from_chip(): return lax.ppermute(value, 'seq', pairs)  5.59 us
    pallas_call x1, Pallas kernels, per_device(): pl.pallas_call(own_lags_kernel, in_specs=[in_smem] + [in_vmem] * 4, out_s...  5.34 us
    ppermute x3, starting transfers between devices, per_device(): terms.append(lax.ppermute(own, 'dp', [(i, i ^ k) for i in range(copies)]))  4.53 us
    pallas_call x1, Pallas kernels, per_device(): pl.pallas_call(functools.partial(round_lags_kernel, chips, k), in_specs=[...  3.66 us
    ppermute x7, starting transfers between devices, swap_cores(): return lax.ppermute(value, 'seq', [(i, i ^ 1) for i in range(shard_count)])  1.98 us
    pallas_call x1, Pallas kernels, per_device(): pl.pallas_call(functools.partial(parts_kernel, chips, slot_rows), in_spec...  1.9 us
  transfers between devices with their start and end apart: 15, of which 6 were waited for; matrix products, arithmetic and copies ran while one was open for 2% of the time, Pallas kernels for 45%

profile of v6, /device:TPU:0, one launch (start us, length us, event | category | flops | bytes accessed | tf_op | source)
XLA Modules:
  0.0 43.3 jit_solution(2238732368503211492)
XLA Ops:
  0.6 0.5 %collective-permute-start.3 = (bf16[2,2048,128]{2,1,0:T(8,128)(2,1)}, bf16[2,2048,128]{2,1,0:T(8,128)(2,1)S(1)}, u32[]{:S(2)}, u32[]{:S(2)}) collective-permute-start(bf16[2,2048,128]{2,1,0:T(8,128)(2,1)} %refs_4_.5), channel_id=1, source_target_pairs={{0,8},{8,0},{16,24},{24,16},{1,9},{9,1},{17,25},{25,17},{2,10},{10... | collective-permute-start | bytes 3145736 | tf_op jit(solution)/shard_map/ppermute | solution.py:318
  1.2 0.1 collective-permute-start.5
  1.2 1.9 %shard_map.50 = (bf16[2,544,128]{2,1,0:T(8,128)(2,1)}, bf16[2,544,128]{2,1,0:T(8,128)(2,1)}) custom-call(bf16[2,2048,128]{2,1,0:T(8,128)(2,1)} %own_input.3, bf16[2,2048,128]{2,1,0:T(8,128)(2,1)} %refs_4_.5, bf16[128,128]{1,0:T(8,128)(2,1)} %refs_0_.5), custom_call_target="tpu_custom_call" | custom-call | tf_op jit(solution)/shard_map/pallas_call | solution.py:332
  3.1 3.0 %collective-permute-start.1 = (bf16[2,544,128]{2,1,0:T(8,128)(2,1)}, bf16[2,544,128]{2,1,0:T(8,128)(2,1)}, u32[]{:S(2)}, u32[]{:S(2)}) collective-permute-start(bf16[2,544,128]{2,1,0:T(8,128)(2,1)} %get-tuple-element.17), channel_id=1, source_target_pairs={{0,16},{8,24},{16,0},{24,8},{1,17},{9,25},{17,1},{25,9},{2,18},{10... | collective-permute-start | bytes 835592 | tf_op jit(solution)/shard_map/ppermute | solution.py:326
  6.2 0.1 pad_add_fusion.place
  6.2 0.0 collective-permute-done.3.refs_5_.peer_grad
  6.2 0.8 %shard_map.52 = (bf16[4,224,128]{2,1,0:T(8,128)(2,1)}, bf16[4,288,128]{2,1,0:T(8,128)(2,1)}) custom-call(bf16[2,2048,128]{2,1,0:T(8,128)(2,1)S(1)} %copy-done, bf16[2,2048,128]{2,1,0:T(8,128)(2,1)S(1)} %collective-permute-done.3.refs_5_.peer_grad), custom_call_target="tpu_custom_call" | custom-call | tf_op jit(solution)/shard_map/pallas_call | solution.py:367
  7.1 1.3 %collective-permute-start.6 = (bf16[4,224,128]{2,1,0:T(8,128)(2,1)}, bf16[4,224,128]{2,1,0:T(8,128)(2,1)}, u32[]{:S(2)}, u32[]{:S(2)}) collective-permute-start(bf16[4,224,128]{2,1,0:T(8,128)(2,1)} %get-tuple-element.21), channel_id=1, source_target_pairs={{16,0},{24,8},{17,1},{25,9},{18,2},{26,10},{19,3},{27,11},{20,4},{... | collective-permute-start | bytes 688136 | tf_op jit(solution)/shard_map/ppermute | solution.py:326
  8.4 5.3 %shard_map.53.running = f32[64,512]{1,0:T(8,128)S(1)} custom-call(s32[2]{0:T(128)S(1)} %pad_add_fusion.place, bf16[2,2048,128]{2,1,0:T(8,128)(2,1)S(1)} %copy-done.1, bf16[2,2048,128]{2,1,0:T(8,128)(2,1)} %collective-permute-done.5.peer_input, bf16[2,2048,128]{2,1,0:T(8,128)(2,1)S(1)} %copy-done, ...), custom_call_target="tpu_custom_call" | custom-call | flops 268435456000 | bytes 2097152000 | tf_op jit(solution)/shard_map/pallas_call | solution.py:378
  13.7 0.2 collective-permute-done.1.refs_2_.refs_6_.own_got
  13.9 4.9 %collective-permute-done.2.refs_3_.refs_7_.peer_got = bf16[2,544,128]{2,1,0:T(8,128)(2,1)} collective-permute-done((bf16[2,544,128]{2,1,0:T(8,128)(2,1)}, bf16[2,544,128]{2,1,0:T(8,128)(2,1)}, u32[]{:S(2)}, u32[]{:S(2)}) %collective-permute-start.2) | collective-permute-done | bytes 278560 | tf_op jit(solution)/shard_map/ppermute | solution.py:326
  18.8 3.7 %shard_map.54 = f32[64,512]{1,0:T(8,128)S(1)} custom-call(s32[2]{0:T(128)S(1)} %pad_add_fusion.place, bf16[2,2048,128]{2,1,0:T(8,128)(2,1)S(1)} %copy-done.1, bf16[2,2048,128]{2,1,0:T(8,128)(2,1)} %collective-permute-done.5.peer_input, bf16[2,2048,128]{2,1,0:T(8,128)(2,1)S(1)} %copy-done, bf16[2,2048,128]{2,1,0:T(8,128)(2,1)S(1)} %collective-permute-done.3.refs_5_.peer_grad, ...), custom_call_target="tpu_custom_call" | custom-call | flops 201326592 | bytes 1572864 | tf_op jit(solution)/shard_map/pallas_call | solution.py:389
  22.5 0.0 copy-start.2
  22.5 1.8 %collective-permute-done.6.refs_6_ = bf16[4,224,128]{2,1,0:T(8,128)(2,1)} collective-permute-done((bf16[4,224,128]{2,1,0:T(8,128)(2,1)}, bf16[4,224,128]{2,1,0:T(8,128)(2,1)}, u32[]{:S(2)}, u32[]{:S(2)}) %collective-permute-start.6) | collective-permute-done | bytes 229408 | tf_op jit(solution)/shard_map/ppermute | solution.py:326
  24.3 0.1 collective-permute-start
  24.4 1.3 %collective-permute-start.4 = (bf16[4,288,128]{2,1,0:T(8,128)(2,1)}, bf16[4,288,128]{2,1,0:T(8,128)(2,1)S(1)}, u32[]{:S(2)}, u32[]{:S(2)}) collective-permute-start(bf16[4,288,128]{2,1,0:T(8,128)(2,1)} %get-tuple-element.20), channel_id=1, source_target_pairs={{16,0},{24,8},{17,1},{25,9},{18,2},{26,10},{19,3},{27,11},{20,4},{... | collective-permute-start | bytes 884744 | tf_op jit(solution)/shard_map/ppermute | solution.py:326
  25.7 3.2 %shard_map.51 = (bf16[2,512,128]{2,1,0:T(8,128)(2,1)S(1)}, bf16[2,512,128]{2,1,0:T(8,128)(2,1)S(1)}) custom-call(s32[2]{0:T(128)S(1)} %pad_add_fusion.place, bf16[128,128]{1,0:T(8,128)(2,1)S(1)} %copy-done.2, bf16[128,128]{1,0:T(8,128)(2,1)S(1)} %collective-permute-done.refs_1_, bf16[2,544,128]{2,1,0:T(8,128)(2,1)} %collective-permute-done.1.refs_2_.refs_6_.own_got, ...), custom_call_target="tpu_custom_call" | custom-call | flops 268435456 | bytes 1572864 | tf_op jit(solution)/shard_map/pallas_call | solution.py:413
  28.9 0.5 %collective-permute-start.7 = (bf16[2,512,128]{2,1,0:T(8,128)(2,1)S(1)}, bf16[2,512,128]{2,1,0:T(8,128)(2,1)S(1)}, u32[]{:S(2)}, u32[]{:S(2)}) collective-permute-start(bf16[2,512,128]{2,1,0:T(8,128)(2,1)S(1)} %get-tuple-element.27), channel_id=1, source_target_pairs={{0,8},{8,0},{16,24},{24,16},{1,9},{9,1},{17,25},{25,17},{2,10},{10... | collective-permute-start | bytes 786440 | tf_op jit(solution)/shard_map/ppermute | solution.py:318
  29.5 0.1 collective-permute-start.11
  29.6 1.2 %collective-permute-done.11 = f32[64,128]{1,0:T(8,128)S(1)} collective-permute-done((f32[64,128]{1,0:T(8,128)S(1)}, f32[64,128]{1,0:T(8,128)S(1)}, u32[]{:S(2)}, u32[]{:S(2)}) %collective-permute-start.11) | collective-permute-done | bytes 32800 | tf_op jit(solution)/shard_map/ppermute | solution.py:318
  30.7 3.9 %collective-permute-start.14 = (f32[128,128]{1,0:T(8,128)S(1)}, f32[128,128]{1,0:T(8,128)S(1)}, u32[]{:S(2)}, u32[]{:S(2)}) collective-permute-start(f32[128,128]{1,0:T(8,128)S(1)} %maximum_select_fusion), channel_id=1, source_target_pairs={{0,3},{1,2},{2,1},{3,0},{4,7},{5,6},{6,5},{7,4},{8,11},{9,10},{10,... | collective-permute-start | bytes 196616 | tf_op jit(solution)/shard_map/ppermute | solution.py:444
  34.6 0.6 %collective-permute-start.12 = (f32[128,128]{1,0:T(8,128)S(1)}, f32[128,128]{1,0:T(8,128)S(1)}, u32[]{:S(2)}, u32[]{:S(2)}) collective-permute-start(f32[128,128]{1,0:T(8,128)S(1)} %maximum_select_fusion), channel_id=1, source_target_pairs={{0,1},{1,0},{2,3},{3,2},{4,5},{5,4},{6,7},{7,6},{8,9},{9,8},{10,11... | collective-permute-start | bytes 196616 | tf_op jit(solution)/shard_map/ppermute | solution.py:444
  35.3 0.6 %collective-permute-done.4.refs_6_ = bf16[4,288,128]{2,1,0:T(8,128)(2,1)S(1)} collective-permute-done((bf16[4,288,128]{2,1,0:T(8,128)(2,1)}, bf16[4,288,128]{2,1,0:T(8,128)(2,1)S(1)}, u32[]{:S(2)}, u32[]{:S(2)}) %collective-permute-start.4) | collective-permute-done | bytes 294944 | tf_op jit(solution)/shard_map/ppermute | solution.py:326
  35.9 2.0 %shard_map.55 = (bf16[2,224,128]{2,1,0:T(8,128)(2,1)S(1)}, bf16[2,224,128]{2,1,0:T(8,128)(2,1)S(1)}) custom-call(s32[2]{0:T(128)S(1)} %pad_add_fusion.place, bf16[128,128]{1,0:T(8,128)(2,1)S(1)} %copy-done.2, bf16[128,128]{1,0:T(8,128)(2,1)S(1)} %collective-permute-done.refs_1_, bf16[2,544,128]{2,1,0:T(8,128)(2,1)} %collective-permute-done.1.refs_2_.refs_6_.own_got, ...), custom_call_target="tpu_custom_call" | custom-call | flops 268435456 | bytes 1310720 | tf_op jit(solution)/shard_map/pallas_call | solution.py:413
  37.9 0.1 collective-permute-start.8
  38.0 2.4 %shard_map.56 = (bf16[2,288,128]{2,1,0:T(8,128)(2,1)S(1)}, bf16[2,288,128]{2,1,0:T(8,128)(2,1)S(1)}) custom-call(s32[2]{0:T(128)S(1)} %pad_add_fusion.place, bf16[128,128]{1,0:T(8,128)(2,1)S(1)} %copy-done.2, bf16[128,128]{1,0:T(8,128)(2,1)S(1)} %collective-permute-done.refs_1_, bf16[2,544,128]{2,1,0:T(8,128)(2,1)} %collective-permute-done.1.refs_2_.refs_6_.own_got, ...), custom_call_target="tpu_custom_call" | custom-call | flops 150994944 | bytes 737280 | tf_op jit(solution)/shard_map/pallas_call | solution.py:413
  40.3 0.6 %collective-permute-start.9 = (bf16[2,288,128]{2,1,0:T(8,128)(2,1)S(1)}, bf16[2,288,128]{2,1,0:T(8,128)(2,1)S(1)}, u32[]{:S(2)}, u32[]{:S(2)}) collective-permute-start(bf16[2,288,128]{2,1,0:T(8,128)(2,1)S(1)} %get-tuple-element.29), channel_id=1, source_target_pairs={{0,8},{8,0},{16,24},{24,16},{1,9},{9,1},{17,25},{25,17},{2,10},{10... | collective-permute-start | bytes 442376 | tf_op jit(solution)/shard_map/ppermute | solution.py:318
  40.9 0.6 %add_add_fusion = f32[128,128]{1,0:T(8,128)} fusion(f32[128,128]{1,0:T(8,128)S(1)} %collective-permute-done.13, f32[128,128]{1,0:T(8,128)S(1)} %collective-permute-done.14, f32[128,128]{1,0:T(8,128)S(1)} %maximum_select_fusion, f32[128,128]{1,0:T(8,128)S(1)} %collective-permute-done.12), kind=kLoop, calls=%fused_computation.2 | loop fusion | flops 49152 | bytes 327680 | tf_op jit(solution)/shard_map/add | solution.py:446
  41.6 0.3 collective-permute-done.9
  41.9 0.1 constant_dynamic-update-slice_fusion.8
  42.1 0.1 constant_dynamic-update-slice_fusion.6
  42.2 1.1 %broadcast_select_fusion = bf16[2,2048,128]{2,1,0:T(8,128)(2,1)} fusion(bf16[2,2048,128]{2,1,0:T(8,128)(2,1)S(1)} %constant_dynamic-update-slice_fusion, bf16[2,2048,128]{2,1,0:T(8,128)(2,1)S(1)} %get-tuple-element.34, pred[]{:T(512)S(6)} %eq.7), kind=kLoop, calls=%fused_computation | loop fusion | flops 524288 | bytes 3145729 | tf_op jit(solution)/shard_map/jit(_where)/select_n | solution.py:434
  (27 shorter events, 0.3 us)
Async XLA Ops:
  0.6 5.6 %copy-start = (bf16[2,2048,128]{2,1,0:T(8,128)(2,1)S(1)}, bf16[2,2048,128]{2,1,0:T(8,128)(2,1)}, u32[]{:S(2)}) copy-start(bf16[2,2048,128]{2,1,0:T(8,128)(2,1)} %refs_4_.5) | copy-start | bytes 3145732
  0.6 5.6 %collective-permute-start.3 = (bf16[2,2048,128]{2,1,0:T(8,128)(2,1)}, bf16[2,2048,128]{2,1,0:T(8,128)(2,1)S(1)}, u32[]{:S(2)}, u32[]{:S(2)}) collective-permute-start(bf16[2,2048,128]{2,1,0:T(8,128)(2,1)} %refs_4_.5), channel_id=1, source_target_pairs={{0,8},{8,0},{16,24},{24,16},{1,9},{9,1},{17,25},{25,17},{2,10},{10... | collective-permute-start | bytes 3145736 | tf_op jit(solution)/shard_map/ppermute | solution.py:318
  1.2 7.2 %collective-permute-start.5 = (bf16[2,2048,128]{2,1,0:T(8,128)(2,1)}, bf16[2,2048,128]{2,1,0:T(8,128)(2,1)}, u32[]{:S(2)}, u32[]{:S(2)}) collective-permute-start(bf16[2,2048,128]{2,1,0:T(8,128)(2,1)} %own_input.3), channel_id=1, source_target_pairs={{0,8},{8,0},{16,24},{24,16},{1,9},{9,1},{17,25},{25,17},{2,10},{10... | collective-permute-start | bytes 3145736 | tf_op jit(solution)/shard_map/ppermute | solution.py:318
  3.1 10.8 %collective-permute-start.1 = (bf16[2,544,128]{2,1,0:T(8,128)(2,1)}, bf16[2,544,128]{2,1,0:T(8,128)(2,1)}, u32[]{:S(2)}, u32[]{:S(2)}) collective-permute-start(bf16[2,544,128]{2,1,0:T(8,128)(2,1)} %get-tuple-element.17), channel_id=1, source_target_pairs={{0,16},{8,24},{16,0},{24,8},{1,17},{9,25},{17,1},{25,9},{2,18},{10... | collective-permute-start | bytes 835592 | tf_op jit(solution)/shard_map/ppermute | solution.py:326
  6.2 12.6 %collective-permute-start.2 = (bf16[2,544,128]{2,1,0:T(8,128)(2,1)}, bf16[2,544,128]{2,1,0:T(8,128)(2,1)}, u32[]{:S(2)}, u32[]{:S(2)}) collective-permute-start(bf16[2,544,128]{2,1,0:T(8,128)(2,1)} %get-tuple-element.18), channel_id=1, source_target_pairs={{0,24},{8,16},{16,8},{24,0},{1,25},{9,17},{17,9},{25,1},{2,26},{10... | collective-permute-start | bytes 835592 | tf_op jit(solution)/shard_map/ppermute | solution.py:326
  6.2 2.2 %copy-start.1 = (bf16[2,2048,128]{2,1,0:T(8,128)(2,1)S(1)}, bf16[2,2048,128]{2,1,0:T(8,128)(2,1)}, u32[]{:S(2)}) copy-start(bf16[2,2048,128]{2,1,0:T(8,128)(2,1)} %own_input.3) | copy-start | bytes 3145732
  7.1 17.2 %collective-permute-start.6 = (bf16[4,224,128]{2,1,0:T(8,128)(2,1)}, bf16[4,224,128]{2,1,0:T(8,128)(2,1)}, u32[]{:S(2)}, u32[]{:S(2)}) collective-permute-start(bf16[4,224,128]{2,1,0:T(8,128)(2,1)} %get-tuple-element.21), channel_id=1, source_target_pairs={{16,0},{24,8},{17,1},{25,9},{18,2},{26,10},{19,3},{27,11},{20,4},{... | collective-permute-start | bytes 688136 | tf_op jit(solution)/shard_map/ppermute | solution.py:326
  22.5 1.8 %copy-start.2 = (bf16[128,128]{1,0:T(8,128)(2,1)S(1)}, bf16[128,128]{1,0:T(8,128)(2,1)}, u32[]{:S(2)}) copy-start(bf16[128,128]{1,0:T(8,128)(2,1)} %refs_0_.5) | copy-start | bytes 98308
  24.3 5.2 %collective-permute-start.10 = (f32[64,256]{1,0:T(8,128)S(1)}, f32[64,256]{1,0:T(8,128)S(1)}, u32[]{:S(2)}, u32[]{:S(2)}) collective-permute-start(f32[64,256]{1,0:T(8,128)S(1)} %constant_dynamic-slice_fusion.2), channel_id=1, source_target_pairs={{0,16},{8,24},{16,0},{24,8},{1,17},{9,25},{17,1},{25,9},{2,18},{10... | collective-permute-start | bytes 196616 | tf_op jit(solution)/shard_map/ppermute | solution.py:326
  24.3 1.4 %collective-permute-start = (bf16[128,128]{1,0:T(8,128)(2,1)S(1)}, bf16[128,128]{1,0:T(8,128)(2,1)S(1)}, u32[]{:S(2)}, u32[]{:S(2)}) collective-permute-start(bf16[128,128]{1,0:T(8,128)(2,1)S(1)} %copy-done.2), channel_id=1, source_target_pairs={{0,8},{8,0},{16,24},{24,16},{1,9},{9,1},{17,25},{25,17},{2,10},{10... | collective-permute-start | bytes 98312 | tf_op jit(solution)/shard_map/ppermute | solution.py:318
  24.4 11.5 %collective-permute-start.4 = (bf16[4,288,128]{2,1,0:T(8,128)(2,1)}, bf16[4,288,128]{2,1,0:T(8,128)(2,1)S(1)}, u32[]{:S(2)}, u32[]{:S(2)}) collective-permute-start(bf16[4,288,128]{2,1,0:T(8,128)(2,1)} %get-tuple-element.20), channel_id=1, source_target_pairs={{16,0},{24,8},{17,1},{25,9},{18,2},{26,10},{19,3},{27,11},{20,4},{... | collective-permute-start | bytes 884744 | tf_op jit(solution)/shard_map/ppermute | solution.py:326
  28.9 6.4 %collective-permute-start.7 = (bf16[2,512,128]{2,1,0:T(8,128)(2,1)S(1)}, bf16[2,512,128]{2,1,0:T(8,128)(2,1)S(1)}, u32[]{:S(2)}, u32[]{:S(2)}) collective-permute-start(bf16[2,512,128]{2,1,0:T(8,128)(2,1)S(1)} %get-tuple-element.27), channel_id=1, source_target_pairs={{0,8},{8,0},{16,24},{24,16},{1,9},{9,1},{17,25},{25,17},{2,10},{10... | collective-permute-start | bytes 786440 | tf_op jit(solution)/shard_map/ppermute | solution.py:318
  29.5 1.3 %collective-permute-start.11 = (f32[64,128]{1,0:T(8,128)S(1)}, f32[64,128]{1,0:T(8,128)S(1)}, u32[]{:S(2)}, u32[]{:S(2)}) collective-permute-start(f32[64,128]{1,0:T(8,128)S(1)} %get-tuple-element.39), channel_id=1, source_target_pairs={{0,8},{8,0},{16,24},{24,16},{1,9},{9,1},{17,25},{25,17},{2,10},{10... | collective-permute-start | bytes 98312 | tf_op jit(solution)/shard_map/ppermute | solution.py:318
  30.7 10.1 %collective-permute-start.14 = (f32[128,128]{1,0:T(8,128)S(1)}, f32[128,128]{1,0:T(8,128)S(1)}, u32[]{:S(2)}, u32[]{:S(2)}) collective-permute-start(f32[128,128]{1,0:T(8,128)S(1)} %maximum_select_fusion), channel_id=1, source_target_pairs={{0,3},{1,2},{2,1},{3,0},{4,7},{5,6},{6,5},{7,4},{8,11},{9,10},{10,... | collective-permute-start | bytes 196616 | tf_op jit(solution)/shard_map/ppermute | solution.py:444
  34.6 6.3 %collective-permute-start.13 = (f32[128,128]{1,0:T(8,128)S(1)}, f32[128,128]{1,0:T(8,128)S(1)}, u32[]{:S(2)}, u32[]{:S(2)}) collective-permute-start(f32[128,128]{1,0:T(8,128)S(1)} %maximum_select_fusion), channel_id=1, source_target_pairs={{0,2},{1,3},{2,0},{3,1},{4,6},{5,7},{6,4},{7,5},{8,10},{9,11},{10,... | collective-permute-start | bytes 196616 | tf_op jit(solution)/shard_map/ppermute | solution.py:444
  34.6 6.3 %collective-permute-start.12 = (f32[128,128]{1,0:T(8,128)S(1)}, f32[128,128]{1,0:T(8,128)S(1)}, u32[]{:S(2)}, u32[]{:S(2)}) collective-permute-start(f32[128,128]{1,0:T(8,128)S(1)} %maximum_select_fusion), channel_id=1, source_target_pairs={{0,1},{1,0},{2,3},{3,2},{4,5},{5,4},{6,7},{7,6},{8,9},{9,8},{10,11... | collective-permute-start | bytes 196616 | tf_op jit(solution)/shard_map/ppermute | solution.py:444
  37.9 3.7 %collective-permute-start.8 = (bf16[2,224,128]{2,1,0:T(8,128)(2,1)S(1)}, bf16[2,224,128]{2,1,0:T(8,128)(2,1)S(1)}, u32[]{:S(2)}, u32[]{:S(2)}) collective-permute-start(bf16[2,224,128]{2,1,0:T(8,128)(2,1)S(1)} %get-tuple-element.28), channel_id=1, source_target_pairs={{0,8},{8,0},{16,24},{24,16},{1,9},{9,1},{17,25},{25,17},{2,10},{10... | collective-permute-start | bytes 344072 | tf_op jit(solution)/shard_map/ppermute | solution.py:318
  40.3 1.6 %collective-permute-start.9 = (bf16[2,288,128]{2,1,0:T(8,128)(2,1)S(1)}, bf16[2,288,128]{2,1,0:T(8,128)(2,1)S(1)}, u32[]{:S(2)}, u32[]{:S(2)}) collective-permute-start(bf16[2,288,128]{2,1,0:T(8,128)(2,1)S(1)} %get-tuple-element.29), channel_id=1, source_target_pairs={{0,8},{8,0},{16,24},{24,16},{1,9},{9,1},{17,25},{25,17},{2,10},{10... | collective-permute-start | bytes 442376 | tf_op jit(solution)/shard_map/ppermute | solution.py:318
